TPU v7x, 32 devices: a whole 2x2x4 slice. The times are simulated.
32 devices in a mesh: groups: 2 (over x), row: 16 (over z, y, core).
Axes of the slice: x: 2, y: 2, z: 4, core: 2. Of those that a mesh axis runs over, the one named last changes fastest.
Arguments:
- t2_panels: bfloat16 [32, 1024, 1280], P(('groups', 'row')), parts along dimension 0, may hold values from -6 to 6
- t2_mask: int32 [32, 4, 5], P(('groups', 'row')), parts along dimension 0, may hold values from 0 to 1, as said below
- v_blocks: bfloat16 [4, 1280, 32768], P('groups', None, 'row'), parts along dimension 0, may hold values from -0.1875 to 0.1875
- v_mask: int32 [4, 5, 128], P('groups', None, 'row'), parts along dimension 0, may hold values 0 or 1
- r_mask: int32 [8, 128], P('groups', 'row'), parts along dimension 0, may hold values 0 or 1
- owner_map: int32 [256, 4, 1], P(('groups', 'row')), parts along dimension 0, may hold values from 0 to 15; in each aligned block of 32 rows (0 to 31, 32 to 63, ..., all dimensions but the last counted through in order) at most 4 rows name the same one
- section_owner: int32 [4], P('groups'), parts along dimension 0, may hold values from 0 to 15
Outputs:
- delivered: bfloat16 [512, 4, 256, 256], P(('groups', 'row')), parts along dimension 0
There are 2 independent parts, one for each index of `groups`. A program takes and returns all parts, laid end to end along the dimension named above; each array names one. Nothing has to cross between parts.
Inputs may be any that keep to these rules, and one draw needn't show every extreme that they name: `t2_mask`: each device's panel has exactly 10 tiles of ones. `owner_map`: among the 32 tiles of one device no owner appears more than 4 times.
All inputs are finite; a program needn't handle non-finite values. No bound on the sum of `v_mask` or of `r_mask` on one device may be relied on, other than what follows from the above.
Results may differ from a plain program's by a relative error of at most 0.001.
Values may be sent and summed in bfloat16 or wider, within the bound.
No kernel may reach another device: no remote copies, remote signals or barrier semaphores. Data moves between devices by JAX's collectives and lax.ppermute only.
A program may use at most 192 MiB of HBM per device.

v0:
```python
import functools

import jax
import jax.numpy as jnp
from jax import lax
from jax.experimental import pallas as pl
from jax.experimental.pallas import tpu as pltpu
from jax.sharding import PartitionSpec as P

TILE = 256
MT = 4
KPT = 5
NT_DEV = 8
SECTIONS = 2
PCAP = 10
TILES = MT * NT_DEV
SPILL = 3
STEP_TILES = 2
STEP_COLS = STEP_TILES * TILE
ANY = pl.BlockSpec(memory_space=pl.ANY)
SMEM = pl.BlockSpec(memory_space=pltpu.SMEM)
VMEM = pl.BlockSpec(memory_space=pltpu.VMEM)


def swap(x, bit, ranks):
    return lax.ppermute(x, "row", [(i, i ^ bit) for i in range(ranks)])


def scatter_step(x, me, roots, bit, ranks):
    half = x.shape[1] // 2
    high = (me & bit) != 0
    low_rows, high_rows = x[:, :half], x[:, half:]
    own = jnp.where(high, high_rows, low_rows)
    got = swap(jnp.where(high, low_rows, high_rows), bit, ranks)
    return jnp.where((((me ^ roots) & bit) == 0)[:, None, None], own, got)


def middle_step(x, me, roots, bit, ranks):
    got = swap(x, bit, ranks)
    return jnp.where((((me ^ roots) & bit) == 0)[:, None, None], x, got)


def gather_step(x, me, bit, ranks):
    got = swap(x, bit, ranks)
    high = (me & bit) != 0
    return jnp.concatenate([jnp.where(high, got, x), jnp.where(high, x, got)], axis=1)


def spread(x, me, roots, ranks):
    x = scatter_step(x, me, roots, 1, ranks)
    half = x.shape[1] // 2
    a, b = x[:, :half], x[:, half:]
    a, b = scatter_step(a, me, roots, 2, ranks), scatter_step(b, me, roots, 4, ranks)
    a, b = scatter_step(a, me, roots, 4, ranks), scatter_step(b, me, roots, 2, ranks)
    bit = 8
    while bit < ranks:
        a, b = middle_step(a, me, roots, bit, ranks), middle_step(b, me, roots, bit, ranks)
        bit *= 2
    a, b = gather_step(a, me, 4, ranks), gather_step(b, me, 2, ranks)
    a, b = gather_step(a, me, 2, ranks), gather_step(b, me, 4, ranks)
    return gather_step(jnp.concatenate([a, b], axis=1), me, 1, ranks)


def gather_table(x, me, ranks):
    bit = 1
    while bit < ranks:
        got = swap(x, bit, ranks)
        high = (me & bit) != 0
        x = jnp.concatenate([jnp.where(high, got, x), jnp.where(high, x, got)], axis=0)
        bit *= 2
    return x


def nonzero_tiles(mask):
    ones = (mask != 0).astype(jnp.int32)
    places = jnp.arange(MT * KPT, dtype=jnp.int32)
    earlier = (places[None, :] < places[:, None]).astype(jnp.int32)
    before = jnp.sum(ones[..., None, :] * earlier, axis=-1)
    hit = ones[..., None, :] * (before[..., None, :] == jnp.arange(PCAP)[:, None])
    return jnp.sum(hit * places, axis=-1)


def ranks_of(owners, keep, direct):
    order = jnp.arange(TILES)
    earlier = order[None, :] < order[:, None]
    same = (owners[:, :, None] == owners[:, None, :]) & earlier
    rank = jnp.sum(same, axis=2, dtype=jnp.int32)
    kept_rank = jnp.sum(same & keep[:, None, :], axis=2, dtype=jnp.int32)
    spills = keep & (kept_rank >= direct)
    spill_place = jnp.sum(spills[:, None, :] & earlier, axis=2, dtype=jnp.int32)
    return rank, kept_rank, spills, spill_place


def pack_kernel(tile_ref, panel_ref, out_ref, sem):
    copies = []
    for i in range(PCAP):
        place = tile_ref[i]
        m, k = place // KPT, lax.rem(place, KPT)
        copies.append(
            pltpu.make_async_copy(
                panel_ref.at[
                    pl.ds(pl.multiple_of(m * TILE, TILE), TILE), pl.ds(pl.multiple_of(k * TILE, TILE), TILE)
                ],
                out_ref.at[pl.ds(i * TILE, TILE)],
                sem.at[i],
            )
        )
    for copy in copies:
        copy.start()
    for copy in copies:
        copy.wait()


def pack(panel, tiles):
    return pl.pallas_call(
        pack_kernel,
        out_shape=jax.ShapeDtypeStruct((PCAP * TILE, TILE), jnp.bfloat16),
        in_specs=[SMEM, ANY],
        out_specs=VMEM,
        scratch_shapes=[pltpu.SemaphoreType.DMA((PCAP,))],
        name="pack_panel",
    )(tiles, panel)


def ladder_kernel(split, tile_ref, place_ref, amp_ref, v_ref, mask_ref, out_ref, spill_ref, acc, staged, sem):
    step = pl.program_id(0)
    acc[...] = jnp.zeros_like(acc)
    for s in range(SECTIONS):
        for i in range(PCAP):
            place = tile_ref[s * PCAP + i]
            m, k = place // KPT, lax.rem(place, KPT)
            masked = v_ref[s, pl.ds(pl.multiple_of(k * TILE, TILE), TILE), :] * mask_ref[s, k]
            acc[m] += jnp.dot(
                amp_ref[s, i * TILE : (i + 1) * TILE, :], masked, preferred_element_type=jnp.float32
            )

    def copy_to(q, ref, place):
        return pltpu.make_async_copy(staged.at[q], ref.at[place], sem.at[q])

    for j in range(STEP_TILES):
        for m in range(MT):
            q = (step * STEP_TILES + j) * MT + m
            staged[q] = acc[m, :, j * TILE : (j + 1) * TILE].astype(jnp.bfloat16)
            place = place_ref[q]

            @pl.when((place >= 0) & (place < split))
            def _():
                copy_to(q, out_ref, place).start()

            @pl.when(place >= split)
            def _():
                copy_to(q, spill_ref, place - split).start()

    @pl.when(step == NT_DEV // STEP_TILES - 1)
    def _():
        def finish(q, carry):
            @pl.when(place_ref[q] >= 0)
            def _():
                copy_to(q, out_ref, 0).wait()

            return carry

        lax.fori_loop(0, TILES, finish, 0)


def ladder(amp, amp_tiles, v_blocks, v_rows, places, split):
    return pl.pallas_call(
        functools.partial(ladder_kernel, split),
        out_shape=(
            jax.ShapeDtypeStruct((split, TILE, TILE), jnp.bfloat16),
            jax.ShapeDtypeStruct((SPILL, TILE, TILE), jnp.bfloat16),
        ),
        grid=(NT_DEV // STEP_TILES,),
        in_specs=[
            SMEM,
            SMEM,
            VMEM,
            pl.BlockSpec((SECTIONS, KPT * TILE, STEP_COLS), lambda j: (0, 0, j)),
            pl.BlockSpec((SECTIONS, KPT, 1, STEP_COLS), lambda j: (0, 0, 0, j)),
        ],
        out_specs=(ANY, ANY),
        scratch_shapes=[
            pltpu.VMEM((MT, TILE, STEP_COLS), jnp.float32),
            pltpu.VMEM((TILES, TILE, TILE), jnp.bfloat16),
            pltpu.SemaphoreType.DMA((TILES,)),
        ],
        compiler_params=pltpu.CompilerParams(vmem_limit_bytes=48 * 1024 * 1024),
        name="ladder",
    )(amp_tiles, places, amp, v_blocks, v_rows)


def place_kernel(slots, split, table_ref, direct_ref, spill_ref, out_ref, zero, held, in_sem, out_sem):
    zero[...] = jnp.zeros_like(zero)

    def fetch(ref, place, j):
        return pltpu.make_async_copy(ref.at[place], held.at[j], in_sem.at[j])

    def begin(j, carry):
        source = table_ref[j]

        @pl.when((source >= 0) & (source < split))
        def _():
            fetch(direct_ref, source, j).start()

        @pl.when(source >= split)
        def _():
            fetch(spill_ref, source - split, j).start()

        @pl.when(source < 0)
        def _():
            pltpu.make_async_copy(zero, out_ref.at[j], out_sem.at[j]).start()

        return carry

    def forward(j, carry):
        @pl.when(table_ref[j] >= 0)
        def _():
            fetch(direct_ref, 0, j).wait()
            pltpu.make_async_copy(held.at[j], out_ref.at[j], out_sem.at[j]).start()

        return carry

    def finish(j, carry):
        pltpu.make_async_copy(zero, out_ref.at[j], out_sem.at[j]).wait()
        return carry

    lax.fori_loop(0, slots, begin, 0)
    lax.fori_loop(0, slots, forward, 0)
    lax.fori_loop(0, slots, finish, 0)


def place_tiles(table, direct, spill):
    slots, split = table.shape[0], direct.shape[0]
    return pl.pallas_call(
        functools.partial(place_kernel, slots, split),
        out_shape=jax.ShapeDtypeStruct((slots, TILE, TILE), jnp.bfloat16),
        in_specs=[SMEM, ANY, ANY],
        out_specs=ANY,
        scratch_shapes=[
            pltpu.VMEM((TILE, TILE), jnp.bfloat16),
            pltpu.VMEM((slots, TILE, TILE), jnp.bfloat16),
            pltpu.SemaphoreType.DMA((slots,)),
            pltpu.SemaphoreType.DMA((slots,)),
        ],
        compiler_params=pltpu.CompilerParams(vmem_limit_bytes=32 * 1024 * 1024),
        name="place_tiles",
    )(table, direct, spill)


def exchange(tiles, ranks):
    count = tiles.shape[0] // ranks
    sent = tiles.reshape(ranks, count, TILE, TILE)
    return lax.all_to_all(sent, "row", split_axis=0, concat_axis=0, tiled=True).reshape(
        ranks * count, TILE, TILE
    )


def local(t2_panels, t2_mask, v_blocks, v_mask, r_mask, owner_map, section_owner):
    ranks, groups = lax.axis_size("row"), lax.axis_size("groups")
    me = lax.axis_index("row")
    slots_each = max(2, 2 * TILES // ranks)
    direct = slots_each // 2
    roots = section_owner

    packed = pack(t2_panels[0], nonzero_tiles(t2_mask.reshape(MT * KPT)))
    amp = spread(
        jnp.broadcast_to(packed[None], (SECTIONS,) + packed.shape), me, roots, ranks
    )

    own_code = owner_map.reshape(1, TILES) * 2 + (r_mask.T.reshape(1, TILES) != 0).astype(jnp.int32)
    codes = gather_table(
        jnp.concatenate([own_code, t2_mask.reshape(1, MT * KPT)], axis=1), me, ranks
    )
    owners, keep = codes[:, :TILES] // 2, codes[:, :TILES] % 2 != 0
    amp_tiles = nonzero_tiles(jnp.take(codes[:, TILES:], roots, axis=0)).reshape(-1)
    rank, kept_rank, spills, spill_place = ranks_of(owners, keep, direct)
    most = jnp.max(jnp.sum(spills, axis=1, dtype=jnp.int32)).reshape(1, 1)
    worst = most
    for turn in range(1, groups):
        worst = jnp.maximum(
            worst, lax.ppermute(most, "groups", [(g, (g + turn) % groups) for g in range(groups)])
        )

    device = jnp.arange(ranks, dtype=jnp.int32)[:, None]
    slot = jnp.arange(slots_each, dtype=jnp.int32)
    arrives = ((owners == me) & keep)[:, None, :] & (rank[:, None, :] == slot[None, :, None])

    def row_of(x):
        return lax.dynamic_index_in_dim(x, me, 0, keepdims=False)

    def table_of(origin):
        return (jnp.sum(jnp.where(arrives, origin[:, None, :] + 1, 0), axis=2) - 1).reshape(-1)

    v_rows = jnp.repeat(v_mask.astype(jnp.bfloat16), TILE, axis=2)[:, :, None, :]

    split = ranks * direct
    short_places = row_of(
        jnp.where(keep, jnp.where(spills, split + spill_place, owners * direct + kept_rank), -1)
    )
    short_table = table_of(
        jnp.where(spills, split + device * SPILL + spill_place, device * direct + kept_rank)
    )
    long_places = row_of(jnp.where(keep, owners * slots_each + kept_rank, -1))
    long_table = table_of(device * slots_each + kept_rank)

    def short(amp, v_blocks):
        tiles, spill = ladder(amp, amp_tiles, v_blocks, v_rows, short_places, split)
        gathered = lax.all_gather(spill, "row", axis=0, tiled=True)
        return place_tiles(short_table, exchange(tiles, ranks), gathered)

    def long(amp, v_blocks):
        tiles, spill = ladder(amp, amp_tiles, v_blocks, v_rows, long_places, ranks * slots_each)
        return place_tiles(long_table, exchange(tiles, ranks), spill)

    delivered = lax.cond(worst[0, 0] <= SPILL, short, long, amp, v_blocks)
    return delivered.reshape(ranks, slots_each, TILE, TILE)


def solution(mesh):
    placed = (
        P(("groups", "row"), None, None),
        P(("groups", "row"), None, None),
        P("groups", None, "row"),
        P("groups", None, "row"),
        P("groups", "row"),
        P(("groups", "row"), None, None),
        P("groups"),
    )
    return jax.shard_map(
        local,
        mesh=mesh,
        in_specs=placed,
        out_specs=P(("groups", "row"), None, None, None),
        check_vma=False,
    )
```

profile of v0, /device:TPU:16, one launch (start us, length us, event | category | flops | bytes accessed | tf_op | source)
XLA Modules:
  0.0 242.7 jit_solution(11353982569419406035)
XLA Ops:
  6.5 0.7 compare_convert_fusion
  7.4 0.7 multiply_reduce_fusion.1.tile_ref
  8.1 3.2 %pack_panel.1 = bf16[2560,256]{1,0:T(8,128)(2,1)} custom-call(s32[10]{0:T(128)} %multiply_reduce_fusion.1.tile_ref, bf16[1024,1280]{1,0:T(8,128)(2,1)} %bitcast.35), custom_call_target="tpu_custom_call" | custom-call | tf_op jit(solution)/shard_map/pack_panel/pallas_call | solution.py:115
  11.4 1.4 select_bitcast_fusion.1
  14.2 1.8 collective-permute-done.5
  16.3 1.6 collective-permute-start.6
  17.9 1.6 collective-permute-start.11
  20.1 6.0 %collective-permute-done.6 = bf16[2,320,256]{2,1,0:T(8,128)(2,1)S(1)} collective-permute-done((bf16[2,320,256]{2,1,0:T(8,128)(2,1)S(1)}, bf16[2,320,256]{2,1,0:T(8,128)(2,1)S(1)}, u32[]{:S(2)}, u32[]{:S(2)}) %collective-permute-start.6) | collective-permute-done | bytes 327712 | tf_op jit(solution)/shard_map/ppermute | solution.py:26
  26.1 1.2 collective-permute-done.11
  28.2 1.6 collective-permute-start.2
  30.2 2.7 %collective-permute-done.12 = bf16[2,160,256]{2,1,0:T(8,128)(2,1)S(1)} collective-permute-done((bf16[2,160,256]{2,1,0:T(8,128)(2,1)S(1)}, bf16[2,160,256]{2,1,0:T(8,128)(2,1)S(1)}, u32[]{:S(2)}, u32[]{:S(2)}) %collective-permute-start.12) | collective-permute-done | bytes 163872 | tf_op jit(solution)/shard_map/ppermute | solution.py:26
  33.4 3.4 %collective-permute-done.7 = bf16[2,160,256]{2,1,0:T(8,128)(2,1)S(1)} collective-permute-done((bf16[2,160,256]{2,1,0:T(8,128)(2,1)S(1)}, bf16[2,160,256]{2,1,0:T(8,128)(2,1)S(1)}, u32[]{:S(2)}, u32[]{:S(2)}) %collective-permute-start.7) | collective-permute-done | bytes 163872 | tf_op jit(solution)/shard_map/ppermute | solution.py:26
  37.3 2.7 %collective-permute-start.3 = (s32[8,52]{1,0:T(8,128)S(1)}, s32[8,52]{1,0:T(8,128)S(1)}, u32[]{:S(2)}, u32[]{:S(2)}) collective-permute-start(s32[8,52]{1,0:T(8,128)S(1)} %pad_add_fusion.1), channel_id=1, source_target_pairs={{0,8},{1,9},{2,10},{3,11},{4,12},{5,13},{6,14},{7,15},{8,0},{9,1},... | collective-permute-start | bytes 5000 | tf_op jit(solution)/shard_map/ppermute | solution.py:26
  40.0 3.8 %collective-permute-done.13 = bf16[2,160,256]{2,1,0:T(8,128)(2,1)S(1)} collective-permute-done((bf16[2,160,256]{2,1,0:T(8,128)(2,1)S(1)}, bf16[2,160,256]{2,1,0:T(8,128)(2,1)S(1)}, u32[]{:S(2)}, u32[]{:S(2)}) %collective-permute-start.13) | collective-permute-done | bytes 163872 | tf_op jit(solution)/shard_map/ppermute | solution.py:26
  43.8 1.8 collective-permute-done.8
  45.7 4.5 %collective-permute-start.9 = (bf16[2,160,256]{2,1,0:T(8,128)(2,1)S(1)}, bf16[2,160,256]{2,1,0:T(8,128)(2,1)S(1)}, u32[]{:S(2)}, u32[]{:S(2)}) collective-permute-start(bf16[2,160,256]{2,1,0:T(8,128)(2,1)S(1)} %get-tuple-element.299), channel_id=1, source_target_pairs={{0,4},{1,5},{2,6},{3,7},{4,0},{5,1},{6,2},{7,3},{8,12},{9,13},{10,... | collective-permute-start | bytes 491528 | tf_op jit(solution)/shard_map/ppermute | solution.py:26
  50.2 0.8 collective-permute-start.14
  51.0 3.4 %collective-permute-done.9 = bf16[2,160,256]{2,1,0:T(8,128)(2,1)S(1)} collective-permute-done((bf16[2,160,256]{2,1,0:T(8,128)(2,1)S(1)}, bf16[2,160,256]{2,1,0:T(8,128)(2,1)S(1)}, u32[]{:S(2)}, u32[]{:S(2)}) %collective-permute-start.9) | collective-permute-done | bytes 163872 | tf_op jit(solution)/shard_map/ppermute | solution.py:26
  54.7 1.2 collective-permute-done.14
  57.2 6.2 %collective-permute-done.10 = bf16[2,320,256]{2,1,0:T(8,128)(2,1)S(1)} collective-permute-done((bf16[2,320,256]{2,1,0:T(8,128)(2,1)S(1)}, bf16[2,320,256]{2,1,0:T(8,128)(2,1)S(1)}, u32[]{:S(2)}, u32[]{:S(2)}) %collective-permute-start.10) | collective-permute-done | bytes 327712 | tf_op jit(solution)/shard_map/ppermute | solution.py:26
  63.5 0.8 collective-permute-done.15
  65.6 0.7 convert_reduce_fusion
  67.1 1.5 collective-permute-start.4
  68.6 2.2 collective-permute-done.4
  72.2 1.8 broadcast_select_fusion.2
  74.2 161.7 %conditional.1 = (bf16[16,4,256,256]{3,2,1,0:T(8,128)(2,1)}) conditional(s32[]{:T(128)} %bitcast.13, (s32[16,1]{0,1:T(1,128)S(1)}, s32[16,32]{1,0:T(8,128)S(1)}, pred[16,4,32]{2,1,0:T(4,128)(4,1)S(1)}, s32[16,4,32]{2,1,0:T(4,128)S(1)}, s32[64]{0:T(128)S(1)}, /*index=5*/s32[16,32]{1,0:T(8,128)S(1)}, pred[16,32]{1,0:T(8,128)(4,1)S(1)}, ...), branch_computations={%region_8.10_spmd, %region_10.13_spmd} | conditional | flops 22224 | bytes 74753360 | solution.py:315
  74.7 14.0 %ladder.3 = (bf16[32,256,256]{2,1,0:T(8,128)(2,1)S(1)}, bf16[3,256,256]{2,1,0:T(8,128)(2,1)}) custom-call(s32[20]{0:T(128)S(1)} %get-tuple-element.159.tile_ref, s32[32]{0:T(128)S(1)} %fusion.6.place_ref, bf16[2,2560,256]{2,1,0:T(8,128)(2,1)S(1)} %get-tuple-element.165.amp_ref, bf16[2,1280,2048]{2,1,0:T(8,128)(2,1)} %get-tuple-element.166.v_ref, ...), custom_call_target="tpu_custom_call" | custom-call | tf_op jit(solution)/shard_map/cond/branch_1_fun/ladder/pallas_call | solution.py:167
  88.7 2.0 copy-done.1
  90.7 5.0 %all-to-all-start.1 = ((bf16[16,2,256,256]{3,2,1,0:T(8,128)(2,1)}), bf16[16,2,256,256]{3,2,1,0:T(8,128)(2,1)}, u32[]{:S(2)}, u32[]{:S(2)}) async-start(bf16[16,2,256,256]{3,2,1,0:T(8,128)(2,1)} %bitcast.32), calls=%async_computation.1 | async-start | bytes 8388608 | tf_op jit(solution)/shard_map/cond/branch_1_fun/all_to_all | solution.py:253
  96.3 130.1 %all-to-all-done.1 = bf16[16,2,256,256]{3,2,1,0:T(8,128)(2,1)} async-done(((bf16[16,2,256,256]{3,2,1,0:T(8,128)(2,1)}), bf16[16,2,256,256]{3,2,1,0:T(8,128)(2,1)}, u32[]{:S(2)}, u32[]{:S(2)}) %all-to-all-start.1) | async-done | bytes 4194336 | tf_op jit(solution)/shard_map/cond/branch_1_fun/all_to_all | solution.py:253
  226.4 2.8 %copy-done = bf16[48,256,256]{2,1,0:T(8,128)(2,1)S(1)} copy-done((bf16[48,256,256]{2,1,0:T(8,128)(2,1)S(1)}, bf16[48,256,256]{2,1,0:T(8,128)(2,1)}, u32[]{:S(2)}) %copy-start) | copy-done | bytes 6291480 | tf_op jit(solution)/shard_map/cond
  229.2 6.7 %place_tiles.3 = bf16[64,256,256]{2,1,0:T(8,128)(2,1)} custom-call(s32[64]{0:T(128)S(1)} %sub.10.table_ref, bf16[32,256,256]{2,1,0:T(8,128)(2,1)} %bitcast.9.direct_ref, bf16[48,256,256]{2,1,0:T(8,128)(2,1)S(1)} %copy-done), custom_call_target="tpu_custom_call" | custom-call | tf_op jit(solution)/shard_map/cond/branch_1_fun/place_tiles/pallas_call | solution.py:234
  (101 shorter events, 9.7 us)
Async XLA Ops:
  11.3 1.6 copy-start.2
  11.4 1.7 copy-start.4
  11.4 1.9 copy-start.5
  11.4 2.6 %copy-start.3 = (s32[2,5,8]{2,0,1:T(2,128)S(1)}, s32[2,5,8]{2,0,1:T(2,128)}, u32[]{:S(2)}) copy-start(s32[2,5,8]{2,0,1:T(2,128)} %param.12) | copy-start | bytes 964
  11.4 2.7 %copy-start.6 = (s32[2]{0:T(128)S(1)}, s32[2]{0:T(128)}, u32[]{:S(2)}) copy-start(s32[2]{0:T(128)} %param.15) | copy-start | bytes 28
  12.9 3.1 %collective-permute-start.5 = (bf16[2,1280,256]{2,1,0:T(8,128)(2,1)S(1)}, bf16[2,1280,256]{2,1,0:T(8,128)(2,1)S(1)}, u32[]{:S(2)}, u32[]{:S(2)}) collective-permute-start(bf16[2,1280,256]{2,1,0:T(8,128)(2,1)S(1)} %broadcast_in_dim.136), channel_id=1, source_target_pairs={{0,1},{1,0},{2,3},{3,2},{4,5},{5,4},{6,7},{7,6},{8,9},{9,8},{10,11... | collective-permute-start | bytes 3932168 | tf_op jit(solution)/shard_map/ppermute | solution.py:26
  13.5 5.9 %collective-permute-start = (s32[1,52]{1,0:T(1,128)S(1)}, s32[1,52]{1,0:T(1,128)S(1)}, u32[]{:S(2)}, u32[]{:S(2)}) collective-permute-start(s32[1,52]{1,0:T(1,128)S(1)} %pad_add_fusion.4), channel_id=1, source_target_pairs={{0,1},{1,0},{2,3},{3,2},{4,5},{5,4},{6,7},{7,6},{8,9},{9,8},{10,11... | collective-permute-start | bytes 632 | tf_op jit(solution)/shard_map/ppermute | solution.py:26
  16.3 9.8 %collective-permute-start.6 = (bf16[2,320,256]{2,1,0:T(8,128)(2,1)S(1)}, bf16[2,320,256]{2,1,0:T(8,128)(2,1)S(1)}, u32[]{:S(2)}, u32[]{:S(2)}) collective-permute-start(bf16[2,320,256]{2,1,0:T(8,128)(2,1)S(1)} %get-tuple-element.279), channel_id=1, source_target_pairs={{0,2},{1,3},{2,0},{3,1},{4,6},{5,7},{6,4},{7,5},{8,10},{9,11},{10,... | collective-permute-start | bytes 983048 | tf_op jit(solution)/shard_map/ppermute | solution.py:26
  17.9 9.5 %collective-permute-start.11 = (bf16[2,320,256]{2,1,0:T(8,128)(2,1)S(1)}, bf16[2,320,256]{2,1,0:T(8,128)(2,1)S(1)}, u32[]{:S(2)}, u32[]{:S(2)}) collective-permute-start(bf16[2,320,256]{2,1,0:T(8,128)(2,1)S(1)} %get-tuple-element.280), channel_id=1, source_target_pairs={{0,4},{1,5},{2,6},{3,7},{4,0},{5,1},{6,2},{7,3},{8,12},{9,13},{10,... | collective-permute-start | bytes 983048 | tf_op jit(solution)/shard_map/ppermute | solution.py:26
  19.5 8.6 %collective-permute-start.1 = (s32[2,52]{1,0:T(2,128)S(1)}, s32[2,52]{1,0:T(2,128)S(1)}, u32[]{:S(2)}, u32[]{:S(2)}) collective-permute-start(s32[2,52]{1,0:T(2,128)S(1)} %pad_add_fusion.3), channel_id=1, source_target_pairs={{0,2},{1,3},{2,0},{3,1},{4,6},{5,7},{6,4},{7,5},{8,10},{9,11},{10,... | collective-permute-start | bytes 1256 | tf_op jit(solution)/shard_map/ppermute | solution.py:26
  27.5 5.4 %collective-permute-start.12 = (bf16[2,160,256]{2,1,0:T(8,128)(2,1)S(1)}, bf16[2,160,256]{2,1,0:T(8,128)(2,1)S(1)}, u32[]{:S(2)}, u32[]{:S(2)}) collective-permute-start(bf16[2,160,256]{2,1,0:T(8,128)(2,1)S(1)} %get-tuple-element.305), channel_id=1, source_target_pairs={{0,2},{1,3},{2,0},{3,1},{4,6},{5,7},{6,4},{7,5},{8,10},{9,11},{10,... | collective-permute-start | bytes 491528 | tf_op jit(solution)/shard_map/ppermute | solution.py:26
  28.2 9.1 %collective-permute-start.2 = (s32[4,52]{1,0:T(4,128)S(1)}, s32[4,52]{1,0:T(4,128)S(1)}, u32[]{:S(2)}, u32[]{:S(2)}) collective-permute-start(s32[4,52]{1,0:T(4,128)S(1)} %pad_add_fusion.2), channel_id=1, source_target_pairs={{0,4},{1,5},{2,6},{3,7},{4,0},{5,1},{6,2},{7,3},{8,12},{9,13},{10,... | collective-permute-start | bytes 2504 | tf_op jit(solution)/shard_map/ppermute | solution.py:26
  29.8 7.0 %collective-permute-start.7 = (bf16[2,160,256]{2,1,0:T(8,128)(2,1)S(1)}, bf16[2,160,256]{2,1,0:T(8,128)(2,1)S(1)}, u32[]{:S(2)}, u32[]{:S(2)}) collective-permute-start(bf16[2,160,256]{2,1,0:T(8,128)(2,1)S(1)} %get-tuple-element.306), channel_id=1, source_target_pairs={{0,4},{1,5},{2,6},{3,7},{4,0},{5,1},{6,2},{7,3},{8,12},{9,13},{10,... | collective-permute-start | bytes 491528 | tf_op jit(solution)/shard_map/ppermute | solution.py:26
  33.0 10.8 %collective-permute-start.13 = (bf16[2,160,256]{2,1,0:T(8,128)(2,1)S(1)}, bf16[2,160,256]{2,1,0:T(8,128)(2,1)S(1)}, u32[]{:S(2)}, u32[]{:S(2)}) collective-permute-start(bf16[2,160,256]{2,1,0:T(8,128)(2,1)S(1)} %select_select_fusion.2), channel_id=1, source_target_pairs={{0,8},{1,9},{2,10},{3,11},{4,12},{5,13},{6,14},{7,15},{8,0},{9,1},... | collective-permute-start | bytes 491528 | tf_op jit(solution)/shard_map/ppermute | solution.py:26
  36.9 8.7 %collective-permute-start.8 = (bf16[2,160,256]{2,1,0:T(8,128)(2,1)S(1)}, bf16[2,160,256]{2,1,0:T(8,128)(2,1)S(1)}, u32[]{:S(2)}, u32[]{:S(2)}) collective-permute-start(bf16[2,160,256]{2,1,0:T(8,128)(2,1)S(1)} %select_select_fusion.3), channel_id=1, source_target_pairs={{0,8},{1,9},{2,10},{3,11},{4,12},{5,13},{6,14},{7,15},{8,0},{9,1},... | collective-permute-start | bytes 491528 | tf_op jit(solution)/shard_map/ppermute | solution.py:26
  37.3 13.0 %collective-permute-start.3 = (s32[8,52]{1,0:T(8,128)S(1)}, s32[8,52]{1,0:T(8,128)S(1)}, u32[]{:S(2)}, u32[]{:S(2)}) collective-permute-start(s32[8,52]{1,0:T(8,128)S(1)} %pad_add_fusion.1), channel_id=1, source_target_pairs={{0,8},{1,9},{2,10},{3,11},{4,12},{5,13},{6,14},{7,15},{8,0},{9,1},... | collective-permute-start | bytes 5000 | tf_op jit(solution)/shard_map/ppermute | solution.py:26
  45.7 8.7 %collective-permute-start.9 = (bf16[2,160,256]{2,1,0:T(8,128)(2,1)S(1)}, bf16[2,160,256]{2,1,0:T(8,128)(2,1)S(1)}, u32[]{:S(2)}, u32[]{:S(2)}) collective-permute-start(bf16[2,160,256]{2,1,0:T(8,128)(2,1)S(1)} %get-tuple-element.299), channel_id=1, source_target_pairs={{0,4},{1,5},{2,6},{3,7},{4,0},{5,1},{6,2},{7,3},{8,12},{9,13},{10,... | collective-permute-start | bytes 491528 | tf_op jit(solution)/shard_map/ppermute | solution.py:26
  50.2 5.7 %collective-permute-start.14 = (bf16[2,160,256]{2,1,0:T(8,128)(2,1)S(1)}, bf16[2,160,256]{2,1,0:T(8,128)(2,1)S(1)}, u32[]{:S(2)}, u32[]{:S(2)}) collective-permute-start(bf16[2,160,256]{2,1,0:T(8,128)(2,1)S(1)} %get-tuple-element.300), channel_id=1, source_target_pairs={{0,2},{1,3},{2,0},{3,1},{4,6},{5,7},{6,4},{7,5},{8,10},{9,11},{10,... | collective-permute-start | bytes 491528 | tf_op jit(solution)/shard_map/ppermute | solution.py:26
  54.4 8.9 %collective-permute-start.10 = (bf16[2,320,256]{2,1,0:T(8,128)(2,1)S(1)}, bf16[2,320,256]{2,1,0:T(8,128)(2,1)S(1)}, u32[]{:S(2)}, u32[]{:S(2)}) collective-permute-start(bf16[2,320,256]{2,1,0:T(8,128)(2,1)S(1)} %pad_maximum_fusion.2), channel_id=1, source_target_pairs={{0,2},{1,3},{2,0},{3,1},{4,6},{5,7},{6,4},{7,5},{8,10},{9,11},{10,... | collective-permute-start | bytes 983048 | tf_op jit(solution)/shard_map/ppermute | solution.py:26
  56.0 8.3 %collective-permute-start.15 = (bf16[2,320,256]{2,1,0:T(8,128)(2,1)S(1)}, bf16[2,320,256]{2,1,0:T(8,128)(2,1)S(1)}, u32[]{:S(2)}, u32[]{:S(2)}) collective-permute-start(bf16[2,320,256]{2,1,0:T(8,128)(2,1)S(1)} %pad_maximum_fusion.3), channel_id=1, source_target_pairs={{0,4},{1,5},{2,6},{3,7},{4,0},{5,1},{6,2},{7,3},{8,12},{9,13},{10,... | collective-permute-start | bytes 983048 | tf_op jit(solution)/shard_map/ppermute | solution.py:26
  64.5 7.7 %collective-permute-start.16 = (bf16[2,1280,256]{2,1,0:T(8,128)(2,1)S(1)}, bf16[2,1280,256]{2,1,0:T(8,128)(2,1)}, u32[]{:S(2)}, u32[]{:S(2)}) collective-permute-start(bf16[2,1280,256]{2,1,0:T(8,128)(2,1)S(1)} %pad_maximum_fusion.1), channel_id=1, source_target_pairs={{0,1},{1,0},{2,3},{3,2},{4,5},{5,4},{6,7},{7,6},{8,9},{9,8},{10,11... | collective-permute-start | bytes 3932168 | tf_op jit(solution)/shard_map/ppermute | solution.py:26
  67.1 3.8 %collective-permute-start.4 = (s32[1,1]{1,0:T(1,128)}, s32[1,1]{1,0:T(1,128)}, u32[]{:S(2)}, u32[]{:S(2)}) collective-permute-start(s32[1,1]{1,0:T(1,128)} %bitcast.12), channel_id=1, source_target_pairs={{0,16},{16,0},{1,17},{17,1},{2,18},{18,2},{3,19},{19,3},{4,20},{20... | collective-permute-start | bytes 20 | tf_op jit(solution)/shard_map/ppermute | solution.py:281
  74.2 152.2 %all-gather.2.cloned.1.call-start = ((), (), s32[]{:S(2)}) async-start(), calls=%async_computation.2 | async-start | bytes 6684672 | tf_op jit(solution)/shard_map/cond/branch_1_fun/all_gather | solution.py:308
  88.7 2.0 copy-start.1
  90.7 135.6 %all-to-all-start.1 = ((bf16[16,2,256,256]{3,2,1,0:T(8,128)(2,1)}), bf16[16,2,256,256]{3,2,1,0:T(8,128)(2,1)}, u32[]{:S(2)}, u32[]{:S(2)}) async-start(bf16[16,2,256,256]{3,2,1,0:T(8,128)(2,1)} %bitcast.32), calls=%async_computation.1 | async-start | bytes 8388608 | tf_op jit(solution)/shard_map/cond/branch_1_fun/all_to_all | solution.py:253
  226.4 2.8 %copy-start = (bf16[48,256,256]{2,1,0:T(8,128)(2,1)S(1)}, bf16[48,256,256]{2,1,0:T(8,128)(2,1)}, u32[]{:S(2)}) copy-start(bf16[48,256,256]{2,1,0:T(8,128)(2,1)} %all-gather.2.cloned.1.call-done.spill_ref) | copy-start | bytes 18874372 | tf_op jit(solution)/shard_map/cond
Sparse Core Ops, SparseCore 0:
  90.9 119.3 all-gather.1
where the time goes:
time: 244 us; the launch traced here: 243 us
  waiting for transfers between devices  165 us (68%)
  Pallas kernels  23.9 us (10%)
  starting transfers between devices  23.2 us (10%)
  between operations  15.1 us (6%)
  other arithmetic  9.44 us (4%)
  local copies, waits for them, and re-layouts  6.5 us (3%)
    all_to_all x1, waiting for transfers between devices, exchange(): lax.all_to_all(sent, 'row', split_axis=0, concat_axis=0, tiled=True)  130 us
    ppermute x16, waiting for transfers between devices, swap(): return lax.ppermute(x, 'row', [(i, i ^ bit) for i in range(ranks)])  32.3 us
    ppermute x16, starting transfers between devices, swap(): return lax.ppermute(x, 'row', [(i, i ^ bit) for i in range(ranks)])  16.6 us
    pallas_call x1, Pallas kernels, ladder(): pl.pallas_call(functools.partial(ladder_kernel, split), out_shape=(jax.Sh...  14 us
    pallas_call x1, Pallas kernels, place_tiles(): pl.pallas_call(functools.partial(place_kernel, slots, split), out_shape=j...  6.69 us
    all_to_all x1, starting transfers between devices, exchange(): lax.all_to_all(sent, 'row', split_axis=0, concat_axis=0, tiled=True)  5.02 us
  transfers between devices with their start and end apart: 19, of which 13 were waited for; matrix products, arithmetic and copies ran while one was open for 2% of the time, Pallas kernels for 0%

commit v1 on v0

v1 whole, which is shorter than its diff:
```python
import functools

import jax
import jax.numpy as jnp
from jax import lax
from jax.experimental import pallas as pl
from jax.experimental.pallas import tpu as pltpu
from jax.sharding import PartitionSpec as P

TILE = 256
MT = 4
KPT = 5
NT_DEV = 8
SECTIONS = 2
PCAP = 10
TILES = MT * NT_DEV
SPILL = 3
STEP_TILES = 2
STEP_COLS = STEP_TILES * TILE
PAIRS = (SECTIONS * PCAP + MT) // 2
ANY = pl.BlockSpec(memory_space=pl.ANY)
HBM = pl.BlockSpec(memory_space=pltpu.HBM)
SMEM = pl.BlockSpec(memory_space=pltpu.SMEM)
VMEM = pl.BlockSpec(memory_space=pltpu.VMEM)


def swap(x, bit, ranks):
    return lax.ppermute(x, "row", [(i, i ^ bit) for i in range(ranks)])


def swap_with(x, note, bit, ranks):
    rows = x.shape[0] * x.shape[1]
    got = swap(jnp.concatenate([x.reshape(rows, -1), note], axis=0), bit, ranks)
    return got[:rows].reshape(x.shape), got[rows:]


def in_order(high, mine, got, axis):
    return jnp.concatenate([jnp.where(high, got, mine), jnp.where(high, mine, got)], axis=axis)


def near(me, roots, bit):
    return (((me ^ roots) & bit) == 0)[:, None, None]


def scatter_step(x, note, me, roots, bit, ranks):
    half = x.shape[1] // 2
    high = (me & bit) != 0
    low_rows, high_rows = x[:, :half], x[:, half:]
    own, give = jnp.where(high, high_rows, low_rows), jnp.where(high, low_rows, high_rows)
    if note is None:
        got = swap(give, bit, ranks)
    else:
        got, got_note = swap_with(give, note, bit, ranks)
        note = in_order(high, note, got_note, 0)
    return jnp.where(near(me, roots, bit), own, got), note


def middle_step(x, note, me, roots, bit, ranks):
    if note is None:
        got = swap(x, bit, ranks)
    else:
        got, got_note = swap_with(x, note, bit, ranks)
        note = in_order((me & bit) != 0, note, got_note, 0)
    return jnp.where(near(me, roots, bit), x, got), note


def gather_step(x, me, bit, ranks):
    return in_order((me & bit) != 0, x, swap(x, bit, ranks), 1)


def spread(own, give, me, roots, ranks):
    rows = own.shape[0]
    got = swap(give, 1, ranks)
    note = in_order((me & 1) != 0, give[rows : rows + 1], got[rows : rows + 1], 0)
    x = jnp.where(near(me, roots, 1), own[None], got[None, :rows])
    half = rows // 2
    a, b = x[:, :half], x[:, half:]
    a, note = scatter_step(a, note, me, roots, 2, ranks)
    b, _ = scatter_step(b, None, me, roots, 4, ranks)
    a, note = scatter_step(a, note, me, roots, 4, ranks)
    b, _ = scatter_step(b, None, me, roots, 2, ranks)
    bit = 8
    while bit < ranks:
        a, note = middle_step(a, note, me, roots, bit, ranks)
        b, _ = middle_step(b, None, me, roots, bit, ranks)
        bit *= 2
    a, b = gather_step(a, me, 4, ranks), gather_step(b, me, 2, ranks)
    a, b, note = lax.optimization_barrier((a, b, note))
    a, b = gather_step(a, me, 2, ranks), gather_step(b, me, 4, ranks)
    return gather_step(jnp.concatenate([a, b], axis=1), me, 1, ranks), note


def nonzero_tiles(mask):
    ones = (mask != 0).astype(jnp.int32)
    places = jnp.arange(MT * KPT, dtype=jnp.int32)
    earlier = (places[None, :] < places[:, None]).astype(jnp.int32)
    before = jnp.sum(ones[..., None, :] * earlier, axis=-1)
    hit = ones[..., None, :] * (before[..., None, :] == jnp.arange(PCAP)[:, None])
    return jnp.sum(hit * places, axis=-1)


def ranks_of(owners, keep, direct):
    order = jnp.arange(TILES)
    earlier = order[None, :] < order[:, None]
    same = (owners[:, :, None] == owners[:, None, :]) & earlier
    rank = jnp.sum(same, axis=2, dtype=jnp.int32)
    kept_rank = jnp.sum(same & keep[:, None, :], axis=2, dtype=jnp.int32)
    spills = keep & (kept_rank >= direct)
    spill_place = jnp.sum(spills[:, None, :] & earlier, axis=2, dtype=jnp.int32)
    return rank, kept_rank, spills, spill_place


def prepare_kernel(
    slots_each, direct, me_ref, mask_ref, owner_ref, keep_ref, panel_ref,
    own_ref, give_ref, short_ref, long_ref, spill_ref, kept, sem,
):
    half = PCAP // 2
    high = me_ref[0] % 2

    def tile_copy(place, ref, row, number):
        m, k = place // KPT, place % KPT
        return pltpu.make_async_copy(
            panel_ref.at[m * TILE : (m + 1) * TILE, k * TILE : (k + 1) * TILE],
            ref.at[pl.ds(pl.multiple_of(row * TILE, TILE), TILE)],
            sem.at[number],
        )

    number = jnp.int32(0)
    for place in range(MT * KPT):
        here = mask_ref[place] != 0
        upper = (number >= half).astype(jnp.int32)
        row = jnp.minimum(number - upper * half, half - 1)
        slot = jnp.minimum(number, PCAP - 1)

        @pl.when(here & (upper == high))
        def _(place=place, row=row, slot=slot):
            tile_copy(place, own_ref, row, slot).start()

        @pl.when(here & (upper != high))
        def _(place=place, row=row, slot=slot):
            tile_copy(place, give_ref, row, slot).start()

        number = number + here.astype(jnp.int32)

    column = lax.broadcasted_iota(jnp.int32, (16, TILE), 1)
    note = jnp.zeros((16, TILE), jnp.float32)
    for place in range(MT * KPT):
        note = jnp.where(column == TILES + place, mask_ref[place].astype(jnp.float32), note)
    for e in range(SPILL):
        spill_ref[e] = -1
    for o in range(kept.shape[0]):
        kept[o] = 0
    spilled_count = jnp.int32(0)
    for q in range(TILES):
        owner = owner_ref[q]
        keep = (keep_ref[q % MT * NT_DEV + q // MT] != 0).astype(jnp.int32)
        rank = kept[owner]
        kept[owner] = rank + keep
        over = keep * (rank >= direct).astype(jnp.int32)
        short_ref[q] = jnp.where(keep * (1 - over) != 0, owner * direct + rank, -1)
        long_ref[q] = jnp.where(keep != 0, owner * slots_each + rank, -1)

        @pl.when((over != 0) & (spilled_count < SPILL))
        def _(q=q, spilled_count=spilled_count):
            spill_ref[jnp.minimum(spilled_count, SPILL - 1)] = q

        spilled_count = spilled_count + over
        note = jnp.where(column == q, (owner * 2 + keep).astype(jnp.float32), note)
    note = jnp.where(column == TILES + MT * KPT, spilled_count.astype(jnp.float32), note)
    give_ref[half * TILE : half * TILE + 16, :] = note.astype(jnp.bfloat16)
    for number in range(PCAP):
        tile_copy(0, own_ref, 0, number).wait()


def prepare(panel, me, mask, owners, keep, ranks, slots_each, direct):
    rows = PCAP // 2 * TILE
    places = jax.ShapeDtypeStruct((TILES,), jnp.int32)
    return pl.pallas_call(
        functools.partial(prepare_kernel, slots_each, direct),
        out_shape=(
            jax.ShapeDtypeStruct((rows, TILE), jnp.bfloat16),
            jax.ShapeDtypeStruct((rows + 16, TILE), jnp.bfloat16),
            places,
            places,
            jax.ShapeDtypeStruct((SPILL,), jnp.int32),
        ),
        in_specs=[SMEM, SMEM, SMEM, SMEM, ANY],
        out_specs=(VMEM, VMEM, SMEM, SMEM, SMEM),
        scratch_shapes=[pltpu.SMEM((ranks,), jnp.int32), pltpu.SemaphoreType.DMA((PCAP,))],
        name="prepare",
    )(me, mask, owners, keep, panel)


def pair_up(tiles):
    m, k = (tiles // KPT).reshape(-1), (tiles % KPT).reshape(-1)
    count = SECTIONS * PCAP
    order = jnp.arange(count, dtype=jnp.int32)
    rows = jnp.arange(MT, dtype=jnp.int32)
    in_row = m[None, :] == rows[:, None]
    pairs = (jnp.sum(in_row, axis=1, dtype=jnp.int32) + 1) // 2
    first = jnp.sum(jnp.where(rows[None, :] < rows[:, None], pairs[None, :], 0), axis=1)
    nth = jnp.sum((m[None, :] == m[:, None]) & (order[None, :] < order[:, None]), axis=1, dtype=jnp.int32)
    member = 2 * jnp.sum(jnp.where(in_row, first[:, None], 0), axis=0) + nth
    hit = member[None, :] == jnp.arange(2 * PAIRS, dtype=jnp.int32)[:, None]
    panel_tile = jnp.sum(jnp.where(hit, order, 0), axis=1)
    none = SECTIONS * KPT
    v_tile = none + jnp.sum(jnp.where(hit, order // PCAP * KPT + k - none, 0), axis=1)
    pair_row = jnp.sum(first[None, 1:] <= jnp.arange(PAIRS, dtype=jnp.int32)[:, None], axis=1, dtype=jnp.int32)
    return pair_row, panel_tile, v_tile


def pair_product(pair, panel_tile_ref, v_tile_ref, amp_ref, v_ref, mask_ref):
    left, right = [], []
    for i in (2 * pair, 2 * pair + 1):
        v_tile = v_tile_ref[i]
        v_row = jnp.minimum(v_tile, SECTIONS * KPT - 1)
        left.append(amp_ref[pl.ds(pl.multiple_of(panel_tile_ref[i] * TILE, TILE), TILE), :])
        right.append(v_ref[pl.ds(pl.multiple_of(v_row * TILE, TILE), TILE), :] * mask_ref[v_tile])
    return jnp.dot(
        jnp.concatenate(left, axis=1), jnp.concatenate(right, axis=0), preferred_element_type=jnp.float32
    )


def ladder_kernel(
    row_ref, panel_tile_ref, v_tile_ref, place_ref, amp_ref, v_ref, mask_ref, out_ref, acc, staged, sem
):
    step = pl.program_id(0)
    acc[...] = jnp.zeros_like(acc)
    for pair in range(PAIRS):
        acc[row_ref[pair]] += pair_product(pair, panel_tile_ref, v_tile_ref, amp_ref, v_ref, mask_ref)

    def copy_to(q, place):
        return pltpu.make_async_copy(staged.at[q], out_ref.at[place], sem.at[q])

    for j in range(STEP_TILES):
        for m in range(MT):
            q = (step * STEP_TILES + j) * MT + m
            staged[q] = acc[m, :, j * TILE : (j + 1) * TILE].astype(jnp.bfloat16)

            @pl.when(place_ref[q] >= 0)
            def _():
                copy_to(q, place_ref[q]).start()

    @pl.when(step == NT_DEV // STEP_TILES - 1)
    def _():
        def finish(q, carry):
            @pl.when(place_ref[q] >= 0)
            def _():
                copy_to(q, 0).wait()

            return carry

        lax.fori_loop(0, TILES, finish, 0)


def ladder(amp, pairs, v, v_rows, places, slots):
    macs = 2 * PAIRS * TILE * TILE * NT_DEV * TILE
    return pl.pallas_call(
        ladder_kernel,
        out_shape=jax.ShapeDtypeStruct((slots, TILE, TILE), jnp.bfloat16),
        grid=(NT_DEV // STEP_TILES,),
        in_specs=[
            SMEM,
            SMEM,
            SMEM,
            SMEM,
            VMEM,
            pl.BlockSpec((SECTIONS * KPT * TILE, STEP_COLS), lambda j: (0, j)),
            pl.BlockSpec((SECTIONS * KPT + 1, 1, STEP_COLS), lambda j: (0, 0, j)),
        ],
        out_specs=HBM,
        scratch_shapes=[
            pltpu.VMEM((MT, TILE, STEP_COLS), jnp.float32),
            pltpu.VMEM((TILES, TILE, TILE), jnp.bfloat16),
            pltpu.SemaphoreType.DMA((TILES,)),
        ],
        compiler_params=pltpu.CompilerParams(vmem_limit_bytes=58 * 1024 * 1024),
        cost_estimate=pl.CostEstimate(flops=4 * macs, bytes_accessed=24 * 1024 * 1024, transcendentals=0),
        name="ladder",
    )(*pairs, places, amp, v, v_rows)


def spill_kernel(
    tile_ref, row_ref, panel_tile_ref, v_tile_ref, amp_ref, v_ref, mask_ref, out_ref, acc
):
    acc[...] = jnp.zeros_like(acc)
    tile = tile_ref[pl.program_id(0)]
    for pair in range(PAIRS):

        @pl.when((tile >= 0) & (row_ref[pair] == lax.rem(tile, MT)))
        def _():
            acc[...] += pair_product(pair, panel_tile_ref, v_tile_ref, amp_ref, v_ref, mask_ref)

    out_ref[0] = acc[...].astype(jnp.bfloat16)


def spilled(amp, pairs, v, v_rows, tiles):
    def column(e, tile_ref, *_):
        return jnp.maximum(tile_ref[e], 0) // MT

    return pl.pallas_call(
        spill_kernel,
        out_shape=jax.ShapeDtypeStruct((SPILL, TILE, TILE), jnp.bfloat16),
        grid_spec=pltpu.PrefetchScalarGridSpec(
            num_scalar_prefetch=4,
            grid=(SPILL,),
            in_specs=[
                VMEM,
                pl.BlockSpec((SECTIONS * KPT * TILE, TILE), lambda e, *refs: (0, column(e, *refs))),
                pl.BlockSpec((SECTIONS * KPT + 1, 1, TILE), lambda e, *refs: (0, 0, column(e, *refs))),
            ],
            out_specs=pl.BlockSpec((1, TILE, TILE), lambda e, *refs: (e, 0, 0)),
            scratch_shapes=[pltpu.VMEM((TILE, TILE), jnp.float32)],
        ),
        compiler_params=pltpu.CompilerParams(vmem_limit_bytes=32 * 1024 * 1024),
        name="spilled",
    )(tiles, *pairs, amp, v, v_rows)


def place_kernel(
    slots, split, reach, table_ref, direct_ref, near_ref, far_ref, out_ref, zero, held, in_sem, out_sem
):
    zero[...] = jnp.zeros_like(zero)

    def fetch(ref, place, j):
        return pltpu.make_async_copy(ref.at[place], held.at[j], in_sem.at[j])

    def begin(j, carry):
        source = table_ref[j]

        @pl.when((source >= 0) & (source < split))
        def _():
            fetch(direct_ref, source, j).start()

        @pl.when((source >= split) & (source < split + reach))
        def _():
            fetch(near_ref, source - split, j).start()

        @pl.when(source >= split + reach)
        def _():
            fetch(far_ref, source - split - reach, j).start()

        @pl.when(source < 0)
        def _():
            pltpu.make_async_copy(zero, out_ref.at[j], out_sem.at[j]).start()

        return carry

    def forward(j, carry):
        @pl.when(table_ref[j] >= 0)
        def _():
            fetch(direct_ref, 0, j).wait()
            pltpu.make_async_copy(held.at[j], out_ref.at[j], out_sem.at[j]).start()

        return carry

    def finish(j, carry):
        pltpu.make_async_copy(zero, out_ref.at[j], out_sem.at[j]).wait()
        return carry

    lax.fori_loop(0, slots, begin, 0)
    lax.fori_loop(0, slots, forward, 0)
    lax.fori_loop(0, slots, finish, 0)


def place_tiles(table, direct, near_spill, far_spill):
    slots, split, reach = table.shape[0], direct.shape[0], near_spill.shape[0]
    return pl.pallas_call(
        functools.partial(place_kernel, slots, split, reach),
        out_shape=jax.ShapeDtypeStruct((slots, TILE, TILE), jnp.bfloat16),
        in_specs=[SMEM, HBM, HBM, HBM],
        out_specs=HBM,
        scratch_shapes=[
            pltpu.VMEM((TILE, TILE), jnp.bfloat16),
            pltpu.VMEM((slots, TILE, TILE), jnp.bfloat16),
            pltpu.SemaphoreType.DMA((slots,)),
            pltpu.SemaphoreType.DMA((slots,)),
        ],
        compiler_params=pltpu.CompilerParams(vmem_limit_bytes=58 * 1024 * 1024),
        name="place_tiles",
    )(table, direct, near_spill, far_spill)


def exchange(tiles, ranks):
    count = tiles.shape[0] // ranks
    sent = tiles.reshape(ranks, count, TILE, TILE)
    return lax.all_to_all(sent, "row", split_axis=0, concat_axis=0, tiled=True).reshape(
        ranks * count, TILE, TILE
    )


def local(t2_panels, t2_mask, v_blocks, v_mask, r_mask, owner_map, section_owner):
    ranks, groups = lax.axis_size("row"), lax.axis_size("groups")
    me = lax.axis_index("row")
    slots_each = max(2, 2 * TILES // ranks)
    direct = slots_each // 2
    top = ranks // 2
    roots = section_owner

    own, give, short_places, long_places, spill_tiles = prepare(
        t2_panels[0],
        me.reshape(1),
        t2_mask.reshape(MT * KPT),
        owner_map.reshape(TILES),
        r_mask.reshape(TILES),
        ranks,
        slots_each,
        direct,
    )
    amp, notes = spread(own, give, me, roots, ranks)
    amp = amp.reshape(SECTIONS * PCAP * TILE, TILE)

    notes = notes[:, : TILES + MT * KPT + 1].astype(jnp.int32)
    owners, keep = notes[:, :TILES] // 2, notes[:, :TILES] % 2 != 0
    most = jnp.max(notes[:, -1:], axis=0, keepdims=True)
    worst = most
    for turn in range(1, groups):
        worst = jnp.maximum(
            worst, lax.ppermute(most, "groups", [(g, (g + turn) % groups) for g in range(groups)])
        )
    pairs = pair_up(nonzero_tiles(jnp.take(notes[:, TILES:-1], roots, axis=0)))
    rank, kept_rank, spills, spill_place = ranks_of(owners, keep, direct)

    v = v_blocks.reshape(SECTIONS * KPT * TILE, NT_DEV * TILE)
    v_rows = jnp.repeat(v_mask.reshape(SECTIONS * KPT, 1, NT_DEV).astype(jnp.bfloat16), TILE, axis=2)
    v_rows = jnp.pad(v_rows, ((0, 1), (0, 0), (0, 0)))

    device = jnp.arange(ranks, dtype=jnp.int32)[:, None]
    slot = jnp.arange(slots_each, dtype=jnp.int32)
    arrives = ((owners == me) & keep)[:, None, :] & (rank[:, None, :] == slot[None, :, None])

    def table_of(origin):
        return (jnp.sum(jnp.where(arrives, origin[:, None, :] + 1, 0), axis=2) - 1).reshape(-1)

    split = ranks * direct
    reach = ranks // 2 * SPILL
    spill_from = ((device ^ me) & top) // top * reach + (device & (top - 1)) * SPILL
    short_table = table_of(
        jnp.where(spills, split + spill_from + spill_place, device * direct + kept_rank)
    )
    long_table = table_of(device * slots_each + kept_rank)
    halves = [list(range(top)), list(range(top, ranks))]

    def short(amp, v, v_rows, spill_tiles, places, table, _, __):
        spill = spilled(amp, pairs, v, v_rows, spill_tiles)
        near_spill = lax.all_gather(spill, "row", axis=0, tiled=True, axis_index_groups=halves)
        other = swap(spill, top, ranks)
        tiles = ladder(amp, pairs, v, v_rows, places, split)
        other, tiles = lax.optimization_barrier((other, tiles))
        far_spill = lax.all_gather(other, "row", axis=0, tiled=True, axis_index_groups=halves)
        return place_tiles(table, exchange(tiles, ranks), near_spill, far_spill)

    def long(amp, v, v_rows, _, __, ___, places, table):
        tiles = ladder(amp, pairs, v, v_rows, places, ranks * slots_each)
        unused = jnp.zeros((1, TILE, TILE), jnp.bfloat16)
        return place_tiles(table, exchange(tiles, ranks), unused, unused)

    delivered = lax.cond(
        worst[0, 0] <= SPILL,
        short,
        long,
        amp,
        v,
        v_rows,
        spill_tiles,
        short_places,
        short_table,
        long_places,
        long_table,
    )
    return delivered.reshape(ranks, slots_each, TILE, TILE)


def solution(mesh):
    placed = (
        P(("groups", "row"), None, None),
        P(("groups", "row"), None, None),
        P("groups", None, "row"),
        P("groups", None, "row"),
        P("groups", "row"),
        P(("groups", "row"), None, None),
        P("groups"),
    )
    return jax.shard_map(
        local,
        mesh=mesh,
        in_specs=placed,
        out_specs=P(("groups", "row"), None, None, None),
        check_vma=False,
    )
```

time: 244 us -> 213 us (0.87)
  waiting for transfers between devices: 165 us -> 131 us
    all_to_all x1, waiting for transfers between devices: 130 us -> 24.1 us  [exchange(): lax.all_to_all(sent, 'row', split_axis=0, concat_axis=0, tiled=True)]
    all_gather x1 -> x2, waiting for transfers between devices: 0.01 us -> 66.5 us  [the longest x1 62.6 us: short(): lax.all_gather(other, 'row', axis=0, tiled=True, axis_index_groups=halves)]
    ppermute x16 -> x13, waiting for transfers between devices: 32.3 us -> 39.8 us  [swap(): return lax.ppermute(x, 'row', [(i, i ^ bit) for i in range(ranks)])]
    cond x4, local copies, waits for them, and re-layouts: 4.79 us -> 0.77 us
    reshape x2 -> x3, local copies, waits for them, and re-layouts: 0.17 us -> 3.21 us  [the longest x1 1.34 us: local(): r_mask.reshape(TILES)]
    all_to_all x1, starting transfers between devices: 5.02 us -> 7.65 us  [exchange(): lax.all_to_all(sent, 'row', split_axis=0, concat_axis=0, tiled=True)]
    ppermute x16 -> x13, starting transfers between devices: 16.6 us -> 16.1 us  [swap(): return lax.ppermute(x, 'row', [(i, i ^ bit) for i in range(ranks)])]
    pallas_call x3 -> x4, Pallas kernels: 23.9 us -> 23.9 us  [the longest x1 11.1 us: ladder(): pl.pallas_call(ladder_kernel, out_shape=jax.ShapeDtypeStruct((slots, TILE...]
  transfers between devices with their start and end apart: 19 -> 17, of which waited for: 13 -> 14; matrix products, arithmetic and copies ran while one was open for 2% -> 2% of each run, Pallas kernels for 0% -> 5%
where the time goes in v1:
time: 213 us; the launch traced here: 210 us
  waiting for transfers between devices  131 us (62%)
  starting transfers between devices  25.5 us (12%)
  Pallas kernels  23.9 us (11%)
  between operations  15.1 us (7%)
  other arithmetic  7.96 us (4%)
  local copies, waits for them, and re-layouts  6.29 us (3%)
    all_gather x1, waiting for transfers between devices, short(): lax.all_gather(other, 'row', axis=0, tiled=True, axis_index_groups=halves)  62.6 us
    ppermute x13, waiting for transfers between devices, swap(): return lax.ppermute(x, 'row', [(i, i ^ bit) for i in range(ranks)])  39.8 us
    all_to_all x1, waiting for transfers between devices, exchange(): lax.all_to_all(sent, 'row', split_axis=0, concat_axis=0, tiled=True)  24.1 us
    ppermute x13, starting transfers between devices, swap(): return lax.ppermute(x, 'row', [(i, i ^ bit) for i in range(ranks)])  16.1 us
    pallas_call x1, Pallas kernels, ladder(): pl.pallas_call(ladder_kernel, out_shape=jax.ShapeDtypeStruct((slots, TILE...  11.1 us
    all_to_all x1, starting transfers between devices, exchange(): lax.all_to_all(sent, 'row', split_axis=0, concat_axis=0, tiled=True)  7.65 us
    pallas_call x1, Pallas kernels, place_tiles(): pl.pallas_call(functools.partial(place_kernel, slots, split, reach), out_...  5.35 us
  transfers between devices with their start and end apart: 17, of which 14 were waited for; matrix products, arithmetic and copies ran while one was open for 2% of the time, Pallas kernels for 5%

profile of v1, /device:TPU:16, one launch (start us, length us, event | category | flops | bytes accessed | tf_op | source)
XLA Modules:
  0.0 210.2 jit_solution(10001461123599363537)
XLA Ops:
  6.5 1.3 reshape.277.mask_ref
  7.8 1.3 reshape.279.keep_ref
  9.1 0.8 copy.32
  10.5 3.3 %prepare.1 = (bf16[1280,256]{1,0:T(8,128)(2,1)}, bf16[1296,256]{1,0:T(8,128)(2,1)}, s32[32]{0:T(128)S(1)}, s32[32]{0:T(128)S(1)}, s32[3]{0:T(128)S(1)}) custom-call(s32[1]{0:T(128)} %bitcast.9.me_ref, s32[20]{0:T(128)} %reshape.277.mask_ref, s32[32]{0:T(128)} %reshape.278.owner_ref, s32[32]{0:T(128)} %reshape.279.keep_ref, bf16[1024,1280]{1,0:T(8,128)(2,1)} %bitcast.34), custom_call_target="tpu_custom_call" | custom-call | tf_op jit(solution)/shard_map/prepare/pallas_call | solution.py:178
  13.9 2.3 %collective-permute-done.1 = bf16[1296,256]{1,0:T(8,128)(2,1)S(1)} collective-permute-done((bf16[1296,256]{1,0:T(8,128)(2,1)}, bf16[1296,256]{1,0:T(8,128)(2,1)S(1)}, u32[]{:S(2)}, u32[]{:S(2)}) %collective-permute-start.1) | collective-permute-done | bytes 663584 | tf_op jit(solution)/shard_map/ppermute | solution.py:28
  16.2 1.3 broadcast_select_fusion
  17.6 1.6 collective-permute-start.6
  19.9 1.6 collective-permute-start.2
  21.5 8.0 %collective-permute-done.2 = bf16[642,256]{1,0:T(8,128)(2,1)S(1)} collective-permute-done((bf16[642,256]{1,0:T(8,128)(2,1)S(1)}, bf16[642,256]{1,0:T(8,128)(2,1)S(1)}, u32[]{:S(2)}, u32[]{:S(2)}) %collective-permute-start.2) | collective-permute-done | bytes 328736 | tf_op jit(solution)/shard_map/ppermute | solution.py:28
  29.8 1.6 collective-permute-start.7
  32.0 3.2 %collective-permute-done.7 = bf16[2,160,256]{2,1,0:T(8,128)(2,1)S(1)} collective-permute-done((bf16[2,160,256]{2,1,0:T(8,128)(2,1)S(1)}, bf16[2,160,256]{2,1,0:T(8,128)(2,1)S(1)}, u32[]{:S(2)}, u32[]{:S(2)}) %collective-permute-start.7) | collective-permute-done | bytes 163872 | tf_op jit(solution)/shard_map/ppermute | solution.py:28
  35.7 3.0 %collective-permute-done.3 = bf16[324,256]{1,0:T(8,128)(2,1)S(1)} collective-permute-done((bf16[324,256]{1,0:T(8,128)(2,1)S(1)}, bf16[324,256]{1,0:T(8,128)(2,1)S(1)}, u32[]{:S(2)}, u32[]{:S(2)}) %collective-permute-start.3) | collective-permute-done | bytes 165920 | tf_op jit(solution)/shard_map/ppermute | solution.py:28
  39.1 8.7 %collective-permute-done.4 = bf16[328,256]{1,0:T(8,128)(2,1)S(1)} collective-permute-done((bf16[328,256]{1,0:T(8,128)(2,1)S(1)}, bf16[328,256]{1,0:T(8,128)(2,1)S(1)}, u32[]{:S(2)}, u32[]{:S(2)}) %collective-permute-start.4) | collective-permute-done | bytes 167968 | tf_op jit(solution)/shard_map/ppermute | solution.py:28
  48.0 1.5 collective-permute-start.9
  49.5 3.6 %collective-permute-start.5 = (bf16[2,160,256]{2,1,0:T(8,128)(2,1)S(1)}, bf16[2,160,256]{2,1,0:T(8,128)(2,1)S(1)}, u32[]{:S(2)}, u32[]{:S(2)}) collective-permute-start(bf16[2,160,256]{2,1,0:T(8,128)(2,1)S(1)} %get-tuple-element.381), channel_id=1, source_target_pairs={{0,4},{1,5},{2,6},{3,7},{4,0},{5,1},{6,2},{7,3},{8,12},{9,13},{10,... | collective-permute-start | bytes 491528 | tf_op jit(solution)/shard_map/ppermute | solution.py:28
  53.5 2.9 %collective-permute-done.5 = bf16[2,160,256]{2,1,0:T(8,128)(2,1)S(1)} collective-permute-done((bf16[2,160,256]{2,1,0:T(8,128)(2,1)S(1)}, bf16[2,160,256]{2,1,0:T(8,128)(2,1)S(1)}, u32[]{:S(2)}, u32[]{:S(2)}) %collective-permute-start.5) | collective-permute-done | bytes 163872 | tf_op jit(solution)/shard_map/ppermute | solution.py:28
  59.6 1.5 collective-permute-start.10
  61.7 2.0 collective-permute-start.12
  63.8 4.5 %collective-permute-done.11 = bf16[2,320,256]{2,1,0:T(8,128)(2,1)S(1)} collective-permute-done((bf16[2,320,256]{2,1,0:T(8,128)(2,1)S(1)}, bf16[2,320,256]{2,1,0:T(8,128)(2,1)S(1)}, u32[]{:S(2)}, u32[]{:S(2)}) %collective-permute-start.11) | collective-permute-done | bytes 327712 | tf_op jit(solution)/shard_map/ppermute | solution.py:28
  69.2 0.7 convert_reduce_fusion
  71.3 0.8 collective-permute-done.13
  72.8 130.5 %conditional.1 = (bf16[16,4,256,256]{3,2,1,0:T(8,128)(2,1)}) conditional(s32[]{:T(128)} %bitcast.18, (s32[16,1]{0,1:T(1,128)S(1)}, s32[16,32]{1,0:T(8,128)S(1)}, pred[16,4,32]{2,1,0:T(4,128)(4,1)S(1)}, s32[16,4,32]{2,1,0:T(4,128)S(1)}, s32[64]{0:T(128)S(1)}, /*index=5*/s32[12]{0:T(128)S(1)}, s32[24]{0:T(128)S(1)}, s32[24]{0:T(128)S(1)}, ...), branch_computations={%region_12.14_spmd, %region_14.17_spmd} | conditional | flops 12884924416 | bytes 62489256 | solution.py:458
  73.2 4.2 %spilled.1 = bf16[3,256,256]{2,1,0:T(8,128)(2,1)} custom-call(s32[3]{0:T(128)S(1)} %get-tuple-element.174.tile_ref, s32[12]{0:T(128)S(1)} %get-tuple-element.175.row_ref, s32[24]{0:T(128)S(1)} %get-tuple-element.176.panel_tile_ref, s32[24]{0:T(128)S(1)} %get-tuple-element.177.v_tile_ref, bf16[5120,256]{1,0:T(8,128)(2,1)S(1)} %get-tuple-element.178.amp_ref, ...), custom_call_target="tpu_custom_call" | custom-call | tf_op jit(solution)/shard_map/cond/branch_1_fun/spilled/pallas_call | solution.py:301
  77.4 2.5 %collective-permute-start = (bf16[3,256,256]{2,1,0:T(8,128)(2,1)}, bf16[3,256,256]{2,1,0:T(8,128)(2,1)S(1)}, u32[]{:S(2)}, u32[]{:S(2)}) collective-permute-start(bf16[3,256,256]{2,1,0:T(8,128)(2,1)} %spilled.1), channel_id=1, source_target_pairs={{0,8},{1,9},{2,10},{3,11},{4,12},{5,13},{6,14},{7,15},{8,0},{9,1},... | collective-permute-start | bytes 1179656 | tf_op jit(solution)/shard_map/cond/branch_1_fun/ppermute | solution.py:28
  79.9 11.1 %ladder.3 = bf16[32,256,256]{2,1,0:T(8,128)(2,1)} custom-call(s32[12]{0:T(128)S(1)} %get-tuple-element.175.row_ref, s32[24]{0:T(128)S(1)} %get-tuple-element.176.panel_tile_ref, s32[24]{0:T(128)S(1)} %get-tuple-element.177.v_tile_ref, s32[32]{0:T(128)S(1)} %get-tuple-element.181.place_ref, bf16[5120,256]{1,0:T(8,128)(2,1)S(1)} %get-tuple-element.178.amp_ref, ...), custom_call_target="tpu_custom_call" | custom-call | flops 12884901888 | bytes 25165824 | tf_op jit(solution)/shard_map/cond/branch_1_fun/ladder/pallas_call | solution.py:258
  91.0 5.6 %collective-permute-done = bf16[3,256,256]{2,1,0:T(8,128)(2,1)S(1)} collective-permute-done((bf16[3,256,256]{2,1,0:T(8,128)(2,1)}, bf16[3,256,256]{2,1,0:T(8,128)(2,1)S(1)}, u32[]{:S(2)}, u32[]{:S(2)}) %collective-permute-start) | collective-permute-done | bytes 393248 | tf_op jit(solution)/shard_map/cond/branch_1_fun/ppermute | solution.py:28
  96.6 0.8 copy-done.1
  97.3 7.6 %all-to-all-start.1 = ((bf16[16,2,256,256]{3,2,1,0:T(8,128)(2,1)}), bf16[16,2,256,256]{3,2,1,0:T(8,128)(2,1)}, u32[]{:S(2)}, u32[]{:S(2)}) async-start(bf16[16,2,256,256]{3,2,1,0:T(8,128)(2,1)} %bitcast.33), calls=%async_computation.1 | async-start | bytes 8388608 | tf_op jit(solution)/shard_map/cond/branch_1_fun/all_to_all | solution.py:387
  107.2 3.9 %all-gather.3.cloned.1.call-done.near_ref = bf16[24,256,256]{2,1,0:T(8,128)(2,1)} async-done(((bf16[3,256,256]{2,1,0:T(8,128)(2,1)}), bf16[24,256,256]{2,1,0:T(8,128)(2,1)}) %all-gather.3.cloned.1.call-update) | async-done | bytes 3145744 | tf_op jit(solution)/shard_map/cond/branch_1_fun/all_gather | solution.py:446
  111.1 62.6 %all-gather.5.cloned.1.call-done.far_ref = bf16[24,256,256]{2,1,0:T(8,128)(2,1)} async-done(((bf16[3,256,256]{2,1,0:T(8,128)(2,1)}), bf16[24,256,256]{2,1,0:T(8,128)(2,1)}) %all-gather.5.cloned.1.call-update) | async-done | bytes 3145744 | tf_op jit(solution)/shard_map/cond/branch_1_fun/all_gather | solution.py:450
  173.6 24.1 %all-to-all-done.1 = bf16[16,2,256,256]{3,2,1,0:T(8,128)(2,1)} async-done(((bf16[16,2,256,256]{3,2,1,0:T(8,128)(2,1)}), bf16[16,2,256,256]{3,2,1,0:T(8,128)(2,1)}, u32[]{:S(2)}, u32[]{:S(2)}) %all-to-all-start.1) | async-done | bytes 4194336 | tf_op jit(solution)/shard_map/cond/branch_1_fun/all_to_all | solution.py:387
  197.8 5.4 %place_tiles.3 = bf16[64,256,256]{2,1,0:T(8,128)(2,1)} custom-call(s32[64]{0:T(128)} %sub.25.table_ref, bf16[32,256,256]{2,1,0:T(8,128)(2,1)} %bitcast.7.direct_ref, bf16[24,256,256]{2,1,0:T(8,128)(2,1)} %all-gather.3.cloned.1.call-done.near_ref, bf16[24,256,256]{2,1,0:T(8,128)(2,1)} %all-gather.5.cloned.1.call-done.far_ref), custom_call_target="tpu_custom_call" | custom-call | tf_op jit(solution)/shard_map/cond/branch_1_fun/place_tiles/pallas_call | solution.py:368
  (103 shorter events, 11.6 us)
Async XLA Ops:
  6.5 7.3 %copy-start.3 = (s32[2]{0:T(128)S(1)}, s32[2]{0:T(128)}, u32[]{:S(2)}) copy-start(s32[2]{0:T(128)} %param.15) | copy-start | bytes 28
  13.8 2.4 %collective-permute-start.1 = (bf16[1296,256]{1,0:T(8,128)(2,1)}, bf16[1296,256]{1,0:T(8,128)(2,1)S(1)}, u32[]{:S(2)}, u32[]{:S(2)}) collective-permute-start(bf16[1296,256]{1,0:T(8,128)(2,1)} %get-tuple-element.193), channel_id=1, source_target_pairs={{0,1},{1,0},{2,3},{3,2},{4,5},{5,4},{6,7},{7,6},{8,9},{9,8},{10,11... | collective-permute-start | bytes 1990664 | tf_op jit(solution)/shard_map/ppermute | solution.py:28
  17.6 12.0 %collective-permute-start.6 = (bf16[2,320,256]{2,1,0:T(8,128)(2,1)S(1)}, bf16[2,320,256]{2,1,0:T(8,128)(2,1)S(1)}, u32[]{:S(2)}, u32[]{:S(2)}) collective-permute-start(bf16[2,320,256]{2,1,0:T(8,128)(2,1)S(1)} %get-tuple-element.359), channel_id=1, source_target_pairs={{0,4},{1,5},{2,6},{3,7},{4,0},{5,1},{6,2},{7,3},{8,12},{9,13},{10,... | collective-permute-start | bytes 983048 | tf_op jit(solution)/shard_map/ppermute | solution.py:28
  19.9 9.6 %collective-permute-start.2 = (bf16[642,256]{1,0:T(8,128)(2,1)S(1)}, bf16[642,256]{1,0:T(8,128)(2,1)S(1)}, u32[]{:S(2)}, u32[]{:S(2)}) collective-permute-start(bf16[642,256]{1,0:T(8,128)(2,1)S(1)} %pad_maximum_fusion.2), channel_id=1, source_target_pairs={{0,2},{1,3},{2,0},{3,1},{4,6},{5,7},{6,4},{7,5},{8,10},{9,11},{10,... | collective-permute-start | bytes 986120 | tf_op jit(solution)/shard_map/ppermute | solution.py:28
  29.6 9.3 %copy-start.2 = (s32[2,5,8]{2,0,1:T(2,128)S(1)}, s32[2,5,8]{2,0,1:T(2,128)}, u32[]{:S(2)}) copy-start(s32[2,5,8]{2,0,1:T(2,128)} %param.12) | copy-start | bytes 964
  29.8 5.4 %collective-permute-start.7 = (bf16[2,160,256]{2,1,0:T(8,128)(2,1)S(1)}, bf16[2,160,256]{2,1,0:T(8,128)(2,1)S(1)}, u32[]{:S(2)}, u32[]{:S(2)}) collective-permute-start(bf16[2,160,256]{2,1,0:T(8,128)(2,1)S(1)} %get-tuple-element.385), channel_id=1, source_target_pairs={{0,2},{1,3},{2,0},{3,1},{4,6},{5,7},{6,4},{7,5},{8,10},{9,11},{10,... | collective-permute-start | bytes 491528 | tf_op jit(solution)/shard_map/ppermute | solution.py:28
  31.5 7.2 %collective-permute-start.3 = (bf16[324,256]{1,0:T(8,128)(2,1)S(1)}, bf16[324,256]{1,0:T(8,128)(2,1)S(1)}, u32[]{:S(2)}, u32[]{:S(2)}) collective-permute-start(bf16[324,256]{1,0:T(8,128)(2,1)S(1)} %pad_maximum_fusion.5), channel_id=1, source_target_pairs={{0,4},{1,5},{2,6},{3,7},{4,0},{5,1},{6,2},{7,3},{8,12},{9,13},{10,... | collective-permute-start | bytes 497672 | tf_op jit(solution)/shard_map/ppermute | solution.py:28
  35.3 12.6 %collective-permute-start.8 = (bf16[2,160,256]{2,1,0:T(8,128)(2,1)S(1)}, bf16[2,160,256]{2,1,0:T(8,128)(2,1)S(1)}, u32[]{:S(2)}, u32[]{:S(2)}) collective-permute-start(bf16[2,160,256]{2,1,0:T(8,128)(2,1)S(1)} %select_select_fusion.2), channel_id=1, source_target_pairs={{0,8},{1,9},{2,10},{3,11},{4,12},{5,13},{6,14},{7,15},{8,0},{9,1},... | collective-permute-start | bytes 491528 | tf_op jit(solution)/shard_map/ppermute | solution.py:28
  38.8 9.0 %collective-permute-start.4 = (bf16[328,256]{1,0:T(8,128)(2,1)S(1)}, bf16[328,256]{1,0:T(8,128)(2,1)S(1)}, u32[]{:S(2)}, u32[]{:S(2)}) collective-permute-start(bf16[328,256]{1,0:T(8,128)(2,1)S(1)} %pad_maximum_fusion.6), channel_id=1, source_target_pairs={{0,8},{1,9},{2,10},{3,11},{4,12},{5,13},{6,14},{7,15},{8,0},{9,1},... | collective-permute-start | bytes 503816 | tf_op jit(solution)/shard_map/ppermute | solution.py:28
  48.0 5.4 %collective-permute-start.9 = (bf16[2,160,256]{2,1,0:T(8,128)(2,1)S(1)}, bf16[2,160,256]{2,1,0:T(8,128)(2,1)S(1)}, u32[]{:S(2)}, u32[]{:S(2)}) collective-permute-start(bf16[2,160,256]{2,1,0:T(8,128)(2,1)S(1)} %get-tuple-element.380), channel_id=1, source_target_pairs={{0,2},{1,3},{2,0},{3,1},{4,6},{5,7},{6,4},{7,5},{8,10},{9,11},{10,... | collective-permute-start | bytes 491528 | tf_op jit(solution)/shard_map/ppermute | solution.py:28
  49.5 6.9 %collective-permute-start.5 = (bf16[2,160,256]{2,1,0:T(8,128)(2,1)S(1)}, bf16[2,160,256]{2,1,0:T(8,128)(2,1)S(1)}, u32[]{:S(2)}, u32[]{:S(2)}) collective-permute-start(bf16[2,160,256]{2,1,0:T(8,128)(2,1)S(1)} %get-tuple-element.381), channel_id=1, source_target_pairs={{0,4},{1,5},{2,6},{3,7},{4,0},{5,1},{6,2},{7,3},{8,12},{9,13},{10,... | collective-permute-start | bytes 491528 | tf_op jit(solution)/shard_map/ppermute | solution.py:28
  59.6 10.4 %collective-permute-start.10 = (s32[1,1]{1,0:T(1,128)}, s32[1,1]{1,0:T(1,128)}, u32[]{:S(2)}, u32[]{:S(2)}) collective-permute-start(s32[1,1]{1,0:T(1,128)} %bitcast.17), channel_id=1, source_target_pairs={{0,16},{16,0},{1,17},{17,1},{2,18},{18,2},{3,19},{19,3},{4,20},{20... | collective-permute-start | bytes 20 | tf_op jit(solution)/shard_map/ppermute | solution.py:419
  61.1 7.1 %collective-permute-start.11 = (bf16[2,320,256]{2,1,0:T(8,128)(2,1)S(1)}, bf16[2,320,256]{2,1,0:T(8,128)(2,1)S(1)}, u32[]{:S(2)}, u32[]{:S(2)}) collective-permute-start(bf16[2,320,256]{2,1,0:T(8,128)(2,1)S(1)} %pad_maximum_fusion.3), channel_id=1, source_target_pairs={{0,2},{1,3},{2,0},{3,1},{4,6},{5,7},{6,4},{7,5},{8,10},{9,11},{10,... | collective-permute-start | bytes 983048 | tf_op jit(solution)/shard_map/ppermute | solution.py:28
  61.7 7.2 %collective-permute-start.12 = (bf16[2,320,256]{2,1,0:T(8,128)(2,1)S(1)}, bf16[2,320,256]{2,1,0:T(8,128)(2,1)S(1)}, u32[]{:S(2)}, u32[]{:S(2)}) collective-permute-start(bf16[2,320,256]{2,1,0:T(8,128)(2,1)S(1)} %pad_maximum_fusion.4), channel_id=1, source_target_pairs={{0,4},{1,5},{2,6},{3,7},{4,0},{5,1},{6,2},{7,3},{8,12},{9,13},{10,... | collective-permute-start | bytes 983048 | tf_op jit(solution)/shard_map/ppermute | solution.py:28
  69.0 3.1 %collective-permute-start.13 = (bf16[2,1280,256]{2,1,0:T(8,128)(2,1)S(1)}, bf16[2,1280,256]{2,1,0:T(8,128)(2,1)S(1)}, u32[]{:S(2)}, u32[]{:S(2)}) collective-permute-start(bf16[2,1280,256]{2,1,0:T(8,128)(2,1)S(1)} %pad_maximum_fusion.1), channel_id=1, source_target_pairs={{0,1},{1,0},{2,3},{3,2},{4,5},{5,4},{6,7},{7,6},{8,9},{9,8},{10,11... | collective-permute-start | bytes 3932168 | tf_op jit(solution)/shard_map/ppermute | solution.py:28
  72.8 38.2 %all-gather.3.cloned.1.call-start = ((), (), s32[]{:S(2)}) async-start(), calls=%async_computation.2 | async-start | bytes 3538944 | tf_op jit(solution)/shard_map/cond/branch_1_fun/all_gather | solution.py:446
  73.2 4.2 %copy-start = (bf16[11,1,2048]{2,1,0:T(2,128)(2,1)}, bf16[11,1,2048]{2,1,0:T(2,128)(2,1)S(1)}, u32[]{:S(2)}) copy-start(bf16[11,1,2048]{2,1,0:T(2,128)(2,1)S(1)} %copy.40.mask_ref) | copy-start | bytes 135172 | tf_op jit(solution)/shard_map/cond
  77.4 19.2 %collective-permute-start = (bf16[3,256,256]{2,1,0:T(8,128)(2,1)}, bf16[3,256,256]{2,1,0:T(8,128)(2,1)S(1)}, u32[]{:S(2)}, u32[]{:S(2)}) collective-permute-start(bf16[3,256,256]{2,1,0:T(8,128)(2,1)} %spilled.1), channel_id=1, source_target_pairs={{0,8},{1,9},{2,10},{3,11},{4,12},{5,13},{6,14},{7,15},{8,0},{9,1},... | collective-permute-start | bytes 1179656 | tf_op jit(solution)/shard_map/cond/branch_1_fun/ppermute | solution.py:28
  96.6 0.8 copy-start.1
  97.3 100.4 %all-to-all-start.1 = ((bf16[16,2,256,256]{3,2,1,0:T(8,128)(2,1)}), bf16[16,2,256,256]{3,2,1,0:T(8,128)(2,1)}, u32[]{:S(2)}, u32[]{:S(2)}) async-start(bf16[16,2,256,256]{3,2,1,0:T(8,128)(2,1)} %bitcast.33), calls=%async_computation.1 | async-start | bytes 8388608 | tf_op jit(solution)/shard_map/cond/branch_1_fun/all_to_all | solution.py:387
  105.0 68.7 %all-gather.5.cloned.1.call-start = ((), (), s32[]{:S(2)}) async-start(), calls=%async_computation.3 | async-start | bytes 3538944 | tf_op jit(solution)/shard_map/cond/branch_1_fun/all_gather | solution.py:450
Sparse Core Ops, SparseCore 0:
  77.5 33.4 all-gather.2
  112.7 60.8 all-gather.4

commit v2 on v1

v2 whole, which is shorter than its diff:
```python
import functools

import jax
import jax.numpy as jnp
from jax import lax
from jax.experimental import pallas as pl
from jax.experimental.pallas import tpu as pltpu
from jax.sharding import PartitionSpec as P

TILE = 256
MT = 4
KPT = 5
NT_DEV = 8
SECTIONS = 2
PCAP = 10
TILES = MT * NT_DEV
SPILL = 3
STEP_TILES = 2
STEP_COLS = STEP_TILES * TILE
PAIRS = (SECTIONS * PCAP + MT) // 2
ANY = pl.BlockSpec(memory_space=pl.ANY)
HBM = pl.BlockSpec(memory_space=pltpu.HBM)
SMEM = pl.BlockSpec(memory_space=pltpu.SMEM)
VMEM = pl.BlockSpec(memory_space=pltpu.VMEM)


def swap(x, bit, ranks):
    return lax.ppermute(x, "row", [(i, i ^ bit) for i in range(ranks)])


def swap_with(x, note, bit, ranks):
    rows = x.shape[0] * x.shape[1]
    got = swap(jnp.concatenate([x.reshape(rows, -1), note], axis=0), bit, ranks)
    return got[:rows].reshape(x.shape), got[rows:]


def in_order(high, mine, got, axis):
    return jnp.concatenate([jnp.where(high, got, mine), jnp.where(high, mine, got)], axis=axis)


def near(me, roots, bit):
    return (((me ^ roots) & bit) == 0)[:, None, None]


def scatter_step(x, note, me, roots, bit, ranks):
    half = x.shape[1] // 2
    high = (me & bit) != 0
    low_rows, high_rows = x[:, :half], x[:, half:]
    own, give = jnp.where(high, high_rows, low_rows), jnp.where(high, low_rows, high_rows)
    if note is None:
        got = swap(give, bit, ranks)
    else:
        got, got_note = swap_with(give, note, bit, ranks)
        note = in_order(high, note, got_note, 0)
    return jnp.where(near(me, roots, bit), own, got), note


def middle_step(x, me, roots, bit, ranks):
    return jnp.where(near(me, roots, bit), x, swap(x, bit, ranks))


def gather_step(x, me, bit, ranks):
    return in_order((me & bit) != 0, x, swap(x, bit, ranks), 1)


def most_of_groups(most):
    groups = lax.axis_size("groups")
    worst = most
    for turn in range(1, groups):
        worst = jnp.maximum(
            worst, lax.ppermute(most, "groups", [(g, (g + turn) % groups) for g in range(groups)])
        )
    return worst


def spread(own, give, me, roots, ranks, digest):
    rows = own.shape[0]
    got = swap(give, 1, ranks)
    note = in_order((me & 1) != 0, give[rows : rows + 1], got[rows : rows + 1], 0)
    x = jnp.where(near(me, roots, 1), own[None], got[None, :rows])
    half = rows // 2
    a, b = x[:, :half], x[:, half:]
    a, note = scatter_step(a, note, me, roots, 2, ranks)
    b, _ = scatter_step(b, None, me, roots, 4, ranks)
    a, note = scatter_step(a, note, me, roots, 4, ranks)
    b, _ = scatter_step(b, None, me, roots, 2, ranks)
    bit = 8
    while bit < ranks:
        note = in_order((me & bit) != 0, note, swap(note, bit, ranks), 0)
        bit *= 2
    facts = digest(note)
    bit = 8
    while bit < ranks:
        a = middle_step(a, me, roots, bit, ranks)
        bit *= 2
    b, facts = lax.optimization_barrier((b, facts))
    bit = 8
    while bit < ranks:
        b = middle_step(b, me, roots, bit, ranks)
        bit *= 2
    worst = most_of_groups(facts[0])
    b, worst = lax.optimization_barrier((b, worst))
    a, b = gather_step(a, me, 4, ranks), gather_step(b, me, 2, ranks)
    a, b = gather_step(a, me, 2, ranks), gather_step(b, me, 4, ranks)
    mine = jnp.concatenate([a, b], axis=1)
    return mine, swap(mine, 1, ranks), worst, facts[1:]


def ranks_of(owners, keep, direct):
    order = jnp.arange(TILES)
    earlier = order[None, :] < order[:, None]
    same = (owners[:, :, None] == owners[:, None, :]) & earlier
    rank = jnp.sum(same, axis=2, dtype=jnp.int32)
    kept_rank = jnp.sum(same & keep[:, None, :], axis=2, dtype=jnp.int32)
    spills = keep & (kept_rank >= direct)
    spill_place = jnp.sum(spills[:, None, :] & earlier, axis=2, dtype=jnp.int32)
    return rank, kept_rank, spills, spill_place


def prepare_kernel(
    slots_each, direct, me_ref, mask_ref, owner_ref, keep_ref, panel_ref,
    own_ref, give_ref, short_ref, long_ref, spill_ref, kept, sem,
):
    half = PCAP // 2
    high = me_ref[0] % 2

    def tile_copy(place, ref, row, number):
        m, k = place // KPT, place % KPT
        return pltpu.make_async_copy(
            panel_ref.at[0, m * TILE : (m + 1) * TILE, k * TILE : (k + 1) * TILE],
            ref.at[pl.ds(pl.multiple_of(row * TILE, TILE), TILE)],
            sem.at[number],
        )

    number = jnp.int32(0)
    for place in range(MT * KPT):
        here = mask_ref[0, place // KPT, place % KPT] != 0
        upper = (number >= half).astype(jnp.int32)
        row = jnp.minimum(number - upper * half, half - 1)
        slot = jnp.minimum(number, PCAP - 1)

        @pl.when(here & (upper == high))
        def _(place=place, row=row, slot=slot):
            tile_copy(place, own_ref, row, slot).start()

        @pl.when(here & (upper != high))
        def _(place=place, row=row, slot=slot):
            tile_copy(place, give_ref, row, slot).start()

        number = number + here.astype(jnp.int32)

    column = lax.broadcasted_iota(jnp.int32, (16, TILE), 1)
    note = jnp.zeros((16, TILE), jnp.float32)
    for place in range(MT * KPT):
        note = jnp.where(column == TILES + place, mask_ref[0, place // KPT, place % KPT].astype(jnp.float32), note)
    for e in range(SPILL):
        spill_ref[e] = -1
    for o in range(kept.shape[0]):
        kept[o] = 0
    spilled_count = jnp.int32(0)
    for q in range(TILES):
        owner = owner_ref[q // MT, q % MT, 0]
        keep = (keep_ref[q % MT, q // MT] != 0).astype(jnp.int32)
        rank = kept[owner]
        kept[owner] = rank + keep
        over = keep * (rank >= direct).astype(jnp.int32)
        short_ref[q] = jnp.where(keep * (1 - over) != 0, owner * direct + rank, -1)
        long_ref[q] = jnp.where(keep != 0, owner * slots_each + rank, -1)

        @pl.when((over != 0) & (spilled_count < SPILL))
        def _(q=q, spilled_count=spilled_count):
            spill_ref[jnp.minimum(spilled_count, SPILL - 1)] = q

        spilled_count = spilled_count + over
        note = jnp.where(column == q, (owner * 2 + keep).astype(jnp.float32), note)
    note = jnp.where(column == TILES + MT * KPT, spilled_count.astype(jnp.float32), note)
    give_ref[half * TILE : half * TILE + 16, :] = note.astype(jnp.bfloat16)
    for number in range(PCAP):
        tile_copy(0, own_ref, 0, number).wait()


def prepare(panel, me, mask, owners, keep, ranks, slots_each, direct):
    rows = PCAP // 2 * TILE
    places = jax.ShapeDtypeStruct((TILES,), jnp.int32)
    return pl.pallas_call(
        functools.partial(prepare_kernel, slots_each, direct),
        out_shape=(
            jax.ShapeDtypeStruct((rows, TILE), jnp.bfloat16),
            jax.ShapeDtypeStruct((rows + 16, TILE), jnp.bfloat16),
            places,
            places,
            jax.ShapeDtypeStruct((SPILL,), jnp.int32),
        ),
        in_specs=[SMEM, SMEM, SMEM, SMEM, ANY],
        out_specs=(VMEM, VMEM, SMEM, SMEM, SMEM),
        scratch_shapes=[pltpu.SMEM((ranks,), jnp.int32), pltpu.SemaphoreType.DMA((PCAP,))],
        name="prepare",
    )(me, mask, owners, keep, panel)


def pair_kernel(me_ref, root_ref, note_ref, row_ref, panel_tile_ref, v_tile_ref, at_ref, most_ref):
    def listed(s, place):
        return (note_ref[root_ref[s], TILES + place] != 0).astype(jnp.int32)

    most = jnp.int32(0)
    for device in range(note_ref.shape[0]):
        most = jnp.maximum(most, note_ref[device, TILES + MT * KPT])
    most_ref[0, 0] = most
    for i in range(2 * PAIRS):
        panel_tile_ref[i] = 0
        v_tile_ref[i] = SECTIONS * KPT
    for pair in range(PAIRS):
        row_ref[pair] = MT - 1
    number = [jnp.int32(0)] * SECTIONS
    place_in_pairs = jnp.int32(0)
    for m in range(MT):
        for s in range(SECTIONS):
            for k in range(KPT):
                here = listed(s, m * KPT + k)
                upper = (number[s] >= PCAP // 2).astype(jnp.int32)
                away = (upper != me_ref[0] % 2).astype(jnp.int32)
                tile = 2 * (s * (PCAP // 2) + number[s] - upper * (PCAP // 2)) + away

                at_ref[(m * SECTIONS + s) * KPT + k] = jnp.where(here != 0, tile, -1)

                @pl.when(here != 0)
                def _(place_in_pairs=place_in_pairs, tile=tile, v_tile=s * KPT + k, m=m):
                    panel_tile_ref[place_in_pairs] = tile
                    v_tile_ref[place_in_pairs] = v_tile
                    row_ref[place_in_pairs // 2] = m

                place_in_pairs = place_in_pairs + here
                number[s] = number[s] + here
        place_in_pairs = (place_in_pairs + 1) // 2 * 2


def pair_up(me, roots, notes):
    members = jax.ShapeDtypeStruct((2 * PAIRS,), jnp.int32)
    *pairs, at, most = pl.pallas_call(
        pair_kernel,
        out_shape=(
            jax.ShapeDtypeStruct((PAIRS,), jnp.int32),
            members,
            members,
            jax.ShapeDtypeStruct((MT * SECTIONS * KPT,), jnp.int32),
            jax.ShapeDtypeStruct((1, 1), jnp.int32),
        ),
        in_specs=[SMEM, SMEM, SMEM],
        out_specs=(SMEM,) * 5,
        cost_estimate=pl.CostEstimate(flops=0, bytes_accessed=8 * 1024 * 1024, transcendentals=0),
        name="pair_up",
    )(me, roots, notes)
    return pairs, at, most


def panel_at(panel_tile, mine_ref, got_ref):
    rows = pl.ds(pl.multiple_of(panel_tile // 2 * TILE, TILE), TILE)
    return jnp.where(panel_tile % 2 == 0, mine_ref[rows, :], got_ref[rows, :])


def pair_product(pair, panel_tile_ref, v_tile_ref, mine_ref, got_ref, v_ref, mask_ref):
    left, right = [], []
    for i in (2 * pair, 2 * pair + 1):
        v_tile = v_tile_ref[i]
        left.append(panel_at(panel_tile_ref[i], mine_ref, got_ref))
        v_row = jnp.minimum(v_tile, SECTIONS * KPT - 1)
        right.append(v_ref[pl.ds(pl.multiple_of(v_row * TILE, TILE), TILE), :] * mask_ref[v_tile])
    return jnp.dot(
        jnp.concatenate(left, axis=1), jnp.concatenate(right, axis=0), preferred_element_type=jnp.float32
    )


def ladder_kernel(
    row_ref, panel_tile_ref, v_tile_ref, place_ref, mine_ref, got_ref, v_ref, mask_ref, out_ref, acc, staged, sem
):
    step = pl.program_id(0)
    acc[...] = jnp.zeros_like(acc)
    for pair in range(PAIRS):
        acc[row_ref[pair]] += pair_product(pair, panel_tile_ref, v_tile_ref, mine_ref, got_ref, v_ref, mask_ref)

    def copy_to(q, place):
        return pltpu.make_async_copy(staged.at[q], out_ref.at[place], sem.at[q])

    for j in range(STEP_TILES):
        for m in range(MT):
            q = (step * STEP_TILES + j) * MT + m
            staged[q] = acc[m, :, j * TILE : (j + 1) * TILE].astype(jnp.bfloat16)

            @pl.when(place_ref[q] >= 0)
            def _():
                copy_to(q, place_ref[q]).start()

    @pl.when(step == NT_DEV // STEP_TILES - 1)
    def _():
        def finish(q, carry):
            @pl.when(place_ref[q] >= 0)
            def _():
                copy_to(q, 0).wait()

            return carry

        lax.fori_loop(0, TILES, finish, 0)


def ladder(mine, got, pairs, v, v_rows, places, slots):
    macs = 2 * PAIRS * TILE * TILE * NT_DEV * TILE
    return pl.pallas_call(
        ladder_kernel,
        out_shape=jax.ShapeDtypeStruct((slots, TILE, TILE), jnp.bfloat16),
        grid=(NT_DEV // STEP_TILES,),
        in_specs=[
            SMEM,
            SMEM,
            SMEM,
            SMEM,
            VMEM,
            VMEM,
            pl.BlockSpec((SECTIONS * KPT * TILE, STEP_COLS), lambda j: (0, j)),
            pl.BlockSpec((SECTIONS * KPT + 1, 1, STEP_COLS), lambda j: (0, 0, j)),
        ],
        out_specs=HBM,
        scratch_shapes=[
            pltpu.VMEM((MT, TILE, STEP_COLS), jnp.float32),
            pltpu.VMEM((TILES, TILE, TILE), jnp.bfloat16),
            pltpu.SemaphoreType.DMA((TILES,)),
        ],
        compiler_params=pltpu.CompilerParams(vmem_limit_bytes=55 * 1024 * 1024),
        cost_estimate=pl.CostEstimate(flops=4 * macs, bytes_accessed=24 * 1024 * 1024, transcendentals=0),
        name="ladder",
    )(*pairs, places, mine, got, v, v_rows)


def column_of(tile):
    return pl.ds(pl.multiple_of(jnp.maximum(tile, 0) // MT * TILE, TILE), TILE)


def fetch_kernel(tile_ref, v_ref, out_ref, sem):
    copies = [
        pltpu.make_async_copy(v_ref.at[:, column_of(tile_ref[e])], out_ref.at[e], sem.at[e]) for e in range(SPILL)
    ]
    for copy in copies:
        copy.start()
    for copy in copies:
        copy.wait()


def fetch_columns(v, tiles):
    return pl.pallas_call(
        fetch_kernel,
        out_shape=jax.ShapeDtypeStruct((SPILL, v.shape[0], TILE), jnp.bfloat16),
        in_specs=[SMEM, HBM],
        out_specs=VMEM,
        scratch_shapes=[pltpu.SemaphoreType.DMA((SPILL,))],
        compiler_params=pltpu.CompilerParams(vmem_limit_bytes=16 * 1024 * 1024),
        cost_estimate=pl.CostEstimate(flops=0, bytes_accessed=8 * 1024 * 1024, transcendentals=0),
        name="fetch_columns",
    )(tiles, v)


def spill_kernel(tile_ref, at_ref, v_mask_ref, mine_ref, got_ref, v_ref, out_ref):
    for e in range(SPILL):
        tile = jnp.maximum(tile_ref[e], 0)
        left = []
        for i in range(SECTIONS * KPT):
            panel_tile = at_ref[lax.rem(tile, MT) * (SECTIONS * KPT) + i]
            counts = (panel_tile >= 0) & (v_mask_ref[i // KPT, i % KPT, tile // MT] != 0)
            value = panel_at(jnp.maximum(panel_tile, 0), mine_ref, got_ref)
            left.append(jnp.where(counts, value, jnp.zeros_like(value)))
        product = jnp.dot(jnp.concatenate(left, axis=1), v_ref[e], preferred_element_type=jnp.float32)
        out_ref[e] = product.astype(jnp.bfloat16)


def spilled(mine, got, at, columns, v_mask, tiles):
    return pl.pallas_call(
        spill_kernel,
        out_shape=jax.ShapeDtypeStruct((SPILL, TILE, TILE), jnp.bfloat16),
        in_specs=[SMEM] * 3 + [VMEM] * 3,
        out_specs=VMEM,
        compiler_params=pltpu.CompilerParams(vmem_limit_bytes=32 * 1024 * 1024),
        name="spilled",
    )(tiles, at, v_mask, mine, got, columns)


def clear_kernel(table_ref, out_ref, zero, sem):
    zero[...] = jnp.zeros_like(zero)

    def each(act):
        def visit(j, carry):
            @pl.when(table_ref[j] < 0)
            def _():
                act(pltpu.make_async_copy(zero, out_ref.at[j], sem.at[j]))

            return carry

        lax.fori_loop(0, out_ref.shape[0], visit, 0)

    each(lambda copy: copy.start())
    each(lambda copy: copy.wait())


def clear(table):
    slots = table.shape[0]
    return pl.pallas_call(
        clear_kernel,
        out_shape=jax.ShapeDtypeStruct((slots, TILE, TILE), jnp.bfloat16),
        in_specs=[SMEM],
        out_specs=HBM,
        scratch_shapes=[pltpu.VMEM((TILE, TILE), jnp.bfloat16), pltpu.SemaphoreType.DMA((slots,))],
        compiler_params=pltpu.CompilerParams(vmem_limit_bytes=55 * 1024 * 1024),
        cost_estimate=pl.CostEstimate(flops=0, bytes_accessed=8 * 1024 * 1024, transcendentals=0),
        name="clear",
    )(table)


def place_kernel(split, reach, table_ref, blank_ref, direct_ref, near_ref, far_ref, out_ref, held, in_sem, out_sem):
    slots = out_ref.shape[0]

    def fetch(ref, place, j):
        return pltpu.make_async_copy(ref.at[place], held.at[j], in_sem.at[j])

    def store(j):
        return pltpu.make_async_copy(held.at[j], out_ref.at[j], out_sem.at[j])

    def begin(j, carry):
        source = table_ref[j]

        @pl.when((source >= 0) & (source < split))
        def _():
            fetch(direct_ref, source, j).start()

        @pl.when((source >= split) & (source < split + reach))
        def _():
            fetch(near_ref, source - split, j).start()

        @pl.when(source >= split + reach)
        def _():
            fetch(far_ref, source - split - reach, j).start()

        return carry

    def forward(j, carry):
        @pl.when(table_ref[j] >= 0)
        def _():
            fetch(direct_ref, 0, j).wait()
            store(j).start()

        return carry

    def finish(j, carry):
        @pl.when(table_ref[j] >= 0)
        def _():
            store(j).wait()

        return carry

    lax.fori_loop(0, slots, begin, 0)
    lax.fori_loop(0, slots, forward, 0)
    lax.fori_loop(0, slots, finish, 0)


def place_tiles(table, blank, direct, near_spill, far_spill):
    slots, split, reach = table.shape[0], direct.shape[0], near_spill.shape[0]
    return pl.pallas_call(
        functools.partial(place_kernel, split, reach),
        out_shape=jax.ShapeDtypeStruct((slots, TILE, TILE), jnp.bfloat16),
        in_specs=[SMEM, HBM, HBM, HBM, HBM],
        out_specs=HBM,
        scratch_shapes=[
            pltpu.VMEM((slots, TILE, TILE), jnp.bfloat16),
            pltpu.SemaphoreType.DMA((slots,)),
            pltpu.SemaphoreType.DMA((slots,)),
        ],
        input_output_aliases={1: 0},
        compiler_params=pltpu.CompilerParams(vmem_limit_bytes=55 * 1024 * 1024),
        name="place_tiles",
    )(table, blank, direct, near_spill, far_spill)


def exchange(tiles, ranks):
    count = tiles.shape[0] // ranks
    sent = tiles.reshape(ranks, count, TILE, TILE)
    return lax.all_to_all(sent, "row", split_axis=0, concat_axis=0, tiled=True).reshape(
        ranks * count, TILE, TILE
    )


def local(t2_panels, t2_mask, v_blocks, v_mask, r_mask, owner_map, section_owner):
    ranks = lax.axis_size("row")
    me = lax.axis_index("row")
    slots_each = max(2, 2 * TILES // ranks)
    direct = slots_each // 2
    top = ranks // 2
    roots = section_owner

    own, give, short_places, long_places, spill_tiles = prepare(
        t2_panels,
        me.reshape(1),
        t2_mask,
        owner_map,
        r_mask,
        ranks,
        slots_each,
        direct,
    )
    v = v_blocks.reshape(SECTIONS * KPT * TILE, NT_DEV * TILE)
    v_rows = jnp.repeat(v_mask.reshape(SECTIONS * KPT, 1, NT_DEV).astype(jnp.bfloat16), TILE, axis=2)
    v_rows = jnp.pad(v_rows, ((0, 1), (0, 0), (0, 0)))
    columns = fetch_columns(v, spill_tiles)

    def digest(notes):
        notes = notes[:, : TILES + MT * KPT + 1].astype(jnp.int32)
        pairs, at, most = pair_up(me.reshape(1), roots, notes)
        return most, notes, pairs, at, columns

    mine, got, worst, (notes, pairs, at, columns) = spread(own, give, me, roots, ranks, digest)
    mine, got = mine.reshape(-1, TILE), got.reshape(-1, TILE)

    split = ranks * direct

    def table_of(notes, short):
        owners, keep = notes[:, :TILES] // 2, notes[:, :TILES] % 2 != 0
        rank, kept_rank, spills, spill_place = ranks_of(owners, keep, direct)
        device = jnp.arange(ranks, dtype=jnp.int32)[:, None]
        slot = jnp.arange(slots_each, dtype=jnp.int32)
        if short:
            far = ((device ^ me) & top) // top
            spill_from = split + far * (top * SPILL) + (device & (top - 1)) * SPILL + spill_place
            origin = jnp.where(spills, spill_from, device * direct + kept_rank)
        else:
            origin = device * slots_each + kept_rank
        arrives = ((owners == me) & keep)[:, None, :] & (rank[:, None, :] == slot[None, :, None])
        return (jnp.sum(jnp.where(arrives, origin[:, None, :] + 1, 0), axis=2) - 1).reshape(-1)

    halves = [list(range(top)), list(range(top, ranks))]

    def short(mine, got, v, v_rows, columns, notes, spill_tiles, places, _):
        spill = spilled(mine, got, at, columns, v_mask, spill_tiles)
        near_spill = lax.all_gather(spill, "row", axis=0, tiled=True, axis_index_groups=halves)
        other = swap(spill, top, ranks)
        tiles = ladder(mine, got, pairs, v, v_rows, places, split)
        other, tiles, notes = lax.optimization_barrier((other, tiles, notes))
        far_spill = lax.all_gather(other, "row", axis=0, tiled=True, axis_index_groups=halves)
        table = table_of(notes, True)
        blank = clear(table)
        return place_tiles(table, blank, exchange(tiles, ranks), near_spill, far_spill)

    def long(mine, got, v, v_rows, _, notes, __, ___, places):
        tiles = ladder(mine, got, pairs, v, v_rows, places, ranks * slots_each)
        unused = jnp.zeros((1, TILE, TILE), jnp.bfloat16)
        table = table_of(notes, False)
        return place_tiles(table, clear(table), exchange(tiles, ranks), unused, unused)

    delivered = lax.cond(
        worst[0, 0] <= SPILL,
        short,
        long,
        mine,
        got,
        v,
        v_rows,
        columns,
        notes,
        spill_tiles,
        short_places,
        long_places,
    )
    return delivered.reshape(ranks, slots_each, TILE, TILE)


def solution(mesh):
    placed = (
        P(("groups", "row"), None, None),
        P(("groups", "row"), None, None),
        P("groups", None, "row"),
        P("groups", None, "row"),
        P("groups", "row"),
        P(("groups", "row"), None, None),
        P("groups"),
    )
    return jax.shard_map(
        local,
        mesh=mesh,
        in_specs=placed,
        out_specs=P(("groups", "row"), None, None, None),
        check_vma=False,
    )
```

time: 213 us -> 206 us (0.967)
  waiting for transfers between devices: 131 us -> 118 us
  Pallas kernels: 23.9 us -> 33.8 us
  other arithmetic: 7.96 us -> 4.49 us
  starting transfers between devices: 25.5 us -> 28.8 us
  local copies, waits for them, and re-layouts: 6.29 us -> 3.79 us
    ppermute x13 -> x14, waiting for transfers between devices: 39.8 us -> 29.1 us  [swap(): return lax.ppermute(x, 'row', [(i, i ^ bit) for i in range(ranks)])]
    pallas_call x1 -> x4, Pallas kernels: 5.35 us -> 14.9 us  [the longest x1 4.88 us: place_tiles(): pl.pallas_call(functools.partial(place_kernel, split, reach), out_shape=j...]
    all_gather x1, waiting for transfers between devices: 3.9 us -> 0.02 us  [short(): lax.all_gather(spill, 'row', axis=0, tiled=True, axis_index_groups=halves)]
    ppermute x13 -> x14, starting transfers between devices: 16.1 us -> 19.5 us  [swap(): return lax.ppermute(x, 'row', [(i, i ^ bit) for i in range(ranks)])]
    reshape x3 -> x0, local copies, waits for them, and re-layouts: 3.21 us -> none  [the longest x1 1.34 us: local(): r_mask.reshape(TILES)]
  transfers between devices with their start and end apart: 17 -> 18, of which waited for: 14 -> 16; matrix products, arithmetic and copies ran while one was open for 2% -> 2% of each run, Pallas kernels for 5% -> 10%
where the time goes in v2:
time: 206 us; the launch traced here: 204 us
  waiting for transfers between devices  118 us (57%)
  Pallas kernels  33.8 us (16%)
  starting transfers between devices  28.8 us (14%)
  between operations  14.9 us (7%)
  other arithmetic  4.49 us (2%)
  local copies, waits for them, and re-layouts  3.79 us (2%)
    all_gather x1, waiting for transfers between devices, short(): lax.all_gather(other, 'row', axis=0, tiled=True, axis_index_groups=halves)  61.8 us
    ppermute x14, waiting for transfers between devices, swap(): return lax.ppermute(x, 'row', [(i, i ^ bit) for i in range(ranks)])  29.1 us
    all_to_all x1, waiting for transfers between devices, exchange(): lax.all_to_all(sent, 'row', split_axis=0, concat_axis=0, tiled=True)  24.5 us
    ppermute x14, starting transfers between devices, swap(): return lax.ppermute(x, 'row', [(i, i ^ bit) for i in range(ranks)])  19.5 us
    pallas_call x1, Pallas kernels, ladder(): pl.pallas_call(ladder_kernel, out_shape=jax.ShapeDtypeStruct((slots, TILE...  11.3 us
    all_to_all x1, starting transfers between devices, exchange(): lax.all_to_all(sent, 'row', split_axis=0, concat_axis=0, tiled=True)  7.66 us
    pallas_call x1, Pallas kernels, place_tiles(): pl.pallas_call(functools.partial(place_kernel, split, reach), out_shape=j...  4.88 us
    pallas_call x1, Pallas kernels, fetch_columns(): pl.pallas_call(fetch_kernel, out_shape=jax.ShapeDtypeStruct((SPILL, v.sha...  4.66 us
  transfers between devices with their start and end apart: 18, of which 16 were waited for; matrix products, arithmetic and copies ran while one was open for 2% of the time, Pallas kernels for 10%

profile of v2, /device:TPU:16, one launch (start us, length us, event | category | flops | bytes accessed | tf_op | source)
XLA Modules:
  0.0 204.0 jit_solution(18269268878681233914)
XLA Ops:
  6.5 1.4 copy.30.owner_ref
  7.9 3.6 %prepare.1 = (bf16[1280,256]{1,0:T(8,128)(2,1)}, bf16[1296,256]{1,0:T(8,128)(2,1)}, s32[32]{0:T(128)S(1)}, s32[32]{0:T(128)S(1)}, s32[3]{0:T(128)S(1)}) custom-call(s32[1]{0:T(128)} %bitcast.6.me_ref, s32[1,4,5]{2,1,0:T(4,128)} %mask_ref.1, s32[8,4,1]{2,1,0:T(4,128)} %copy.30.owner_ref, s32[4,8]{1,0:T(4,128)} %keep_ref.1, bf16[1,1024,1280]{2,1,0:T(8,128)(2,1)} %panel_ref.1), custom_call_target="tpu_custom_call" | custom-call | tf_op jit(solution)/shard_map/prepare/pallas_call | solution.py:185
  11.6 2.3 %collective-permute-done.1 = bf16[1296,256]{1,0:T(8,128)(2,1)S(1)} collective-permute-done((bf16[1296,256]{1,0:T(8,128)(2,1)}, bf16[1296,256]{1,0:T(8,128)(2,1)S(1)}, u32[]{:S(2)}, u32[]{:S(2)}) %collective-permute-start.1) | collective-permute-done | bytes 663584 | tf_op jit(solution)/shard_map/ppermute | solution.py:28
  16.0 1.6 collective-permute-start.4
  17.6 1.6 collective-permute-start.2
  19.2 4.7 %fetch_columns.1 = bf16[3,2560,256]{2,1,0:T(8,128)(2,1)} custom-call(s32[3]{0:T(128)S(1)} %get-tuple-element.111.tile_ref, bf16[2560,2048]{1,0:T(8,128)(2,1)} %bitcast.17), custom_call_target="tpu_custom_call" | custom-call | bytes 8388608 | tf_op jit(solution)/shard_map/fetch_columns/pallas_call | solution.py:348
  23.9 2.1 %collective-permute-done.4 = bf16[642,256]{1,0:T(8,128)(2,1)S(1)} collective-permute-done((bf16[642,256]{1,0:T(8,128)(2,1)S(1)}, bf16[642,256]{1,0:T(8,128)(2,1)S(1)}, u32[]{:S(2)}, u32[]{:S(2)}) %collective-permute-start.4) | collective-permute-done | bytes 328736 | tf_op jit(solution)/shard_map/ppermute | solution.py:28
  27.9 1.6 collective-permute-start.5
  29.6 3.1 %collective-permute-done.3 = bf16[2,160,256]{2,1,0:T(8,128)(2,1)S(1)} collective-permute-done((bf16[2,160,256]{2,1,0:T(8,128)(2,1)S(1)}, bf16[2,160,256]{2,1,0:T(8,128)(2,1)S(1)}, u32[]{:S(2)}, u32[]{:S(2)}) %collective-permute-start.3) | collective-permute-done | bytes 163872 | tf_op jit(solution)/shard_map/ppermute | solution.py:28
  33.8 2.8 %collective-permute-start.9 = (bf16[2,160,256]{2,1,0:T(8,128)(2,1)S(1)}, bf16[2,160,256]{2,1,0:T(8,128)(2,1)S(1)}, u32[]{:S(2)}, u32[]{:S(2)}) collective-permute-start(bf16[2,160,256]{2,1,0:T(8,128)(2,1)S(1)} %select_select_fusion.2), channel_id=1, source_target_pairs={{0,8},{1,9},{2,10},{3,11},{4,12},{5,13},{6,14},{7,15},{8,0},{9,1},... | collective-permute-start | bytes 491528 | tf_op jit(solution)/shard_map/ppermute | solution.py:28
  36.5 1.5 collective-permute-done.6
  38.1 1.8 pair_up.1
  40.2 1.6 collective-permute-start.8
  41.7 2.1 %collective-permute-done.8 = s32[1,1]{1,0:T(1,128)} collective-permute-done((s32[1,1]{1,0:T(1,128)}, s32[1,1]{1,0:T(1,128)}, u32[]{:S(2)}, u32[]{:S(2)}) %collective-permute-start.8) | collective-permute-done | bytes 36 | tf_op jit(solution)/shard_map/ppermute | solution.py:71
  45.0 1.4 collective-permute-done.9
  46.5 2.1 %collective-permute-done.7 = bf16[2,160,256]{2,1,0:T(8,128)(2,1)S(1)} collective-permute-done((bf16[2,160,256]{2,1,0:T(8,128)(2,1)S(1)}, bf16[2,160,256]{2,1,0:T(8,128)(2,1)S(1)}, u32[]{:S(2)}, u32[]{:S(2)}) %collective-permute-start.7) | collective-permute-done | bytes 163872 | tf_op jit(solution)/shard_map/ppermute | solution.py:28
  50.0 2.3 %collective-permute-start.10 = (bf16[2,160,256]{2,1,0:T(8,128)(2,1)S(1)}, bf16[2,160,256]{2,1,0:T(8,128)(2,1)S(1)}, u32[]{:S(2)}, u32[]{:S(2)}) collective-permute-start(bf16[2,160,256]{2,1,0:T(8,128)(2,1)S(1)} %get-tuple-element.243), channel_id=1, source_target_pairs={{0,4},{1,5},{2,6},{3,7},{4,0},{5,1},{6,2},{7,3},{8,12},{9,13},{10,... | collective-permute-start | bytes 491528 | tf_op jit(solution)/shard_map/ppermute | solution.py:28
  52.3 1.8 collective-permute-done.12
  54.1 2.3 %collective-permute-start.13 = (bf16[2,320,256]{2,1,0:T(8,128)(2,1)S(1)}, bf16[2,320,256]{2,1,0:T(8,128)(2,1)S(1)}, u32[]{:S(2)}, u32[]{:S(2)}) collective-permute-start(bf16[2,320,256]{2,1,0:T(8,128)(2,1)S(1)} %pad_maximum_fusion.3), channel_id=1, source_target_pairs={{0,4},{1,5},{2,6},{3,7},{4,0},{5,1},{6,2},{7,3},{8,12},{9,13},{10,... | collective-permute-start | bytes 983048 | tf_op jit(solution)/shard_map/ppermute | solution.py:28
  56.5 1.4 collective-permute-start.11
  57.9 4.7 %collective-permute-done.13 = bf16[2,320,256]{2,1,0:T(8,128)(2,1)S(1)} collective-permute-done((bf16[2,320,256]{2,1,0:T(8,128)(2,1)S(1)}, bf16[2,320,256]{2,1,0:T(8,128)(2,1)S(1)}, u32[]{:S(2)}, u32[]{:S(2)}) %collective-permute-start.13) | collective-permute-done | bytes 327712 | tf_op jit(solution)/shard_map/ppermute | solution.py:28
  64.2 2.8 %collective-permute-done.14 = bf16[2,1280,256]{2,1,0:T(8,128)(2,1)S(1)} collective-permute-done((bf16[2,1280,256]{2,1,0:T(8,128)(2,1)S(1)}, bf16[2,1280,256]{2,1,0:T(8,128)(2,1)S(1)}, u32[]{:S(2)}, u32[]{:S(2)}) %collective-permute-start.14) | collective-permute-done | bytes 1310752 | tf_op jit(solution)/shard_map/ppermute | solution.py:28
  67.0 130.2 %conditional.1 = (bf16[16,4,256,256]{3,2,1,0:T(8,128)(2,1)}) conditional(s32[]{:T(128)} %bitcast.11, (s32[16,53]{1,0:T(8,128)S(1)}, s32[]{:T(128)}, s32[12]{0:T(128)S(1)}, s32[24]{0:T(128)S(1)}, s32[24]{0:T(128)S(1)}, /*index=5*/s32[32]{0:T(128)S(1)}, bf16[2560,256]{1,0:T(8,128)(2,1)S(1)}, bf16[2560,256]{1,0:T(8,128)(2,1)S(1)}, ...), branch_computations={%region_0.4_spmd, %region_4.9_spmd} | conditional | flops 12885089280 | bytes 70641480 | solution.py:553
  67.0 4.1 %spilled.1 = bf16[3,256,256]{2,1,0:T(8,128)(2,1)} custom-call(s32[3]{0:T(128)S(1)} %get-tuple-element.67.tile_ref, s32[40]{0:T(128)S(1)} %get-tuple-element.68.at_ref, s32[2,5,8]{2,1,0:T(8,128)S(1)} %copy.34.v_mask_ref, bf16[2560,256]{1,0:T(8,128)(2,1)S(1)} %get-tuple-element.70.mine_ref, bf16[2560,256]{1,0:T(8,128)(2,1)S(1)} %get-tuple-element.71.got_ref, ...), custom_call_target="tpu_custom_call" | custom-call | tf_op jit(solution)/shard_map/cond/branch_1_fun/spilled/pallas_call | solution.py:374
  71.1 3.4 %collective-permute-start = (bf16[3,256,256]{2,1,0:T(8,128)(2,1)}, bf16[3,256,256]{2,1,0:T(8,128)(2,1)S(1)}, u32[]{:S(2)}, u32[]{:S(2)}) collective-permute-start(bf16[3,256,256]{2,1,0:T(8,128)(2,1)} %spilled.1), channel_id=1, source_target_pairs={{0,8},{1,9},{2,10},{3,11},{4,12},{5,13},{6,14},{7,15},{8,0},{9,1},... | collective-permute-start | bytes 1179656 | tf_op jit(solution)/shard_map/cond/branch_1_fun/ppermute | solution.py:28
  75.2 11.3 %ladder.3 = bf16[32,256,256]{2,1,0:T(8,128)(2,1)} custom-call(s32[12]{0:T(128)S(1)} %get-tuple-element.73.row_ref, s32[24]{0:T(128)S(1)} %get-tuple-element.74.panel_tile_ref, s32[24]{0:T(128)S(1)} %get-tuple-element.75.v_tile_ref, s32[32]{0:T(128)S(1)} %get-tuple-element.76.place_ref, bf16[2560,256]{1,0:T(8,128)(2,1)S(1)} %get-tuple-element.70.mine_ref, ...), custom_call_target="tpu_custom_call" | custom-call | flops 12884901888 | bytes 25165824 | tf_op jit(solution)/shard_map/cond/branch_1_fun/ladder/pallas_call | solution.py:307
  86.5 4.7 %collective-permute-done = bf16[3,256,256]{2,1,0:T(8,128)(2,1)S(1)} collective-permute-done((bf16[3,256,256]{2,1,0:T(8,128)(2,1)}, bf16[3,256,256]{2,1,0:T(8,128)(2,1)S(1)}, u32[]{:S(2)}, u32[]{:S(2)}) %collective-permute-start) | collective-permute-done | bytes 393248 | tf_op jit(solution)/shard_map/cond/branch_1_fun/ppermute | solution.py:28
  91.9 7.7 %all-to-all-start.1 = ((bf16[16,2,256,256]{3,2,1,0:T(8,128)(2,1)}), bf16[16,2,256,256]{3,2,1,0:T(8,128)(2,1)}, u32[]{:S(2)}, u32[]{:S(2)}) async-start(bf16[16,2,256,256]{3,2,1,0:T(8,128)(2,1)} %bitcast.23), calls=%async_computation.1 | async-start | bytes 8388608 | tf_op jit(solution)/shard_map/cond/branch_1_fun/all_to_all | solution.py:482
  102.5 3.5 %clear.3.blank_ref = bf16[64,256,256]{2,1,0:T(8,128)(2,1)} custom-call(s32[64]{0:T(128)} %sub.23.table_ref), custom_call_target="tpu_custom_call" | custom-call | bytes 8388608 | tf_op jit(solution)/shard_map/cond/branch_1_fun/clear/pallas_call | solution.py:403
  106.0 61.8 %all-gather.5.cloned.1.call-done.far_ref = bf16[24,256,256]{2,1,0:T(8,128)(2,1)} async-done(((bf16[3,256,256]{2,1,0:T(8,128)(2,1)}), bf16[24,256,256]{2,1,0:T(8,128)(2,1)}) %all-gather.5.cloned.1.call-update) | async-done | bytes 3145744 | tf_op jit(solution)/shard_map/cond/branch_1_fun/all_gather | solution.py:542
  167.8 24.5 %all-to-all-done.1 = bf16[16,2,256,256]{3,2,1,0:T(8,128)(2,1)} async-done(((bf16[16,2,256,256]{3,2,1,0:T(8,128)(2,1)}), bf16[16,2,256,256]{3,2,1,0:T(8,128)(2,1)}, u32[]{:S(2)}, u32[]{:S(2)}) %all-to-all-start.1) | async-done | bytes 4194336 | tf_op jit(solution)/shard_map/cond/branch_1_fun/all_to_all | solution.py:482
  192.3 4.9 %place_tiles.3 = bf16[64,256,256]{2,1,0:T(8,128)(2,1)} custom-call(s32[64]{0:T(128)} %sub.23.table_ref, bf16[64,256,256]{2,1,0:T(8,128)(2,1)} %clear.3.blank_ref, bf16[32,256,256]{2,1,0:T(8,128)(2,1)} %bitcast.4.direct_ref, bf16[24,256,256]{2,1,0:T(8,128)(2,1)} %all-gather.3.cloned.1.call-done.near_ref, ...), custom_call_target="tpu_custom_call", output_to_operand_aliasing={{}: (1, {})} | custom-call | tf_op jit(solution)/shard_map/cond/branch_1_fun/place_tiles/pallas_call | solution.py:463
  (68 shorter events, 12.9 us)
Async XLA Ops:
  6.5 5.0 %copy-start.2 = (s32[2]{0:T(128)S(1)}, s32[2]{0:T(128)}, u32[]{:S(2)}) copy-start(s32[2]{0:T(128)} %root_ref.1) | copy-start | bytes 28
  11.5 2.4 %collective-permute-start.1 = (bf16[1296,256]{1,0:T(8,128)(2,1)}, bf16[1296,256]{1,0:T(8,128)(2,1)S(1)}, u32[]{:S(2)}, u32[]{:S(2)}) collective-permute-start(bf16[1296,256]{1,0:T(8,128)(2,1)} %get-tuple-element.105), channel_id=1, source_target_pairs={{0,1},{1,0},{2,3},{3,2},{4,5},{5,4},{6,7},{7,6},{8,9},{9,8},{10,11... | collective-permute-start | bytes 1990664 | tf_op jit(solution)/shard_map/ppermute | solution.py:28
  16.0 9.9 %collective-permute-start.4 = (bf16[642,256]{1,0:T(8,128)(2,1)S(1)}, bf16[642,256]{1,0:T(8,128)(2,1)S(1)}, u32[]{:S(2)}, u32[]{:S(2)}) collective-permute-start(bf16[642,256]{1,0:T(8,128)(2,1)S(1)} %pad_maximum_fusion.1), channel_id=1, source_target_pairs={{0,2},{1,3},{2,0},{3,1},{4,6},{5,7},{6,4},{7,5},{8,10},{9,11},{10,... | collective-permute-start | bytes 986120 | tf_op jit(solution)/shard_map/ppermute | solution.py:28
  17.6 9.5 %collective-permute-start.2 = (bf16[2,320,256]{2,1,0:T(8,128)(2,1)S(1)}, bf16[2,320,256]{2,1,0:T(8,128)(2,1)S(1)}, u32[]{:S(2)}, u32[]{:S(2)}) collective-permute-start(bf16[2,320,256]{2,1,0:T(8,128)(2,1)S(1)} %get-tuple-element.228), channel_id=1, source_target_pairs={{0,4},{1,5},{2,6},{3,7},{4,0},{5,1},{6,2},{7,3},{8,12},{9,13},{10,... | collective-permute-start | bytes 983048 | tf_op jit(solution)/shard_map/ppermute | solution.py:28
  27.3 5.4 %collective-permute-start.3 = (bf16[2,160,256]{2,1,0:T(8,128)(2,1)S(1)}, bf16[2,160,256]{2,1,0:T(8,128)(2,1)S(1)}, u32[]{:S(2)}, u32[]{:S(2)}) collective-permute-start(bf16[2,160,256]{2,1,0:T(8,128)(2,1)S(1)} %get-tuple-element.249), channel_id=1, source_target_pairs={{0,2},{1,3},{2,0},{3,1},{4,6},{5,7},{6,4},{7,5},{8,10},{9,11},{10,... | collective-permute-start | bytes 491528 | tf_op jit(solution)/shard_map/ppermute | solution.py:28
  27.9 5.4 %collective-permute-start.5 = (bf16[324,256]{1,0:T(8,128)(2,1)S(1)}, bf16[324,256]{1,0:T(8,128)(2,1)S(1)}, u32[]{:S(2)}, u32[]{:S(2)}) collective-permute-start(bf16[324,256]{1,0:T(8,128)(2,1)S(1)} %pad_maximum_fusion.4), channel_id=1, source_target_pairs={{0,4},{1,5},{2,6},{3,7},{4,0},{5,1},{6,2},{7,3},{8,12},{9,13},{10,... | collective-permute-start | bytes 497672 | tf_op jit(solution)/shard_map/ppermute | solution.py:28
  33.4 4.7 %collective-permute-start.6 = (bf16[8,256]{1,0:T(8,128)(2,1)S(1)}, bf16[8,256]{1,0:T(8,128)(2,1)S(1)}, u32[]{:S(2)}, u32[]{:S(2)}) collective-permute-start(bf16[8,256]{1,0:T(8,128)(2,1)S(1)} %pad_maximum_fusion.6), channel_id=1, source_target_pairs={{0,8},{1,9},{2,10},{3,11},{4,12},{5,13},{6,14},{7,15},{8,0},{9,1},... | collective-permute-start | bytes 12296 | tf_op jit(solution)/shard_map/ppermute | solution.py:28
  33.8 12.7 %collective-permute-start.9 = (bf16[2,160,256]{2,1,0:T(8,128)(2,1)S(1)}, bf16[2,160,256]{2,1,0:T(8,128)(2,1)S(1)}, u32[]{:S(2)}, u32[]{:S(2)}) collective-permute-start(bf16[2,160,256]{2,1,0:T(8,128)(2,1)S(1)} %select_select_fusion.2), channel_id=1, source_target_pairs={{0,8},{1,9},{2,10},{3,11},{4,12},{5,13},{6,14},{7,15},{8,0},{9,1},... | collective-permute-start | bytes 491528 | tf_op jit(solution)/shard_map/ppermute | solution.py:28
  39.9 8.7 %collective-permute-start.7 = (bf16[2,160,256]{2,1,0:T(8,128)(2,1)S(1)}, bf16[2,160,256]{2,1,0:T(8,128)(2,1)S(1)}, u32[]{:S(2)}, u32[]{:S(2)}) collective-permute-start(bf16[2,160,256]{2,1,0:T(8,128)(2,1)S(1)} %select_select_fusion.3), channel_id=1, source_target_pairs={{0,8},{1,9},{2,10},{3,11},{4,12},{5,13},{6,14},{7,15},{8,0},{9,1},... | collective-permute-start | bytes 491528 | tf_op jit(solution)/shard_map/ppermute | solution.py:28
  40.2 3.6 %collective-permute-start.8 = (s32[1,1]{1,0:T(1,128)}, s32[1,1]{1,0:T(1,128)}, u32[]{:S(2)}, u32[]{:S(2)}) collective-permute-start(s32[1,1]{1,0:T(1,128)} %get-tuple-element.113), channel_id=1, source_target_pairs={{0,16},{16,0},{1,17},{17,1},{2,18},{18,2},{3,19},{19,3},{4,20},{20... | collective-permute-start | bytes 20 | tf_op jit(solution)/shard_map/ppermute | solution.py:71
  48.7 5.4 %collective-permute-start.12 = (bf16[2,160,256]{2,1,0:T(8,128)(2,1)S(1)}, bf16[2,160,256]{2,1,0:T(8,128)(2,1)S(1)}, u32[]{:S(2)}, u32[]{:S(2)}) collective-permute-start(bf16[2,160,256]{2,1,0:T(8,128)(2,1)S(1)} %get-tuple-element.120), channel_id=1, source_target_pairs={{0,2},{1,3},{2,0},{3,1},{4,6},{5,7},{6,4},{7,5},{8,10},{9,11},{10,... | collective-permute-start | bytes 491528 | tf_op jit(solution)/shard_map/ppermute | solution.py:28
  50.0 6.4 %collective-permute-start.10 = (bf16[2,160,256]{2,1,0:T(8,128)(2,1)S(1)}, bf16[2,160,256]{2,1,0:T(8,128)(2,1)S(1)}, u32[]{:S(2)}, u32[]{:S(2)}) collective-permute-start(bf16[2,160,256]{2,1,0:T(8,128)(2,1)S(1)} %get-tuple-element.243), channel_id=1, source_target_pairs={{0,4},{1,5},{2,6},{3,7},{4,0},{5,1},{6,2},{7,3},{8,12},{9,13},{10,... | collective-permute-start | bytes 491528 | tf_op jit(solution)/shard_map/ppermute | solution.py:28
  54.1 8.5 %collective-permute-start.13 = (bf16[2,320,256]{2,1,0:T(8,128)(2,1)S(1)}, bf16[2,320,256]{2,1,0:T(8,128)(2,1)S(1)}, u32[]{:S(2)}, u32[]{:S(2)}) collective-permute-start(bf16[2,320,256]{2,1,0:T(8,128)(2,1)S(1)} %pad_maximum_fusion.3), channel_id=1, source_target_pairs={{0,4},{1,5},{2,6},{3,7},{4,0},{5,1},{6,2},{7,3},{8,12},{9,13},{10,... | collective-permute-start | bytes 983048 | tf_op jit(solution)/shard_map/ppermute | solution.py:28
  56.5 7.5 %copy-start.1 = (s32[2,5,8]{2,0,1:T(2,128)S(1)}, s32[2,5,8]{2,0,1:T(2,128)}, u32[]{:S(2)}) copy-start(s32[2,5,8]{2,0,1:T(2,128)} %param.12) | copy-start | bytes 964
  56.5 7.1 %collective-permute-start.11 = (bf16[2,320,256]{2,1,0:T(8,128)(2,1)S(1)}, bf16[2,320,256]{2,1,0:T(8,128)(2,1)S(1)}, u32[]{:S(2)}, u32[]{:S(2)}) collective-permute-start(bf16[2,320,256]{2,1,0:T(8,128)(2,1)S(1)} %pad_maximum_fusion.2), channel_id=1, source_target_pairs={{0,2},{1,3},{2,0},{3,1},{4,6},{5,7},{6,4},{7,5},{8,10},{9,11},{10,... | collective-permute-start | bytes 983048 | tf_op jit(solution)/shard_map/ppermute | solution.py:28
  63.9 3.1 %collective-permute-start.14 = (bf16[2,1280,256]{2,1,0:T(8,128)(2,1)S(1)}, bf16[2,1280,256]{2,1,0:T(8,128)(2,1)S(1)}, u32[]{:S(2)}, u32[]{:S(2)}) collective-permute-start(bf16[2,1280,256]{2,1,0:T(8,128)(2,1)S(1)} %pad_maximum_fusion), channel_id=1, source_target_pairs={{0,1},{1,0},{2,3},{3,2},{4,5},{5,4},{6,7},{7,6},{8,9},{9,8},{10,11... | collective-permute-start | bytes 3932168 | tf_op jit(solution)/shard_map/ppermute | solution.py:28
  67.0 39.0 %all-gather.3.cloned.1.call-start = ((), (), s32[]{:S(2)}) async-start(), calls=%async_computation.2 | async-start | bytes 3538944 | tf_op jit(solution)/shard_map/cond/branch_1_fun/all_gather | solution.py:538
  71.1 20.1 %collective-permute-start = (bf16[3,256,256]{2,1,0:T(8,128)(2,1)}, bf16[3,256,256]{2,1,0:T(8,128)(2,1)S(1)}, u32[]{:S(2)}, u32[]{:S(2)}) collective-permute-start(bf16[3,256,256]{2,1,0:T(8,128)(2,1)} %spilled.1), channel_id=1, source_target_pairs={{0,8},{1,9},{2,10},{3,11},{4,12},{5,13},{6,14},{7,15},{8,0},{9,1},... | collective-permute-start | bytes 1179656 | tf_op jit(solution)/shard_map/cond/branch_1_fun/ppermute | solution.py:28
  91.2 0.8 copy-start
  91.9 100.3 %all-to-all-start.1 = ((bf16[16,2,256,256]{3,2,1,0:T(8,128)(2,1)}), bf16[16,2,256,256]{3,2,1,0:T(8,128)(2,1)}, u32[]{:S(2)}, u32[]{:S(2)}) async-start(bf16[16,2,256,256]{3,2,1,0:T(8,128)(2,1)} %bitcast.23), calls=%async_computation.1 | async-start | bytes 8388608 | tf_op jit(solution)/shard_map/cond/branch_1_fun/all_to_all | solution.py:482
  99.6 68.2 %all-gather.5.cloned.1.call-start = ((), (), s32[]{:S(2)}) async-start(), calls=%async_computation.3 | async-start | bytes 3538944 | tf_op jit(solution)/shard_map/cond/branch_1_fun/all_gather | solution.py:542
Sparse Core Ops, SparseCore 0:
  71.2 32.4 all-gather.2
  105.4 62.3 all-gather.4

commit v3 on v2

--- a/solution.py
+++ b/solution.py
@@ -34,10 +34,6 @@
     return got[:rows].reshape(x.shape), got[rows:]
 
 
-def in_order(high, mine, got, axis):
-    return jnp.concatenate([jnp.where(high, got, mine), jnp.where(high, mine, got)], axis=axis)
-
-
 def near(me, roots, bit):
     return (((me ^ roots) & bit) == 0)[:, None, None]
 
@@ -50,8 +46,7 @@
     if note is None:
         got = swap(give, bit, ranks)
     else:
-        got, got_note = swap_with(give, note, bit, ranks)
-        note = in_order(high, note, got_note, 0)
+        got, note = swap_with(give, note, bit, ranks)
     return jnp.where(near(me, roots, bit), own, got), note
 
 
@@ -60,7 +55,8 @@
 
 
 def gather_step(x, me, bit, ranks):
-    return in_order((me & bit) != 0, x, swap(x, bit, ranks), 1)
+    got, high = swap(x, bit, ranks), (me & bit) != 0
+    return jnp.concatenate([jnp.where(high, got, x), jnp.where(high, x, got)], axis=1)
 
 
 def most_of_groups(most):
@@ -76,30 +72,33 @@
 def spread(own, give, me, roots, ranks, digest):
     rows = own.shape[0]
     got = swap(give, 1, ranks)
-    note = in_order((me & 1) != 0, give[rows : rows + 1], got[rows : rows + 1], 0)
+    note, xors = jnp.concatenate([give[rows : rows + 1], got[rows : rows + 1]], axis=0), [0, 1]
     x = jnp.where(near(me, roots, 1), own[None], got[None, :rows])
     half = rows // 2
     a, b = x[:, :half], x[:, half:]
-    a, note = scatter_step(a, note, me, roots, 2, ranks)
+    a, got_note = scatter_step(a, note, me, roots, 2, ranks)
     b, _ = scatter_step(b, None, me, roots, 4, ranks)
-    a, note = scatter_step(a, note, me, roots, 4, ranks)
+    across, across_xors, bit = note, xors, 8
+    while bit < ranks:
+        across = jnp.concatenate([across, swap(across, bit, ranks)], axis=0)
+        across_xors = across_xors + [i ^ bit for i in across_xors]
+        bit *= 2
+    note, xors = jnp.concatenate([across, got_note], axis=0), across_xors + [2, 3]
+    a, got_note = scatter_step(a, note, me, roots, 4, ranks)
     b, _ = scatter_step(b, None, me, roots, 2, ranks)
+    note, xors = jnp.concatenate([note, got_note], axis=0), xors + [i ^ 4 for i in xors]
+    missing = [i for i, other in enumerate(xors) if other >= 8]
+    if missing:
+        sent = jnp.concatenate([note[i : i + 1] for i in missing], axis=0)
+        note = jnp.concatenate([note, swap(sent, 2, ranks)], axis=0)
+        xors = xors + [xors[i] ^ 2 for i in missing]
+    facts = digest(note, xors)
+    worst = most_of_groups(facts[0])
     bit = 8
     while bit < ranks:
-        note = in_order((me & bit) != 0, note, swap(note, bit, ranks), 0)
+        a, b = middle_step(a, me, roots, bit, ranks), middle_step(b, me, roots, bit, ranks)
         bit *= 2
-    facts = digest(note)
-    bit = 8
-    while bit < ranks:
-        a = middle_step(a, me, roots, bit, ranks)
-        bit *= 2
-    b, facts = lax.optimization_barrier((b, facts))
-    bit = 8
-    while bit < ranks:
-        b = middle_step(b, me, roots, bit, ranks)
-        bit *= 2
-    worst = most_of_groups(facts[0])
-    b, worst = lax.optimization_barrier((b, worst))
+    a, b, worst, facts = lax.optimization_barrier((a, b, worst, facts))
     a, b = gather_step(a, me, 4, ranks), gather_step(b, me, 2, ranks)
     a, b = gather_step(a, me, 2, ranks), gather_step(b, me, 4, ranks)
     mine = jnp.concatenate([a, b], axis=1)
@@ -159,7 +158,7 @@
         kept[o] = 0
     spilled_count = jnp.int32(0)
     for q in range(TILES):
-        owner = owner_ref[q // MT, q % MT, 0]
+        owner = owner_ref[q % MT, q // MT]
         keep = (keep_ref[q % MT, q // MT] != 0).astype(jnp.int32)
         rank = kept[owner]
         kept[owner] = rank + keep
@@ -194,13 +193,14 @@
         in_specs=[SMEM, SMEM, SMEM, SMEM, ANY],
         out_specs=(VMEM, VMEM, SMEM, SMEM, SMEM),
         scratch_shapes=[pltpu.SMEM((ranks,), jnp.int32), pltpu.SemaphoreType.DMA((PCAP,))],
+        compiler_params=pltpu.CompilerParams(vmem_limit_bytes=62 * 1024 * 1024),
         name="prepare",
     )(me, mask, owners, keep, panel)
 
 
-def pair_kernel(me_ref, root_ref, note_ref, row_ref, panel_tile_ref, v_tile_ref, at_ref, most_ref):
+def pair_kernel(me_ref, root_row_ref, note_ref, row_ref, panel_tile_ref, v_tile_ref, at_ref, most_ref):
     def listed(s, place):
-        return (note_ref[root_ref[s], TILES + place] != 0).astype(jnp.int32)
+        return (note_ref[root_row_ref[s], TILES + place] != 0).astype(jnp.int32)
 
     most = jnp.int32(0)
     for device in range(note_ref.shape[0]):
@@ -234,7 +234,7 @@
         place_in_pairs = (place_in_pairs + 1) // 2 * 2
 
 
-def pair_up(me, roots, notes):
+def pair_up(me, root_rows, notes):
     members = jax.ShapeDtypeStruct((2 * PAIRS,), jnp.int32)
     *pairs, at, most = pl.pallas_call(
         pair_kernel,
@@ -247,9 +247,10 @@
         ),
         in_specs=[SMEM, SMEM, SMEM],
         out_specs=(SMEM,) * 5,
+        compiler_params=pltpu.CompilerParams(vmem_limit_bytes=4 * 1024 * 1024),
         cost_estimate=pl.CostEstimate(flops=0, bytes_accessed=8 * 1024 * 1024, transcendentals=0),
         name="pair_up",
-    )(me, roots, notes)
+    )(me, root_rows, notes)
     return pairs, at, most
 
 
@@ -376,44 +377,76 @@
         out_shape=jax.ShapeDtypeStruct((SPILL, TILE, TILE), jnp.bfloat16),
         in_specs=[SMEM] * 3 + [VMEM] * 3,
         out_specs=VMEM,
-        compiler_params=pltpu.CompilerParams(vmem_limit_bytes=32 * 1024 * 1024),
+        compiler_params=pltpu.CompilerParams(vmem_limit_bytes=24 * 1024 * 1024),
         name="spilled",
     )(tiles, at, v_mask, mine, got, columns)
 
 
-def clear_kernel(table_ref, out_ref, zero, sem):
+def begin_kernel(split, table_ref, near_ref, out_ref, zero, held, in_sem, out_sem):
     zero[...] = jnp.zeros_like(zero)
-
-    def each(act):
-        def visit(j, carry):
-            @pl.when(table_ref[j] < 0)
-            def _():
-                act(pltpu.make_async_copy(zero, out_ref.at[j], sem.at[j]))
-
-            return carry
-
-        lax.fori_loop(0, out_ref.shape[0], visit, 0)
-
-    each(lambda copy: copy.start())
-    each(lambda copy: copy.wait())
-
-
-def clear(table):
+    slots, reach = out_ref.shape[0], near_ref.shape[0]
+
+    def is_near(j):
+        return (table_ref[j] >= split) & (table_ref[j] < split + reach)
+
+    def fetch(j):
+        return pltpu.make_async_copy(near_ref.at[jnp.maximum(table_ref[j] - split, 0)], held.at[j], in_sem.at[j])
+
+    def start(j, carry):
+        @pl.when(table_ref[j] < 0)
+        def _():
+            pltpu.make_async_copy(zero, out_ref.at[j], out_sem.at[j]).start()
+
+        @pl.when(is_near(j))
+        def _():
+            fetch(j).start()
+
+        return carry
+
+    def forward(j, carry):
+        @pl.when(is_near(j))
+        def _():
+            fetch(j).wait()
+            pltpu.make_async_copy(held.at[j], out_ref.at[j], out_sem.at[j]).start()
+
+        return carry
+
+    def finish(j, carry):
+        @pl.when((table_ref[j] < 0) | is_near(j))
+        def _():
+            pltpu.make_async_copy(zero, out_ref.at[j], out_sem.at[j]).wait()
+
+        return carry
+
+    lax.fori_loop(0, slots, start, 0)
+    lax.fori_loop(0, slots, forward, 0)
+    lax.fori_loop(0, slots, finish, 0)
+
+
+def begin_output(table, split, near_spill):
     slots = table.shape[0]
     return pl.pallas_call(
-        clear_kernel,
+        functools.partial(begin_kernel, split),
         out_shape=jax.ShapeDtypeStruct((slots, TILE, TILE), jnp.bfloat16),
-        in_specs=[SMEM],
+        in_specs=[SMEM, HBM],
         out_specs=HBM,
-        scratch_shapes=[pltpu.VMEM((TILE, TILE), jnp.bfloat16), pltpu.SemaphoreType.DMA((slots,))],
+        scratch_shapes=[
+            pltpu.VMEM((TILE, TILE), jnp.bfloat16),
+            pltpu.VMEM((slots, TILE, TILE), jnp.bfloat16),
+            pltpu.SemaphoreType.DMA((slots,)),
+            pltpu.SemaphoreType.DMA((slots,)),
+        ],
         compiler_params=pltpu.CompilerParams(vmem_limit_bytes=55 * 1024 * 1024),
         cost_estimate=pl.CostEstimate(flops=0, bytes_accessed=8 * 1024 * 1024, transcendentals=0),
-        name="clear",
-    )(table)
-
-
-def place_kernel(split, reach, table_ref, blank_ref, direct_ref, near_ref, far_ref, out_ref, held, in_sem, out_sem):
+        name="begin_output",
+    )(table, near_spill)
+
+
+def place_kernel(split, far_from, table_ref, begun_ref, direct_ref, far_ref, out_ref, held, in_sem, out_sem):
     slots = out_ref.shape[0]
+
+    def is_direct(j):
+        return (table_ref[j] >= 0) & (table_ref[j] < split)
 
     def fetch(ref, place, j):
         return pltpu.make_async_copy(ref.at[place], held.at[j], in_sem.at[j])
@@ -424,22 +457,18 @@
     def begin(j, carry):
         source = table_ref[j]
 
-        @pl.when((source >= 0) & (source < split))
+        @pl.when(is_direct(j))
         def _():
             fetch(direct_ref, source, j).start()
 
-        @pl.when((source >= split) & (source < split + reach))
-        def _():
-            fetch(near_ref, source - split, j).start()
-
-        @pl.when(source >= split + reach)
-        def _():
-            fetch(far_ref, source - split - reach, j).start()
+        @pl.when(source >= far_from)
+        def _():
+            fetch(far_ref, source - far_from, j).start()
 
         return carry
 
     def forward(j, carry):
-        @pl.when(table_ref[j] >= 0)
+        @pl.when(is_direct(j) | (table_ref[j] >= far_from))
         def _():
             fetch(direct_ref, 0, j).wait()
             store(j).start()
@@ -447,7 +476,7 @@
         return carry
 
     def finish(j, carry):
-        @pl.when(table_ref[j] >= 0)
+        @pl.when(is_direct(j) | (table_ref[j] >= far_from))
         def _():
             store(j).wait()
 
@@ -458,12 +487,12 @@
     lax.fori_loop(0, slots, finish, 0)
 
 
-def place_tiles(table, blank, direct, near_spill, far_spill):
-    slots, split, reach = table.shape[0], direct.shape[0], near_spill.shape[0]
+def place_tiles(table, begun, direct, far_from, far_spill):
+    slots = table.shape[0]
     return pl.pallas_call(
-        functools.partial(place_kernel, split, reach),
+        functools.partial(place_kernel, direct.shape[0], far_from),
         out_shape=jax.ShapeDtypeStruct((slots, TILE, TILE), jnp.bfloat16),
-        in_specs=[SMEM, HBM, HBM, HBM, HBM],
+        in_specs=[SMEM, HBM, HBM, HBM],
         out_specs=HBM,
         scratch_shapes=[
             pltpu.VMEM((slots, TILE, TILE), jnp.bfloat16),
@@ -473,7 +502,7 @@
         input_output_aliases={1: 0},
         compiler_params=pltpu.CompilerParams(vmem_limit_bytes=55 * 1024 * 1024),
         name="place_tiles",
-    )(table, blank, direct, near_spill, far_spill)
+    )(table, begun, direct, far_spill)
 
 
 def exchange(tiles, ranks):
@@ -496,7 +525,7 @@
         t2_panels,
         me.reshape(1),
         t2_mask,
-        owner_map,
+        owner_map[:, :, 0].T,
         r_mask,
         ranks,
         slots_each,
@@ -507,12 +536,15 @@
     v_rows = jnp.pad(v_rows, ((0, 1), (0, 0), (0, 0)))
     columns = fetch_columns(v, spill_tiles)
 
-    def digest(notes):
+    def digest(notes, xors):
         notes = notes[:, : TILES + MT * KPT + 1].astype(jnp.int32)
-        pairs, at, most = pair_up(me.reshape(1), roots, notes)
-        return most, notes, pairs, at, columns
-
-    mine, got, worst, (notes, pairs, at, columns) = spread(own, give, me, roots, ranks, digest)
+        devices = me ^ jnp.asarray(xors, jnp.int32)
+        order = jnp.arange(ranks, dtype=jnp.int32)
+        root_rows = jnp.sum(jnp.where(devices[None, :] == roots[:, None], order, 0), axis=1)
+        pairs, at, most = pair_up(me.reshape(1), root_rows, notes)
+        return most, notes, devices, pairs, at, columns
+
+    mine, got, worst, (notes, devices, pairs, at, columns) = spread(own, give, me, roots, ranks, digest)
     mine, got = mine.reshape(-1, TILE), got.reshape(-1, TILE)
 
     split = ranks * direct
@@ -520,7 +552,7 @@
     def table_of(notes, short):
         owners, keep = notes[:, :TILES] // 2, notes[:, :TILES] % 2 != 0
         rank, kept_rank, spills, spill_place = ranks_of(owners, keep, direct)
-        device = jnp.arange(ranks, dtype=jnp.int32)[:, None]
+        device = devices[:, None]
         slot = jnp.arange(slots_each, dtype=jnp.int32)
         if short:
             far = ((device ^ me) & top) // top
@@ -529,7 +561,9 @@
         else:
             origin = device * slots_each + kept_rank
         arrives = ((owners == me) & keep)[:, None, :] & (rank[:, None, :] == slot[None, :, None])
-        return (jnp.sum(jnp.where(arrives, origin[:, None, :] + 1, 0), axis=2) - 1).reshape(-1)
+        listed = jnp.sum(jnp.where(arrives, origin[:, None, :] + 1, 0), axis=2)
+        in_place = devices[None, :] == jnp.arange(ranks, dtype=jnp.int32)[:, None]
+        return (jnp.sum(jnp.where(in_place[:, :, None], listed[None], 0), axis=1) - 1).reshape(-1)
 
     halves = [list(range(top)), list(range(top, ranks))]
 
@@ -541,14 +575,16 @@
         other, tiles, notes = lax.optimization_barrier((other, tiles, notes))
         far_spill = lax.all_gather(other, "row", axis=0, tiled=True, axis_index_groups=halves)
         table = table_of(notes, True)
-        blank = clear(table)
-        return place_tiles(table, blank, exchange(tiles, ranks), near_spill, far_spill)
+        begun = begin_output(table, split, near_spill)
+        far_from = split + near_spill.shape[0]
+        return place_tiles(table, begun, exchange(tiles, ranks), far_from, far_spill)
 
     def long(mine, got, v, v_rows, _, notes, __, ___, places):
         tiles = ladder(mine, got, pairs, v, v_rows, places, ranks * slots_each)
         unused = jnp.zeros((1, TILE, TILE), jnp.bfloat16)
         table = table_of(notes, False)
-        return place_tiles(table, clear(table), exchange(tiles, ranks), unused, unused)
+        begun = begin_output(table, ranks * slots_each, unused)
+        return place_tiles(table, begun, exchange(tiles, ranks), ranks * slots_each + 1, unused)
 
     delivered = lax.cond(
         worst[0, 0] <= SPILL,

time: 206 us -> 201 us (0.976)
  starting transfers between devices: 28.8 us -> 21.2 us
  waiting for transfers between devices: 118 us -> 121 us
    ppermute x14 -> x15, starting transfers between devices: 19.5 us -> 12.5 us  [swap(): return lax.ppermute(x, 'row', [(i, i ^ bit) for i in range(ranks)])]
    ppermute x14 -> x15, waiting for transfers between devices: 29.1 us -> 32.1 us  [swap(): return lax.ppermute(x, 'row', [(i, i ^ bit) for i in range(ranks)])]
    all_gather x1, waiting for transfers between devices: 61.8 us -> 58.8 us  [short(): lax.all_gather(other, 'row', axis=0, tiled=True, axis_index_groups=halves)]
    all_gather x1, waiting for transfers between devices: 0.02 us -> 2.2 us  [short(): lax.all_gather(spill, 'row', axis=0, tiled=True, axis_index_groups=halves)]
  transfers between devices with their start and end apart: 18 -> 19, of which waited for: 16 -> 15; matrix products, arithmetic and copies ran while one was open for 2% -> 3% of each run, Pallas kernels for 10% -> 11%
where the time goes in v3:
time: 201 us; the launch traced here: 198 us
  waiting for transfers between devices  121 us (60%)
  Pallas kernels  33.8 us (17%)
  starting transfers between devices  21.2 us (11%)
  between operations  15 us (7%)
  other arithmetic  4.12 us (2%)
  local copies, waits for them, and re-layouts  3.41 us (2%)
    all_gather x1, waiting for transfers between devices, short(): lax.all_gather(other, 'row', axis=0, tiled=True, axis_index_groups=halves)  58.8 us
    ppermute x15, waiting for transfers between devices, swap(): return lax.ppermute(x, 'row', [(i, i ^ bit) for i in range(ranks)])  32.1 us
    all_to_all x1, waiting for transfers between devices, exchange(): lax.all_to_all(sent, 'row', split_axis=0, concat_axis=0, tiled=True)  24.3 us
    ppermute x15, starting transfers between devices, swap(): return lax.ppermute(x, 'row', [(i, i ^ bit) for i in range(ranks)])  12.5 us
    pallas_call x1, Pallas kernels, ladder(): pl.pallas_call(ladder_kernel, out_shape=jax.ShapeDtypeStruct((slots, TILE...  11.3 us
    all_to_all x1, starting transfers between devices, exchange(): lax.all_to_all(sent, 'row', split_axis=0, concat_axis=0, tiled=True)  7.66 us
    pallas_call x1, Pallas kernels, fetch_columns(): pl.pallas_call(fetch_kernel, out_shape=jax.ShapeDtypeStruct((SPILL, v.sha...  4.57 us
    pallas_call x1, Pallas kernels, place_tiles(): pl.pallas_call(functools.partial(place_kernel, direct.shape[0], far_from)...  4.36 us
  transfers between devices with their start and end apart: 19, of which 15 were waited for; matrix products, arithmetic and copies ran while one was open for 3% of the time, Pallas kernels for 11%

profile of v3, /device:TPU:16, one launch (start us, length us, event | category | flops | bytes accessed | tf_op | source)
XLA Modules:
  0.0 198.4 jit_solution(14050003886647669899)
XLA Ops:
  6.5 3.5 %prepare.1 = (bf16[1280,256]{1,0:T(8,128)(2,1)}, bf16[1296,256]{1,0:T(8,128)(2,1)}, s32[32]{0:T(128)S(1)}, s32[32]{0:T(128)S(1)}, s32[3]{0:T(128)S(1)}) custom-call(s32[1]{0:T(128)} %bitcast.6.me_ref, s32[1,4,5]{2,1,0:T(4,128)} %mask_ref.1, s32[4,8]{1,0:T(4,128)} %bitcast.33, s32[4,8]{1,0:T(4,128)} %keep_ref.1, bf16[1,1024,1280]{2,1,0:T(8,128)(2,1)} %panel_ref.1), custom_call_target="tpu_custom_call" | custom-call | tf_op jit(solution)/shard_map/prepare/pallas_call | solution.py:184
  10.8 1.6 collective-permute-done.1
  12.5 1.3 broadcast_select_fusion
  13.8 1.6 collective-permute-start.6
  15.5 1.6 collective-permute-start.2
  17.1 4.6 %fetch_columns.1 = bf16[3,2560,256]{2,1,0:T(8,128)(2,1)} custom-call(s32[3]{0:T(128)S(1)} %get-tuple-element.117.tile_ref, bf16[2560,2048]{1,0:T(8,128)(2,1)} %bitcast.20), custom_call_target="tpu_custom_call" | custom-call | bytes 8388608 | tf_op jit(solution)/shard_map/fetch_columns/pallas_call | solution.py:349
  22.4 2.7 %collective-permute-done.2 = bf16[642,256]{1,0:T(8,128)(2,1)S(1)} collective-permute-done((bf16[642,256]{1,0:T(8,128)(2,1)S(1)}, bf16[642,256]{1,0:T(8,128)(2,1)S(1)}, u32[]{:S(2)}, u32[]{:S(2)}) %collective-permute-start.2) | collective-permute-done | bytes 328736 | tf_op jit(solution)/shard_map/ppermute | solution.py:28
  25.4 1.6 collective-permute-start.7
  27.6 3.1 %collective-permute-done.7 = bf16[2,160,256]{2,1,0:T(8,128)(2,1)S(1)} collective-permute-done((bf16[2,160,256]{2,1,0:T(8,128)(2,1)S(1)}, bf16[2,160,256]{2,1,0:T(8,128)(2,1)S(1)}, u32[]{:S(2)}, u32[]{:S(2)}) %collective-permute-start.7) | collective-permute-done | bytes 163872 | tf_op jit(solution)/shard_map/ppermute | solution.py:28
  31.3 3.1 %collective-permute-done.4 = bf16[326,256]{1,0:T(8,128)(2,1)S(1)} collective-permute-done((bf16[326,256]{1,0:T(8,128)(2,1)S(1)}, bf16[326,256]{1,0:T(8,128)(2,1)S(1)}, u32[]{:S(2)}, u32[]{:S(2)}) %collective-permute-start.4) | collective-permute-done | bytes 166944 | tf_op jit(solution)/shard_map/ppermute | solution.py:28
  35.6 2.4 %collective-permute-done.9 = bf16[4,256]{1,0:T(4,128)(2,1)S(1)} collective-permute-done((bf16[4,256]{1,0:T(4,128)(2,1)S(1)}, bf16[4,256]{1,0:T(4,128)(2,1)S(1)}, u32[]{:S(2)}, u32[]{:S(2)}) %collective-permute-start.9) | collective-permute-done | bytes 2080 | tf_op jit(solution)/shard_map/ppermute | solution.py:28
  38.2 1.8 pair_up.1
  40.0 1.1 collective-permute-start.10
  41.0 2.6 %collective-permute-done.10 = s32[1,1]{1,0:T(1,128)} collective-permute-done((s32[1,1]{1,0:T(1,128)}, s32[1,1]{1,0:T(1,128)}, u32[]{:S(2)}, u32[]{:S(2)}) %collective-permute-start.10) | collective-permute-done | bytes 36 | tf_op jit(solution)/shard_map/ppermute | solution.py:67
  45.1 1.8 collective-permute-start.11
  47.0 1.5 collective-permute-start.13
  48.5 2.1 %collective-permute-done.11 = bf16[2,160,256]{2,1,0:T(8,128)(2,1)S(1)} collective-permute-done((bf16[2,160,256]{2,1,0:T(8,128)(2,1)S(1)}, bf16[2,160,256]{2,1,0:T(8,128)(2,1)S(1)}, u32[]{:S(2)}, u32[]{:S(2)}) %collective-permute-start.11) | collective-permute-done | bytes 163872 | tf_op jit(solution)/shard_map/ppermute | solution.py:28
  50.6 1.3 collective-permute-start.12
  51.9 1.8 collective-permute-done.13
  54.1 5.2 %collective-permute-done.12 = bf16[2,320,256]{2,1,0:T(8,128)(2,1)S(1)} collective-permute-done((bf16[2,320,256]{2,1,0:T(8,128)(2,1)S(1)}, bf16[2,320,256]{2,1,0:T(8,128)(2,1)S(1)}, u32[]{:S(2)}, u32[]{:S(2)}) %collective-permute-start.12) | collective-permute-done | bytes 327712 | tf_op jit(solution)/shard_map/ppermute | solution.py:28
  59.4 1.5 collective-permute-done.14
  61.5 2.8 %collective-permute-done.15 = bf16[2,1280,256]{2,1,0:T(8,128)(2,1)S(1)} collective-permute-done((bf16[2,1280,256]{2,1,0:T(8,128)(2,1)S(1)}, bf16[2,1280,256]{2,1,0:T(8,128)(2,1)S(1)}, u32[]{:S(2)}, u32[]{:S(2)}) %collective-permute-start.15) | collective-permute-done | bytes 1310752 | tf_op jit(solution)/shard_map/ppermute | solution.py:28
  64.3 127.3 %conditional.1 = (bf16[16,4,256,256]{3,2,1,0:T(8,128)(2,1)}) conditional(s32[]{:T(128)} %bitcast.14, (s32[16]{0:T(128)S(1)}, s32[16,53]{1,0:T(8,128)S(1)}, s32[]{:T(128)}, s32[12]{0:T(128)S(1)}, s32[24]{0:T(128)S(1)}, /*index=5*/s32[24]{0:T(128)S(1)}, s32[32]{0:T(128)S(1)}, bf16[2560,256]{1,0:T(8,128)(2,1)S(1)}, bf16[2560,256]{1,0:T(8,128)(2,1)S(1)}, ...), branch_computations={%region_1.6_spmd, %region_6.12_spmd} | conditional | flops 12885091328 | bytes 70642632 | solution.py:589
  64.3 4.1 %spilled.1 = bf16[3,256,256]{2,1,0:T(8,128)(2,1)} custom-call(s32[3]{0:T(128)S(1)} %get-tuple-element.73.tile_ref, s32[40]{0:T(128)S(1)} %get-tuple-element.74.at_ref, s32[2,5,8]{2,1,0:T(8,128)S(1)} %copy.31.v_mask_ref, bf16[2560,256]{1,0:T(8,128)(2,1)S(1)} %get-tuple-element.76.mine_ref, bf16[2560,256]{1,0:T(8,128)(2,1)S(1)} %get-tuple-element.77.got_ref, ...), custom_call_target="tpu_custom_call" | custom-call | tf_op jit(solution)/shard_map/cond/branch_1_fun/spilled/pallas_call | solution.py:375
  69.1 11.3 %ladder.3 = bf16[32,256,256]{2,1,0:T(8,128)(2,1)} custom-call(s32[12]{0:T(128)S(1)} %get-tuple-element.79.row_ref, s32[24]{0:T(128)S(1)} %get-tuple-element.80.panel_tile_ref, s32[24]{0:T(128)S(1)} %get-tuple-element.81.v_tile_ref, s32[32]{0:T(128)S(1)} %get-tuple-element.82.place_ref, bf16[2560,256]{1,0:T(8,128)(2,1)S(1)} %get-tuple-element.76.mine_ref, ...), custom_call_target="tpu_custom_call" | custom-call | flops 12884901888 | bytes 25165824 | tf_op jit(solution)/shard_map/cond/branch_1_fun/ladder/pallas_call | solution.py:308
  80.4 5.7 %collective-permute-done = bf16[3,256,256]{2,1,0:T(8,128)(2,1)S(1)} collective-permute-done((bf16[3,256,256]{2,1,0:T(8,128)(2,1)}, bf16[3,256,256]{2,1,0:T(8,128)(2,1)S(1)}, u32[]{:S(2)}, u32[]{:S(2)}) %collective-permute-start) | collective-permute-done | bytes 393248 | tf_op jit(solution)/shard_map/cond/branch_1_fun/ppermute | solution.py:28
  86.9 7.7 %all-to-all-start.1 = ((bf16[16,2,256,256]{3,2,1,0:T(8,128)(2,1)}), bf16[16,2,256,256]{3,2,1,0:T(8,128)(2,1)}, u32[]{:S(2)}, u32[]{:S(2)}) async-start(bf16[16,2,256,256]{3,2,1,0:T(8,128)(2,1)} %bitcast.26), calls=%async_computation.1 | async-start | bytes 8388608 | tf_op jit(solution)/shard_map/cond/branch_1_fun/all_to_all | solution.py:511
  97.6 2.2 %all-gather.3.cloned.1.call-done.near_ref = bf16[24,256,256]{2,1,0:T(8,128)(2,1)} async-done(((bf16[3,256,256]{2,1,0:T(8,128)(2,1)}), bf16[24,256,256]{2,1,0:T(8,128)(2,1)}) %all-gather.3.cloned.1.call-update) | async-done | bytes 3145744 | tf_op jit(solution)/shard_map/cond/branch_1_fun/all_gather | solution.py:572
  99.8 4.3 %begin_output.3.begun_ref = bf16[64,256,256]{2,1,0:T(8,128)(2,1)} custom-call(s32[64]{0:T(128)} %sub.23.table_ref, bf16[24,256,256]{2,1,0:T(8,128)(2,1)} %all-gather.3.cloned.1.call-done.near_ref), custom_call_target="tpu_custom_call" | custom-call | bytes 8388608 | tf_op jit(solution)/shard_map/cond/branch_1_fun/begin_output/pallas_call | solution.py:428
  104.1 58.8 %all-gather.5.cloned.1.call-done.far_ref = bf16[24,256,256]{2,1,0:T(8,128)(2,1)} async-done(((bf16[3,256,256]{2,1,0:T(8,128)(2,1)}), bf16[24,256,256]{2,1,0:T(8,128)(2,1)}) %all-gather.5.cloned.1.call-update) | async-done | bytes 3145744 | tf_op jit(solution)/shard_map/cond/branch_1_fun/all_gather | solution.py:576
  162.9 24.3 %all-to-all-done.1 = bf16[16,2,256,256]{3,2,1,0:T(8,128)(2,1)} async-done(((bf16[16,2,256,256]{3,2,1,0:T(8,128)(2,1)}), bf16[16,2,256,256]{3,2,1,0:T(8,128)(2,1)}, u32[]{:S(2)}, u32[]{:S(2)}) %all-to-all-start.1) | async-done | bytes 4194336 | tf_op jit(solution)/shard_map/cond/branch_1_fun/all_to_all | solution.py:511
  187.2 4.4 %place_tiles.3 = bf16[64,256,256]{2,1,0:T(8,128)(2,1)} custom-call(s32[64]{0:T(128)} %sub.23.table_ref, bf16[64,256,256]{2,1,0:T(8,128)(2,1)} %begin_output.3.begun_ref, bf16[32,256,256]{2,1,0:T(8,128)(2,1)} %bitcast.4.direct_ref, bf16[24,256,256]{2,1,0:T(8,128)(2,1)} %all-gather.5.cloned.1.call-done.far_ref), custom_call_target="tpu_custom_call", output_to_operand_aliasing={{}: (1, {})} | custom-call | tf_op jit(solution)/shard_map/cond/branch_1_fun/place_tiles/pallas_call | solution.py:492
  (78 shorter events, 10.1 us)
Async XLA Ops:
  6.5 4.2 %copy-start.2 = (s32[2]{0:T(128)S(1)}, s32[2]{0:T(128)}, u32[]{:S(2)}) copy-start(s32[2]{0:T(128)} %param.16) | copy-start | bytes 28
  10.0 2.4 %collective-permute-start.1 = (bf16[1296,256]{1,0:T(8,128)(2,1)}, bf16[1296,256]{1,0:T(8,128)(2,1)S(1)}, u32[]{:S(2)}, u32[]{:S(2)}) collective-permute-start(bf16[1296,256]{1,0:T(8,128)(2,1)} %get-tuple-element.111), channel_id=1, source_target_pairs={{0,1},{1,0},{2,3},{3,2},{4,5},{5,4},{6,7},{7,6},{8,9},{9,8},{10,11... | collective-permute-start | bytes 1990664 | tf_op jit(solution)/shard_map/ppermute | solution.py:28
  12.4 4.6 %copy-start.3 = (s32[16]{0:T(128)S(1)}, s32[16]{0:T(128)}, u32[]{:S(2)}) copy-start(s32[16]{0:T(128)} %constant.108.clone) | copy-start | bytes 196
  13.8 11.3 %collective-permute-start.6 = (bf16[2,320,256]{2,1,0:T(8,128)(2,1)S(1)}, bf16[2,320,256]{2,1,0:T(8,128)(2,1)S(1)}, u32[]{:S(2)}, u32[]{:S(2)}) collective-permute-start(bf16[2,320,256]{2,1,0:T(8,128)(2,1)S(1)} %get-tuple-element.240), channel_id=1, source_target_pairs={{0,4},{1,5},{2,6},{3,7},{4,0},{5,1},{6,2},{7,3},{8,12},{9,13},{10,... | collective-permute-start | bytes 983048 | tf_op jit(solution)/shard_map/ppermute | solution.py:28
  15.5 9.6 %collective-permute-start.2 = (bf16[642,256]{1,0:T(8,128)(2,1)S(1)}, bf16[642,256]{1,0:T(8,128)(2,1)S(1)}, u32[]{:S(2)}, u32[]{:S(2)}) collective-permute-start(bf16[642,256]{1,0:T(8,128)(2,1)S(1)} %pad_maximum_fusion.1), channel_id=1, source_target_pairs={{0,2},{1,3},{2,0},{3,1},{4,6},{5,7},{6,4},{7,5},{8,10},{9,11},{10,... | collective-permute-start | bytes 986120 | tf_op jit(solution)/shard_map/ppermute | solution.py:28
  21.9 5.1 %collective-permute-start.3 = (bf16[2,256]{1,0:T(2,128)(2,1)S(1)}, bf16[2,256]{1,0:T(2,128)(2,1)S(1)}, u32[]{:S(2)}, u32[]{:S(2)}) collective-permute-start(bf16[2,256]{1,0:T(2,128)(2,1)S(1)} %pad_maximum_fusion.5), channel_id=1, source_target_pairs={{0,8},{1,9},{2,10},{3,11},{4,12},{5,13},{6,14},{7,15},{8,0},{9,1},... | collective-permute-start | bytes 3080 | tf_op jit(solution)/shard_map/ppermute | solution.py:28
  25.4 5.4 %collective-permute-start.7 = (bf16[2,160,256]{2,1,0:T(8,128)(2,1)S(1)}, bf16[2,160,256]{2,1,0:T(8,128)(2,1)S(1)}, u32[]{:S(2)}, u32[]{:S(2)}) collective-permute-start(bf16[2,160,256]{2,1,0:T(8,128)(2,1)S(1)} %broadcast_select_fusion.11), channel_id=1, source_target_pairs={{0,2},{1,3},{2,0},{3,1},{4,6},{5,7},{6,4},{7,5},{8,10},{9,11},{10,... | collective-permute-start | bytes 491528 | tf_op jit(solution)/shard_map/ppermute | solution.py:28
  27.1 7.2 %collective-permute-start.4 = (bf16[326,256]{1,0:T(8,128)(2,1)S(1)}, bf16[326,256]{1,0:T(8,128)(2,1)S(1)}, u32[]{:S(2)}, u32[]{:S(2)}) collective-permute-start(bf16[326,256]{1,0:T(8,128)(2,1)S(1)} %concatenate.32), channel_id=1, source_target_pairs={{0,4},{1,5},{2,6},{3,7},{4,0},{5,1},{6,2},{7,3},{8,12},{9,13},{10,... | collective-permute-start | bytes 500744 | tf_op jit(solution)/shard_map/ppermute | solution.py:28
  30.9 14.2 %collective-permute-start.8 = (bf16[2,160,256]{2,1,0:T(8,128)(2,1)S(1)}, bf16[2,160,256]{2,1,0:T(8,128)(2,1)S(1)}, u32[]{:S(2)}, u32[]{:S(2)}) collective-permute-start(bf16[2,160,256]{2,1,0:T(8,128)(2,1)S(1)} %select_select_fusion.2), channel_id=1, source_target_pairs={{0,8},{1,9},{2,10},{3,11},{4,12},{5,13},{6,14},{7,15},{8,0},{9,1},... | collective-permute-start | bytes 491528 | tf_op jit(solution)/shard_map/ppermute | solution.py:28
  34.4 3.6 %collective-permute-start.9 = (bf16[4,256]{1,0:T(4,128)(2,1)S(1)}, bf16[4,256]{1,0:T(4,128)(2,1)S(1)}, u32[]{:S(2)}, u32[]{:S(2)}) collective-permute-start(bf16[4,256]{1,0:T(4,128)(2,1)S(1)} %pad_maximum_fusion.4), channel_id=1, source_target_pairs={{0,2},{1,3},{2,0},{3,1},{4,6},{5,7},{6,4},{7,5},{8,10},{9,11},{10,... | collective-permute-start | bytes 6152 | tf_op jit(solution)/shard_map/ppermute | solution.py:28
  34.7 10.3 %collective-permute-start.5 = (bf16[2,160,256]{2,1,0:T(8,128)(2,1)S(1)}, bf16[2,160,256]{2,1,0:T(8,128)(2,1)S(1)}, u32[]{:S(2)}, u32[]{:S(2)}) collective-permute-start(bf16[2,160,256]{2,1,0:T(8,128)(2,1)S(1)} %select_select_fusion.3), channel_id=1, source_target_pairs={{0,8},{1,9},{2,10},{3,11},{4,12},{5,13},{6,14},{7,15},{8,0},{9,1},... | collective-permute-start | bytes 491528 | tf_op jit(solution)/shard_map/ppermute | solution.py:28
  40.0 3.7 %collective-permute-start.10 = (s32[1,1]{1,0:T(1,128)}, s32[1,1]{1,0:T(1,128)}, u32[]{:S(2)}, u32[]{:S(2)}) collective-permute-start(s32[1,1]{1,0:T(1,128)} %get-tuple-element.112), channel_id=1, source_target_pairs={{0,16},{16,0},{1,17},{17,1},{2,18},{18,2},{3,19},{19,3},{4,20},{20... | collective-permute-start | bytes 20 | tf_op jit(solution)/shard_map/ppermute | solution.py:67
  45.1 5.4 %collective-permute-start.11 = (bf16[2,160,256]{2,1,0:T(8,128)(2,1)S(1)}, bf16[2,160,256]{2,1,0:T(8,128)(2,1)S(1)}, u32[]{:S(2)}, u32[]{:S(2)}) collective-permute-start(bf16[2,160,256]{2,1,0:T(8,128)(2,1)S(1)} %get-tuple-element.125), channel_id=1, source_target_pairs={{0,4},{1,5},{2,6},{3,7},{4,0},{5,1},{6,2},{7,3},{8,12},{9,13},{10,... | collective-permute-start | bytes 491528 | tf_op jit(solution)/shard_map/ppermute | solution.py:28
  47.0 6.8 %collective-permute-start.13 = (bf16[2,160,256]{2,1,0:T(8,128)(2,1)S(1)}, bf16[2,160,256]{2,1,0:T(8,128)(2,1)S(1)}, u32[]{:S(2)}, u32[]{:S(2)}) collective-permute-start(bf16[2,160,256]{2,1,0:T(8,128)(2,1)S(1)} %get-tuple-element.126), channel_id=1, source_target_pairs={{0,2},{1,3},{2,0},{3,1},{4,6},{5,7},{6,4},{7,5},{8,10},{9,11},{10,... | collective-permute-start | bytes 491528 | tf_op jit(solution)/shard_map/ppermute | solution.py:28
  50.6 8.7 %collective-permute-start.12 = (bf16[2,320,256]{2,1,0:T(8,128)(2,1)S(1)}, bf16[2,320,256]{2,1,0:T(8,128)(2,1)S(1)}, u32[]{:S(2)}, u32[]{:S(2)}) collective-permute-start(bf16[2,320,256]{2,1,0:T(8,128)(2,1)S(1)} %pad_maximum_fusion.2), channel_id=1, source_target_pairs={{0,2},{1,3},{2,0},{3,1},{4,6},{5,7},{6,4},{7,5},{8,10},{9,11},{10,... | collective-permute-start | bytes 983048 | tf_op jit(solution)/shard_map/ppermute | solution.py:28
  53.8 7.5 %copy-start.1 = (s32[2,5,8]{2,0,1:T(2,128)S(1)}, s32[2,5,8]{2,0,1:T(2,128)}, u32[]{:S(2)}) copy-start(s32[2,5,8]{2,0,1:T(2,128)} %param.13) | copy-start | bytes 964
  53.8 7.1 %collective-permute-start.14 = (bf16[2,320,256]{2,1,0:T(8,128)(2,1)S(1)}, bf16[2,320,256]{2,1,0:T(8,128)(2,1)S(1)}, u32[]{:S(2)}, u32[]{:S(2)}) collective-permute-start(bf16[2,320,256]{2,1,0:T(8,128)(2,1)S(1)} %pad_maximum_fusion.3), channel_id=1, source_target_pairs={{0,4},{1,5},{2,6},{3,7},{4,0},{5,1},{6,2},{7,3},{8,12},{9,13},{10,... | collective-permute-start | bytes 983048 | tf_op jit(solution)/shard_map/ppermute | solution.py:28
  61.2 3.1 %collective-permute-start.15 = (bf16[2,1280,256]{2,1,0:T(8,128)(2,1)S(1)}, bf16[2,1280,256]{2,1,0:T(8,128)(2,1)S(1)}, u32[]{:S(2)}, u32[]{:S(2)}) collective-permute-start(bf16[2,1280,256]{2,1,0:T(8,128)(2,1)S(1)} %pad_maximum_fusion), channel_id=1, source_target_pairs={{0,1},{1,0},{2,3},{3,2},{4,5},{5,4},{6,7},{7,6},{8,9},{9,8},{10,11... | collective-permute-start | bytes 3932168 | tf_op jit(solution)/shard_map/ppermute | solution.py:28
  64.3 35.5 %all-gather.3.cloned.1.call-start = ((), (), s32[]{:S(2)}) async-start(), calls=%async_computation.2 | async-start | bytes 3538944 | tf_op jit(solution)/shard_map/cond/branch_1_fun/all_gather | solution.py:572
  68.4 17.8 %collective-permute-start = (bf16[3,256,256]{2,1,0:T(8,128)(2,1)}, bf16[3,256,256]{2,1,0:T(8,128)(2,1)S(1)}, u32[]{:S(2)}, u32[]{:S(2)}) collective-permute-start(bf16[3,256,256]{2,1,0:T(8,128)(2,1)} %spilled.1), channel_id=1, source_target_pairs={{0,8},{1,9},{2,10},{3,11},{4,12},{5,13},{6,14},{7,15},{8,0},{9,1},... | collective-permute-start | bytes 1179656 | tf_op jit(solution)/shard_map/cond/branch_1_fun/ppermute | solution.py:28
  86.1 0.7 copy-start
  86.9 100.4 %all-to-all-start.1 = ((bf16[16,2,256,256]{3,2,1,0:T(8,128)(2,1)}), bf16[16,2,256,256]{3,2,1,0:T(8,128)(2,1)}, u32[]{:S(2)}, u32[]{:S(2)}) async-start(bf16[16,2,256,256]{3,2,1,0:T(8,128)(2,1)} %bitcast.26), calls=%async_computation.1 | async-start | bytes 8388608 | tf_op jit(solution)/shard_map/cond/branch_1_fun/all_to_all | solution.py:511
  94.5 68.4 %all-gather.5.cloned.1.call-start = ((), (), s32[]{:S(2)}) async-start(), calls=%async_computation.3 | async-start | bytes 3538944 | tf_op jit(solution)/shard_map/cond/branch_1_fun/all_gather | solution.py:576
Sparse Core Ops, SparseCore 0:
  68.5 31.2 all-gather.2
  101.5 61.4 all-gather.4

commit v4 on v3

--- a/solution.py
+++ b/solution.py
@@ -15,6 +15,7 @@
 PCAP = 10
 TILES = MT * NT_DEV
 SPILL = 3
+SPILL_TERMS = 4
 STEP_TILES = 2
 STEP_COLS = STEP_TILES * TILE
 PAIRS = (SECTIONS * PCAP + MT) // 2
@@ -105,20 +106,21 @@
     return mine, swap(mine, 1, ranks), worst, facts[1:]
 
 
-def ranks_of(owners, keep, direct):
+def ranks_of(owners, keep, far, direct):
     order = jnp.arange(TILES)
     earlier = order[None, :] < order[:, None]
     same = (owners[:, :, None] == owners[:, None, :]) & earlier
     rank = jnp.sum(same, axis=2, dtype=jnp.int32)
     kept_rank = jnp.sum(same & keep[:, None, :], axis=2, dtype=jnp.int32)
     spills = keep & (kept_rank >= direct)
-    spill_place = jnp.sum(spills[:, None, :] & earlier, axis=2, dtype=jnp.int32)
+    alike = (far[:, :, None] == far[:, None, :]) & earlier
+    spill_place = jnp.sum(spills[:, None, :] & alike, axis=2, dtype=jnp.int32)
     return rank, kept_rank, spills, spill_place
 
 
 def prepare_kernel(
     slots_each, direct, me_ref, mask_ref, owner_ref, keep_ref, panel_ref,
-    own_ref, give_ref, short_ref, long_ref, spill_ref, kept, sem,
+    own_ref, give_ref, short_ref, long_ref, spill_ref, goes_ref, kept, sem,
 ):
     half = PCAP // 2
     high = me_ref[0] % 2
@@ -154,9 +156,11 @@
         note = jnp.where(column == TILES + place, mask_ref[0, place // KPT, place % KPT].astype(jnp.float32), note)
     for e in range(SPILL):
         spill_ref[e] = -1
+        goes_ref[e] = -1
     for o in range(kept.shape[0]):
         kept[o] = 0
-    spilled_count = jnp.int32(0)
+    near_count, far_count = jnp.int32(0), jnp.int32(0)
+    top = kept.shape[0] // 2
     for q in range(TILES):
         owner = owner_ref[q % MT, q // MT]
         keep = (keep_ref[q % MT, q // MT] != 0).astype(jnp.int32)
@@ -166,13 +170,20 @@
         short_ref[q] = jnp.where(keep * (1 - over) != 0, owner * direct + rank, -1)
         long_ref[q] = jnp.where(keep != 0, owner * slots_each + rank, -1)
 
-        @pl.when((over != 0) & (spilled_count < SPILL))
-        def _(q=q, spilled_count=spilled_count):
-            spill_ref[jnp.minimum(spilled_count, SPILL - 1)] = q
-
-        spilled_count = spilled_count + over
+        far = (owner // top != me_ref[0] // top).astype(jnp.int32) * over
+        near = over - far
+
+        count = near_count + far_count
+
+        @pl.when((over != 0) & (count < SPILL))
+        def _(q=q, count=count, goes=jnp.where(far != 0, SPILL + far_count, near_count)):
+            spill_ref[jnp.minimum(count, SPILL - 1)] = q
+            goes_ref[jnp.minimum(count, SPILL - 1)] = goes
+
+        far_count, near_count = far_count + far, near_count + near
         note = jnp.where(column == q, (owner * 2 + keep).astype(jnp.float32), note)
-    note = jnp.where(column == TILES + MT * KPT, spilled_count.astype(jnp.float32), note)
+    note = jnp.where(column == TILES + MT * KPT, (near_count + far_count).astype(jnp.float32), note)
+    note = jnp.where(column == TILES + MT * KPT + 1, far_count.astype(jnp.float32), note)
     give_ref[half * TILE : half * TILE + 16, :] = note.astype(jnp.bfloat16)
     for number in range(PCAP):
         tile_copy(0, own_ref, 0, number).wait()
@@ -189,9 +200,10 @@
             places,
             places,
             jax.ShapeDtypeStruct((SPILL,), jnp.int32),
+            jax.ShapeDtypeStruct((SPILL,), jnp.int32),
         ),
         in_specs=[SMEM, SMEM, SMEM, SMEM, ANY],
-        out_specs=(VMEM, VMEM, SMEM, SMEM, SMEM),
+        out_specs=(VMEM, VMEM, SMEM, SMEM, SMEM, SMEM),
         scratch_shapes=[pltpu.SMEM((ranks,), jnp.int32), pltpu.SemaphoreType.DMA((PCAP,))],
         compiler_params=pltpu.CompilerParams(vmem_limit_bytes=62 * 1024 * 1024),
         name="prepare",
@@ -202,10 +214,11 @@
     def listed(s, place):
         return (note_ref[root_row_ref[s], TILES + place] != 0).astype(jnp.int32)
 
-    most = jnp.int32(0)
-    for device in range(note_ref.shape[0]):
-        most = jnp.maximum(most, note_ref[device, TILES + MT * KPT])
-    most_ref[0, 0] = most
+    for kind in range(2):
+        most = jnp.int32(0)
+        for device in range(note_ref.shape[0]):
+            most = jnp.maximum(most, note_ref[device, TILES + MT * KPT + kind])
+        most_ref[0, kind] = most
     for i in range(2 * PAIRS):
         panel_tile_ref[i] = 0
         v_tile_ref[i] = SECTIONS * KPT
@@ -243,7 +256,7 @@
             members,
             members,
             jax.ShapeDtypeStruct((MT * SECTIONS * KPT,), jnp.int32),
-            jax.ShapeDtypeStruct((1, 1), jnp.int32),
+            jax.ShapeDtypeStruct((1, 2), jnp.int32),
         ),
         in_specs=[SMEM, SMEM, SMEM],
         out_specs=(SMEM,) * 5,
@@ -358,28 +371,71 @@
     )(tiles, v)
 
 
-def spill_kernel(tile_ref, at_ref, v_mask_ref, mine_ref, got_ref, v_ref, out_ref):
+def spill_kernel(
+    tile_ref, goes_ref, at_ref, v_mask_ref, mine_ref, got_ref, v_ref, near_ref, far_ref, acc, panel_tiles, v_tiles
+):
+    terms = SECTIONS * KPT
     for e in range(SPILL):
-        tile = jnp.maximum(tile_ref[e], 0)
-        left = []
-        for i in range(SECTIONS * KPT):
-            panel_tile = at_ref[lax.rem(tile, MT) * (SECTIONS * KPT) + i]
-            counts = (panel_tile >= 0) & (v_mask_ref[i // KPT, i % KPT, tile // MT] != 0)
-            value = panel_at(jnp.maximum(panel_tile, 0), mine_ref, got_ref)
-            left.append(jnp.where(counts, value, jnp.zeros_like(value)))
-        product = jnp.dot(jnp.concatenate(left, axis=1), v_ref[e], preferred_element_type=jnp.float32)
-        out_ref[e] = product.astype(jnp.bfloat16)
-
-
-def spilled(mine, got, at, columns, v_mask, tiles):
+
+        @pl.when(tile_ref[e] >= 0)
+        def _(e=e):
+            tile, goes = tile_ref[e], goes_ref[e]
+            count = jnp.int32(0)
+            for i in range(terms):
+                panel_tile = at_ref[lax.rem(tile, MT) * terms + i]
+                counts = (panel_tile >= 0) & (v_mask_ref[i // KPT, i % KPT, tile // MT] != 0)
+
+                @pl.when(counts)
+                def _(i=i, count=count, panel_tile=panel_tile):
+                    panel_tiles[count] = panel_tile
+                    v_tiles[count] = i
+
+                count = count + counts.astype(jnp.int32)
+            acc[...] = jnp.zeros_like(acc)
+            for first in range(0, terms, SPILL_TERMS):
+
+                @pl.when(count > first)
+                def _(first=first):
+                    left, right = [], []
+                    for j in range(first, min(first + SPILL_TERMS, terms)):
+                        used = j < count
+                        value = panel_at(jnp.where(used, panel_tiles[j], 0), mine_ref, got_ref)
+                        left.append(jnp.where(used, value, jnp.zeros_like(value)))
+                        rows = pl.ds(pl.multiple_of(jnp.where(used, v_tiles[j], 0) * TILE, TILE), TILE)
+                        right.append(v_ref[e, rows, :])
+                    acc[...] += jnp.dot(
+                        jnp.concatenate(left, axis=1),
+                        jnp.concatenate(right, axis=0),
+                        preferred_element_type=jnp.float32,
+                    )
+
+            @pl.when(goes < SPILL)
+            def _():
+                near_ref[jnp.minimum(goes, SPILL - 1)] = acc[...].astype(jnp.bfloat16)
+
+            @pl.when((goes >= SPILL) & (goes < SPILL + far_ref.shape[0]))
+            def _():
+                far_ref[jnp.clip(goes - SPILL, 0, far_ref.shape[0] - 1)] = acc[...].astype(jnp.bfloat16)
+
+
+def spilled(far_each, mine, got, at, columns, v_mask, tiles, goes):
+    terms = SECTIONS * KPT
     return pl.pallas_call(
         spill_kernel,
-        out_shape=jax.ShapeDtypeStruct((SPILL, TILE, TILE), jnp.bfloat16),
-        in_specs=[SMEM] * 3 + [VMEM] * 3,
-        out_specs=VMEM,
+        out_shape=(
+            jax.ShapeDtypeStruct((SPILL, TILE, TILE), jnp.bfloat16),
+            jax.ShapeDtypeStruct((far_each, TILE, TILE), jnp.bfloat16),
+        ),
+        in_specs=[SMEM] * 4 + [VMEM] * 3,
+        out_specs=(VMEM, VMEM),
+        scratch_shapes=[
+            pltpu.VMEM((TILE, TILE), jnp.float32),
+            pltpu.SMEM((terms,), jnp.int32),
+            pltpu.SMEM((terms,), jnp.int32),
+        ],
         compiler_params=pltpu.CompilerParams(vmem_limit_bytes=24 * 1024 * 1024),
         name="spilled",
-    )(tiles, at, v_mask, mine, got, columns)
+    )(tiles, goes, at, v_mask, mine, got, columns)
 
 
 def begin_kernel(split, table_ref, near_ref, out_ref, zero, held, in_sem, out_sem):
@@ -521,7 +577,7 @@
     top = ranks // 2
     roots = section_owner
 
-    own, give, short_places, long_places, spill_tiles = prepare(
+    own, give, short_places, long_places, spill_tiles, spill_goes = prepare(
         t2_panels,
         me.reshape(1),
         t2_mask,
@@ -537,27 +593,30 @@
     columns = fetch_columns(v, spill_tiles)
 
     def digest(notes, xors):
-        notes = notes[:, : TILES + MT * KPT + 1].astype(jnp.int32)
+        notes = notes[:, : TILES + MT * KPT + 2].astype(jnp.int32)
         devices = me ^ jnp.asarray(xors, jnp.int32)
         order = jnp.arange(ranks, dtype=jnp.int32)
         root_rows = jnp.sum(jnp.where(devices[None, :] == roots[:, None], order, 0), axis=1)
         pairs, at, most = pair_up(me.reshape(1), root_rows, notes)
         return most, notes, devices, pairs, at, columns
 
-    mine, got, worst, (notes, devices, pairs, at, columns) = spread(own, give, me, roots, ranks, digest)
+    mine, got, worst, facts = spread(own, give, me, roots, ranks, digest)
+    notes, devices, pairs, at, columns = facts
     mine, got = mine.reshape(-1, TILE), got.reshape(-1, TILE)
 
     split = ranks * direct
 
-    def table_of(notes, short):
+    def table_of(notes, far_each):
         owners, keep = notes[:, :TILES] // 2, notes[:, :TILES] % 2 != 0
-        rank, kept_rank, spills, spill_place = ranks_of(owners, keep, direct)
         device = devices[:, None]
+        rank, kept_rank, spills, spill_place = ranks_of(owners, keep, ((owners ^ device) & top) != 0, direct)
         slot = jnp.arange(slots_each, dtype=jnp.int32)
-        if short:
-            far = ((device ^ me) & top) // top
-            spill_from = split + far * (top * SPILL) + (device & (top - 1)) * SPILL + spill_place
-            origin = jnp.where(spills, spill_from, device * direct + kept_rank)
+        if far_each:
+            member = device & (top - 1)
+            from_near = split + member * SPILL + spill_place
+            from_far = split + (top * SPILL) + member * far_each + spill_place
+            spilled_from = jnp.where(((device ^ me) & top) != 0, from_far, from_near)
+            origin = jnp.where(spills, spilled_from, device * direct + kept_rank)
         else:
             origin = device * slots_each + kept_rank
         arrives = ((owners == me) & keep)[:, None, :] & (rank[:, None, :] == slot[None, :, None])
@@ -567,29 +626,31 @@
 
     halves = [list(range(top)), list(range(top, ranks))]
 
-    def short(mine, got, v, v_rows, columns, notes, spill_tiles, places, _):
-        spill = spilled(mine, got, at, columns, v_mask, spill_tiles)
-        near_spill = lax.all_gather(spill, "row", axis=0, tiled=True, axis_index_groups=halves)
-        other = swap(spill, top, ranks)
+    def gathered(spill):
+        return lax.all_gather(spill, "row", axis=0, tiled=True, axis_index_groups=halves)
+
+    def short(far_each, mine, got, v, v_rows, columns, notes, spill_tiles, spill_goes, places, _):
+        near, far = spilled(far_each, mine, got, at, columns, v_mask, spill_tiles, spill_goes)
+        near_spill = gathered(near)
+        far = swap(far, top, ranks)
         tiles = ladder(mine, got, pairs, v, v_rows, places, split)
-        other, tiles, notes = lax.optimization_barrier((other, tiles, notes))
-        far_spill = lax.all_gather(other, "row", axis=0, tiled=True, axis_index_groups=halves)
-        table = table_of(notes, True)
+        far, tiles, notes = lax.optimization_barrier((far, tiles, notes))
+        far_spill = gathered(far)
+        table = table_of(notes, far_each)
         begun = begin_output(table, split, near_spill)
-        far_from = split + near_spill.shape[0]
-        return place_tiles(table, begun, exchange(tiles, ranks), far_from, far_spill)
-
-    def long(mine, got, v, v_rows, _, notes, __, ___, places):
+        return place_tiles(table, begun, exchange(tiles, ranks), split + top * SPILL, far_spill)
+
+    def long(mine, got, v, v_rows, _, notes, __, ___, ____, places):
         tiles = ladder(mine, got, pairs, v, v_rows, places, ranks * slots_each)
         unused = jnp.zeros((1, TILE, TILE), jnp.bfloat16)
-        table = table_of(notes, False)
+        table = table_of(notes, 0)
         begun = begin_output(table, ranks * slots_each, unused)
         return place_tiles(table, begun, exchange(tiles, ranks), ranks * slots_each + 1, unused)
 
-    delivered = lax.cond(
-        worst[0, 0] <= SPILL,
-        short,
-        long,
+    way = jnp.where(worst[0, 0] > SPILL, 2, (worst[0, 1] == SPILL).astype(jnp.int32))
+    delivered = lax.switch(
+        way,
+        [functools.partial(short, SPILL - 1), functools.partial(short, SPILL), long],
         mine,
         got,
         v,
@@ -597,6 +658,7 @@
         columns,
         notes,
         spill_tiles,
+        spill_goes,
         short_places,
         long_places,
     )

time: 201 us -> 198 us (0.985); the launches traced: 198 us -> 201 us
  waiting for transfers between devices: 121 us -> 118 us
  Pallas kernels: 33.8 us -> 36 us
    ppermute x15, waiting for transfers between devices: 32.1 us -> 30.1 us  [swap(): return lax.ppermute(x, 'row', [(i, i ^ bit) for i in range(ranks)])]
    pallas_call x1, Pallas kernels: 4.36 us -> 6.38 us  [place_tiles(): pl.pallas_call(functools.partial(place_kernel, direct.shape[0], far_from)...]
where the time goes in v4:
time: 198 us; the launch traced here: 201 us
  waiting for transfers between devices  118 us (60%)
  Pallas kernels  36 us (18%)
  starting transfers between devices  23 us (12%)
  between operations  14.9 us (8%)
  other arithmetic  4.32 us (2%)
  local copies, waits for them, and re-layouts  3.93 us (2%)
    all_gather x2, waiting for transfers between devices, gathered(): lax.all_gather(spill, 'row', axis=0, tiled=True, axis_index_groups=halves)  60.7 us
    ppermute x15, waiting for transfers between devices, swap(): return lax.ppermute(x, 'row', [(i, i ^ bit) for i in range(ranks)])  30.1 us
    all_to_all x1, waiting for transfers between devices, exchange(): lax.all_to_all(sent, 'row', split_axis=0, concat_axis=0, tiled=True)  24.1 us
    ppermute x15, starting transfers between devices, swap(): return lax.ppermute(x, 'row', [(i, i ^ bit) for i in range(ranks)])  13.9 us
    pallas_call x1, Pallas kernels, ladder(): pl.pallas_call(ladder_kernel, out_shape=jax.ShapeDtypeStruct((slots, TILE...  11.1 us
    all_to_all x1, starting transfers between devices, exchange(): lax.all_to_all(sent, 'row', split_axis=0, concat_axis=0, tiled=True)  8.09 us
    pallas_call x1, Pallas kernels, place_tiles(): pl.pallas_call(functools.partial(place_kernel, direct.shape[0], far_from)...  6.38 us
    pallas_call x1, Pallas kernels, begin_output(): pl.pallas_call(functools.partial(begin_kernel, split), out_shape=jax.Shap...  4.69 us
  transfers between devices with their start and end apart: 19, of which 15 were waited for; matrix products, arithmetic and copies ran while one was open for 3% of the time, Pallas kernels for 11%

profile of v4, /device:TPU:16, one launch (start us, length us, event | category | flops | bytes accessed | tf_op | source)
XLA Modules:
  0.0 201.0 jit_solution(5677861490868694663)
XLA Ops:
  6.5 3.5 %prepare.1 = (bf16[1280,256]{1,0:T(8,128)(2,1)}, bf16[1296,256]{1,0:T(8,128)(2,1)}, s32[32]{0:T(128)S(1)}, s32[32]{0:T(128)S(1)}, s32[3]{0:T(128)S(1)}, /*index=5*/s32[3]{0:T(128)S(1)}) custom-call(s32[1]{0:T(128)} %bitcast.9.me_ref, s32[1,4,5]{2,1,0:T(4,128)} %mask_ref.1, s32[4,8]{1,0:T(4,128)} %bitcast.41, s32[4,8]{1,0:T(4,128)} %keep_ref.1, ...), custom_call_target="tpu_custom_call" | custom-call | tf_op jit(solution)/shard_map/prepare/pallas_call | solution.py:195
  10.8 1.6 collective-permute-done.2
  12.5 1.3 broadcast_select_fusion
  13.8 1.6 collective-permute-start.7
  15.5 1.6 collective-permute-start.3
  17.1 4.6 %fetch_columns.1 = bf16[3,2560,256]{2,1,0:T(8,128)(2,1)} custom-call(s32[3]{0:T(128)S(1)} %get-tuple-element.177.tile_ref, bf16[2560,2048]{1,0:T(8,128)(2,1)} %bitcast.27), custom_call_target="tpu_custom_call" | custom-call | bytes 8388608 | tf_op jit(solution)/shard_map/fetch_columns/pallas_call | solution.py:362
  22.3 2.9 %collective-permute-done.3 = bf16[642,256]{1,0:T(8,128)(2,1)S(1)} collective-permute-done((bf16[642,256]{1,0:T(8,128)(2,1)S(1)}, bf16[642,256]{1,0:T(8,128)(2,1)S(1)}, u32[]{:S(2)}, u32[]{:S(2)}) %collective-permute-start.3) | collective-permute-done | bytes 328736 | tf_op jit(solution)/shard_map/ppermute | solution.py:29
  25.4 1.6 collective-permute-start.8
  27.6 3.1 %collective-permute-done.8 = bf16[2,160,256]{2,1,0:T(8,128)(2,1)S(1)} collective-permute-done((bf16[2,160,256]{2,1,0:T(8,128)(2,1)S(1)}, bf16[2,160,256]{2,1,0:T(8,128)(2,1)S(1)}, u32[]{:S(2)}, u32[]{:S(2)}) %collective-permute-start.8) | collective-permute-done | bytes 163872 | tf_op jit(solution)/shard_map/ppermute | solution.py:29
  31.3 3.1 %collective-permute-done.5 = bf16[326,256]{1,0:T(8,128)(2,1)S(1)} collective-permute-done((bf16[326,256]{1,0:T(8,128)(2,1)S(1)}, bf16[326,256]{1,0:T(8,128)(2,1)S(1)}, u32[]{:S(2)}, u32[]{:S(2)}) %collective-permute-start.5) | collective-permute-done | bytes 166944 | tf_op jit(solution)/shard_map/ppermute | solution.py:29
  35.6 2.4 %collective-permute-done.10 = bf16[4,256]{1,0:T(4,128)(2,1)S(1)} collective-permute-done((bf16[4,256]{1,0:T(4,128)(2,1)S(1)}, bf16[4,256]{1,0:T(4,128)(2,1)S(1)}, u32[]{:S(2)}, u32[]{:S(2)}) %collective-permute-start.10) | collective-permute-done | bytes 2080 | tf_op jit(solution)/shard_map/ppermute | solution.py:29
  38.2 1.9 pair_up.1
  40.0 1.0 collective-permute-start.11
  41.1 2.6 %collective-permute-done.11 = s32[1,2]{1,0:T(1,128)S(1)} collective-permute-done((s32[1,2]{1,0:T(1,128)S(1)}, s32[1,2]{1,0:T(1,128)S(1)}, u32[]{:S(2)}, u32[]{:S(2)}) %collective-permute-start.11) | collective-permute-done | bytes 40 | tf_op jit(solution)/shard_map/ppermute | solution.py:68
  43.8 3.2 %collective-permute-start.12 = (bf16[2,160,256]{2,1,0:T(8,128)(2,1)S(1)}, bf16[2,160,256]{2,1,0:T(8,128)(2,1)S(1)}, u32[]{:S(2)}, u32[]{:S(2)}) collective-permute-start(bf16[2,160,256]{2,1,0:T(8,128)(2,1)S(1)} %get-tuple-element.182), channel_id=1, source_target_pairs={{0,4},{1,5},{2,6},{3,7},{4,0},{5,1},{6,2},{7,3},{8,12},{9,13},{10,... | collective-permute-start | bytes 491528 | tf_op jit(solution)/shard_map/ppermute | solution.py:29
  47.0 1.5 collective-permute-start.14
  48.4 1.8 collective-permute-done.12
  50.4 1.5 collective-permute-start.13
  51.9 1.9 collective-permute-done.14
  54.1 5.3 %collective-permute-done.13 = bf16[2,320,256]{2,1,0:T(8,128)(2,1)S(1)} collective-permute-done((bf16[2,320,256]{2,1,0:T(8,128)(2,1)S(1)}, bf16[2,320,256]{2,1,0:T(8,128)(2,1)S(1)}, u32[]{:S(2)}, u32[]{:S(2)}) %collective-permute-start.13) | collective-permute-done | bytes 327712 | tf_op jit(solution)/shard_map/ppermute | solution.py:29
  59.5 1.5 collective-permute-done.15
  63.3 1.0 collective-permute-done.16
  64.3 129.8 %conditional.1 = (bf16[16,4,256,256]{3,2,1,0:T(8,128)(2,1)}) conditional(s32[]{:T(128)} %bitcast.17, (s32[16]{0:T(128)S(1)}, s32[3]{0:T(128)S(1)}, s32[3]{0:T(128)S(1)}, s32[40]{0:T(128)S(1)}, s32[2,5,8]{2,0,1:T(2,128)S(1)}, /*index=5*/bf16[2560,256]{1,0:T(8,128)(2,1)S(1)}, bf16[2560,256]{1,0:T(8,128)(2,1)S(1)}, ...), branch_computations={%region_1.7_spmd, %region_7.13_spmd, %region_13.18_spmd} | conditional | flops 12885126144 | bytes 70645992 | solution.py:651
  64.3 3.8 %spilled.3 = (bf16[3,256,256]{2,1,0:T(8,128)(2,1)}, bf16[3,256,256]{2,1,0:T(8,128)(2,1)S(1)}) custom-call(s32[3]{0:T(128)S(1)} %get-tuple-element.118.tile_ref, s32[3]{0:T(128)S(1)} %get-tuple-element.119.goes_ref, s32[40]{0:T(128)S(1)} %get-tuple-element.120.at_ref, s32[2,5,8]{2,1,0:T(8,128)S(1)} %copy.40.v_mask_ref, ...), custom_call_target="tpu_custom_call" | custom-call | tf_op jit(solution)/shard_map/cond/branch_1_fun/spilled/pallas_call | solution.py:423
  69.0 11.1 %ladder.4 = bf16[32,256,256]{2,1,0:T(8,128)(2,1)} custom-call(s32[12]{0:T(128)S(1)} %get-tuple-element.126.row_ref, s32[24]{0:T(128)S(1)} %get-tuple-element.127.panel_tile_ref, s32[24]{0:T(128)S(1)} %get-tuple-element.128.v_tile_ref, s32[32]{0:T(128)S(1)} %get-tuple-element.129.place_ref, bf16[2560,256]{1,0:T(8,128)(2,1)S(1)} %get-tuple-element.122.mine_ref, ...), custom_call_target="tpu_custom_call" | custom-call | flops 12884901888 | bytes 25165824 | tf_op jit(solution)/shard_map/cond/branch_1_fun/ladder/pallas_call | solution.py:321
  80.1 5.5 %collective-permute-done.1 = bf16[3,256,256]{2,1,0:T(8,128)(2,1)S(1)} collective-permute-done((bf16[3,256,256]{2,1,0:T(8,128)(2,1)S(1)}, bf16[3,256,256]{2,1,0:T(8,128)(2,1)S(1)}, u32[]{:S(2)}, u32[]{:S(2)}) %collective-permute-start.1) | collective-permute-done | bytes 393248 | tf_op jit(solution)/shard_map/cond/branch_1_fun/ppermute | solution.py:29
  86.4 8.1 %all-to-all-start.1 = ((bf16[16,2,256,256]{3,2,1,0:T(8,128)(2,1)}), bf16[16,2,256,256]{3,2,1,0:T(8,128)(2,1)}, u32[]{:S(2)}, u32[]{:S(2)}) async-start(bf16[16,2,256,256]{3,2,1,0:T(8,128)(2,1)} %bitcast.36), calls=%async_computation.1 | async-start | bytes 8388608 | tf_op jit(solution)/shard_map/cond/branch_1_fun/all_to_all | solution.py:567
  97.7 3.3 %all-gather.9.cloned.1.call-done.near_ref = bf16[24,256,256]{2,1,0:T(8,128)(2,1)} async-done(((bf16[3,256,256]{2,1,0:T(8,128)(2,1)}), bf16[24,256,256]{2,1,0:T(8,128)(2,1)}) %all-gather.9.cloned.1.call-update) | async-done | bytes 3145744 | tf_op jit(solution)/shard_map/cond/branch_1_fun/all_gather | solution.py:630
  101.0 4.7 %begin_output.4.begun_ref = bf16[64,256,256]{2,1,0:T(8,128)(2,1)} custom-call(s32[64]{0:T(128)} %sub.25.table_ref, bf16[24,256,256]{2,1,0:T(8,128)(2,1)} %all-gather.9.cloned.1.call-done.near_ref), custom_call_target="tpu_custom_call" | custom-call | bytes 8388608 | tf_op jit(solution)/shard_map/cond/branch_1_fun/begin_output/pallas_call | solution.py:484
  105.7 57.4 %all-gather.11.cloned.1.call-done.far_ref = bf16[24,256,256]{2,1,0:T(8,128)(2,1)} async-done(((bf16[3,256,256]{2,1,0:T(8,128)(2,1)}), bf16[24,256,256]{2,1,0:T(8,128)(2,1)}) %all-gather.11.cloned.1.call-update) | async-done | bytes 3145744 | tf_op jit(solution)/shard_map/cond/branch_1_fun/all_gather | solution.py:630
  163.2 24.1 %all-to-all-done.1 = bf16[16,2,256,256]{3,2,1,0:T(8,128)(2,1)} async-done(((bf16[16,2,256,256]{3,2,1,0:T(8,128)(2,1)}), bf16[16,2,256,256]{3,2,1,0:T(8,128)(2,1)}, u32[]{:S(2)}, u32[]{:S(2)}) %all-to-all-start.1) | async-done | bytes 4194336 | tf_op jit(solution)/shard_map/cond/branch_1_fun/all_to_all | solution.py:567
  187.2 6.4 %place_tiles.4 = bf16[64,256,256]{2,1,0:T(8,128)(2,1)} custom-call(s32[64]{0:T(128)} %sub.25.table_ref, bf16[64,256,256]{2,1,0:T(8,128)(2,1)} %begin_output.4.begun_ref, bf16[32,256,256]{2,1,0:T(8,128)(2,1)} %bitcast.4.direct_ref, bf16[24,256,256]{2,1,0:T(8,128)(2,1)} %all-gather.11.cloned.1.call-done.far_ref), custom_call_target="tpu_custom_call", output_to_operand_aliasing={{}: (1, {})} | custom-call | tf_op jit(solution)/shard_map/cond/branch_1_fun/place_tiles/pallas_call | solution.py:548
  (82 shorter events, 10.6 us)
Async XLA Ops:
  6.5 4.3 %copy-start.3 = (s32[2]{0:T(128)S(1)}, s32[2]{0:T(128)}, u32[]{:S(2)}) copy-start(s32[2]{0:T(128)} %param.17) | copy-start | bytes 28
  10.0 2.4 %collective-permute-start.2 = (bf16[1296,256]{1,0:T(8,128)(2,1)}, bf16[1296,256]{1,0:T(8,128)(2,1)S(1)}, u32[]{:S(2)}, u32[]{:S(2)}) collective-permute-start(bf16[1296,256]{1,0:T(8,128)(2,1)} %get-tuple-element.171), channel_id=1, source_target_pairs={{0,1},{1,0},{2,3},{3,2},{4,5},{5,4},{6,7},{7,6},{8,9},{9,8},{10,11... | collective-permute-start | bytes 1990664 | tf_op jit(solution)/shard_map/ppermute | solution.py:29
  12.4 4.6 %copy-start.4 = (s32[16]{0:T(128)S(1)}, s32[16]{0:T(128)}, u32[]{:S(2)}) copy-start(s32[16]{0:T(128)} %constant.145.clone) | copy-start | bytes 196
  13.8 11.3 %collective-permute-start.7 = (bf16[2,320,256]{2,1,0:T(8,128)(2,1)S(1)}, bf16[2,320,256]{2,1,0:T(8,128)(2,1)S(1)}, u32[]{:S(2)}, u32[]{:S(2)}) collective-permute-start(bf16[2,320,256]{2,1,0:T(8,128)(2,1)S(1)} %get-tuple-element.378), channel_id=1, source_target_pairs={{0,4},{1,5},{2,6},{3,7},{4,0},{5,1},{6,2},{7,3},{8,12},{9,13},{10,... | collective-permute-start | bytes 983048 | tf_op jit(solution)/shard_map/ppermute | solution.py:29
  15.5 9.6 %collective-permute-start.3 = (bf16[642,256]{1,0:T(8,128)(2,1)S(1)}, bf16[642,256]{1,0:T(8,128)(2,1)S(1)}, u32[]{:S(2)}, u32[]{:S(2)}) collective-permute-start(bf16[642,256]{1,0:T(8,128)(2,1)S(1)} %pad_maximum_fusion.1), channel_id=1, source_target_pairs={{0,2},{1,3},{2,0},{3,1},{4,6},{5,7},{6,4},{7,5},{8,10},{9,11},{10,... | collective-permute-start | bytes 986120 | tf_op jit(solution)/shard_map/ppermute | solution.py:29
  21.9 5.1 %collective-permute-start.4 = (bf16[2,256]{1,0:T(2,128)(2,1)S(1)}, bf16[2,256]{1,0:T(2,128)(2,1)S(1)}, u32[]{:S(2)}, u32[]{:S(2)}) collective-permute-start(bf16[2,256]{1,0:T(2,128)(2,1)S(1)} %pad_maximum_fusion.5), channel_id=1, source_target_pairs={{0,8},{1,9},{2,10},{3,11},{4,12},{5,13},{6,14},{7,15},{8,0},{9,1},... | collective-permute-start | bytes 3080 | tf_op jit(solution)/shard_map/ppermute | solution.py:29
  25.4 5.4 %collective-permute-start.8 = (bf16[2,160,256]{2,1,0:T(8,128)(2,1)S(1)}, bf16[2,160,256]{2,1,0:T(8,128)(2,1)S(1)}, u32[]{:S(2)}, u32[]{:S(2)}) collective-permute-start(bf16[2,160,256]{2,1,0:T(8,128)(2,1)S(1)} %broadcast_select_fusion.11), channel_id=1, source_target_pairs={{0,2},{1,3},{2,0},{3,1},{4,6},{5,7},{6,4},{7,5},{8,10},{9,11},{10,... | collective-permute-start | bytes 491528 | tf_op jit(solution)/shard_map/ppermute | solution.py:29
  27.1 7.2 %collective-permute-start.5 = (bf16[326,256]{1,0:T(8,128)(2,1)S(1)}, bf16[326,256]{1,0:T(8,128)(2,1)S(1)}, u32[]{:S(2)}, u32[]{:S(2)}) collective-permute-start(bf16[326,256]{1,0:T(8,128)(2,1)S(1)} %concatenate.32), channel_id=1, source_target_pairs={{0,4},{1,5},{2,6},{3,7},{4,0},{5,1},{6,2},{7,3},{8,12},{9,13},{10,... | collective-permute-start | bytes 500744 | tf_op jit(solution)/shard_map/ppermute | solution.py:29
  30.9 12.8 %collective-permute-start.9 = (bf16[2,160,256]{2,1,0:T(8,128)(2,1)S(1)}, bf16[2,160,256]{2,1,0:T(8,128)(2,1)S(1)}, u32[]{:S(2)}, u32[]{:S(2)}) collective-permute-start(bf16[2,160,256]{2,1,0:T(8,128)(2,1)S(1)} %select_select_fusion.2), channel_id=1, source_target_pairs={{0,8},{1,9},{2,10},{3,11},{4,12},{5,13},{6,14},{7,15},{8,0},{9,1},... | collective-permute-start | bytes 491528 | tf_op jit(solution)/shard_map/ppermute | solution.py:29
  34.4 3.6 %collective-permute-start.10 = (bf16[4,256]{1,0:T(4,128)(2,1)S(1)}, bf16[4,256]{1,0:T(4,128)(2,1)S(1)}, u32[]{:S(2)}, u32[]{:S(2)}) collective-permute-start(bf16[4,256]{1,0:T(4,128)(2,1)S(1)} %pad_maximum_fusion.4), channel_id=1, source_target_pairs={{0,2},{1,3},{2,0},{3,1},{4,6},{5,7},{6,4},{7,5},{8,10},{9,11},{10,... | collective-permute-start | bytes 6152 | tf_op jit(solution)/shard_map/ppermute | solution.py:29
  34.8 8.9 %collective-permute-start.6 = (bf16[2,160,256]{2,1,0:T(8,128)(2,1)S(1)}, bf16[2,160,256]{2,1,0:T(8,128)(2,1)S(1)}, u32[]{:S(2)}, u32[]{:S(2)}) collective-permute-start(bf16[2,160,256]{2,1,0:T(8,128)(2,1)S(1)} %select_select_fusion.3), channel_id=1, source_target_pairs={{0,8},{1,9},{2,10},{3,11},{4,12},{5,13},{6,14},{7,15},{8,0},{9,1},... | collective-permute-start | bytes 491528 | tf_op jit(solution)/shard_map/ppermute | solution.py:29
  40.0 3.6 %collective-permute-start.11 = (s32[1,2]{1,0:T(1,128)S(1)}, s32[1,2]{1,0:T(1,128)S(1)}, u32[]{:S(2)}, u32[]{:S(2)}) collective-permute-start(s32[1,2]{1,0:T(1,128)S(1)} %get-tuple-element.172), channel_id=1, source_target_pairs={{0,16},{16,0},{1,17},{17,1},{2,18},{18,2},{3,19},{19,3},{4,20},{20... | collective-permute-start | bytes 32 | tf_op jit(solution)/shard_map/ppermute | solution.py:68
  43.8 6.5 %collective-permute-start.12 = (bf16[2,160,256]{2,1,0:T(8,128)(2,1)S(1)}, bf16[2,160,256]{2,1,0:T(8,128)(2,1)S(1)}, u32[]{:S(2)}, u32[]{:S(2)}) collective-permute-start(bf16[2,160,256]{2,1,0:T(8,128)(2,1)S(1)} %get-tuple-element.182), channel_id=1, source_target_pairs={{0,4},{1,5},{2,6},{3,7},{4,0},{5,1},{6,2},{7,3},{8,12},{9,13},{10,... | collective-permute-start | bytes 491528 | tf_op jit(solution)/shard_map/ppermute | solution.py:29
  47.0 6.8 %collective-permute-start.14 = (bf16[2,160,256]{2,1,0:T(8,128)(2,1)S(1)}, bf16[2,160,256]{2,1,0:T(8,128)(2,1)S(1)}, u32[]{:S(2)}, u32[]{:S(2)}) collective-permute-start(bf16[2,160,256]{2,1,0:T(8,128)(2,1)S(1)} %get-tuple-element.183), channel_id=1, source_target_pairs={{0,2},{1,3},{2,0},{3,1},{4,6},{5,7},{6,4},{7,5},{8,10},{9,11},{10,... | collective-permute-start | bytes 491528 | tf_op jit(solution)/shard_map/ppermute | solution.py:29
  50.4 9.0 %collective-permute-start.13 = (bf16[2,320,256]{2,1,0:T(8,128)(2,1)S(1)}, bf16[2,320,256]{2,1,0:T(8,128)(2,1)S(1)}, u32[]{:S(2)}, u32[]{:S(2)}) collective-permute-start(bf16[2,320,256]{2,1,0:T(8,128)(2,1)S(1)} %pad_maximum_fusion.2), channel_id=1, source_target_pairs={{0,2},{1,3},{2,0},{3,1},{4,6},{5,7},{6,4},{7,5},{8,10},{9,11},{10,... | collective-permute-start | bytes 983048 | tf_op jit(solution)/shard_map/ppermute | solution.py:29
  53.8 7.5 %copy-start.2 = (s32[2,5,8]{2,0,1:T(2,128)S(1)}, s32[2,5,8]{2,0,1:T(2,128)}, u32[]{:S(2)}) copy-start(s32[2,5,8]{2,0,1:T(2,128)} %param.14) | copy-start | bytes 964
  53.8 7.1 %collective-permute-start.15 = (bf16[2,320,256]{2,1,0:T(8,128)(2,1)S(1)}, bf16[2,320,256]{2,1,0:T(8,128)(2,1)S(1)}, u32[]{:S(2)}, u32[]{:S(2)}) collective-permute-start(bf16[2,320,256]{2,1,0:T(8,128)(2,1)S(1)} %pad_maximum_fusion.3), channel_id=1, source_target_pairs={{0,4},{1,5},{2,6},{3,7},{4,0},{5,1},{6,2},{7,3},{8,12},{9,13},{10,... | collective-permute-start | bytes 983048 | tf_op jit(solution)/shard_map/ppermute | solution.py:29
  61.2 3.1 %collective-permute-start.16 = (bf16[2,1280,256]{2,1,0:T(8,128)(2,1)S(1)}, bf16[2,1280,256]{2,1,0:T(8,128)(2,1)S(1)}, u32[]{:S(2)}, u32[]{:S(2)}) collective-permute-start(bf16[2,1280,256]{2,1,0:T(8,128)(2,1)S(1)} %pad_maximum_fusion), channel_id=1, source_target_pairs={{0,1},{1,0},{2,3},{3,2},{4,5},{5,4},{6,7},{7,6},{8,9},{9,8},{10,11... | collective-permute-start | bytes 3932168 | tf_op jit(solution)/shard_map/ppermute | solution.py:29
  64.3 36.8 %all-gather.9.cloned.1.call-start = ((), (), s32[]{:S(2)}) async-start(), calls=%async_computation.5 | async-start | bytes 3538944 | tf_op jit(solution)/shard_map/cond/branch_1_fun/all_gather | solution.py:630
  68.2 17.5 %collective-permute-start.1 = (bf16[3,256,256]{2,1,0:T(8,128)(2,1)S(1)}, bf16[3,256,256]{2,1,0:T(8,128)(2,1)S(1)}, u32[]{:S(2)}, u32[]{:S(2)}) collective-permute-start(bf16[3,256,256]{2,1,0:T(8,128)(2,1)S(1)} %get-tuple-element.125), channel_id=1, source_target_pairs={{0,8},{1,9},{2,10},{3,11},{4,12},{5,13},{6,14},{7,15},{8,0},{9,1},... | collective-permute-start | bytes 1179656 | tf_op jit(solution)/shard_map/cond/branch_1_fun/ppermute | solution.py:29
  85.7 0.7 copy-start
  86.4 100.8 %all-to-all-start.1 = ((bf16[16,2,256,256]{3,2,1,0:T(8,128)(2,1)}), bf16[16,2,256,256]{3,2,1,0:T(8,128)(2,1)}, u32[]{:S(2)}, u32[]{:S(2)}) async-start(bf16[16,2,256,256]{3,2,1,0:T(8,128)(2,1)} %bitcast.36), calls=%async_computation.1 | async-start | bytes 8388608 | tf_op jit(solution)/shard_map/cond/branch_1_fun/all_to_all | solution.py:567
  94.5 68.6 %all-gather.11.cloned.1.call-start = ((), (), s32[]{:S(2)}) async-start(), calls=%async_computation.6 | async-start | bytes 3538944 | tf_op jit(solution)/shard_map/cond/branch_1_fun/all_gather | solution.py:630
Sparse Core Ops, SparseCore 0:
  68.3 32.7 all-gather.8
  102.7 60.4 all-gather.10

commit v5 on v4

--- a/solution.py
+++ b/solution.py
@@ -272,25 +272,32 @@
     return jnp.where(panel_tile % 2 == 0, mine_ref[rows, :], got_ref[rows, :])
 
 
-def pair_product(pair, panel_tile_ref, v_tile_ref, mine_ref, got_ref, v_ref, mask_ref):
+def pair_product(pair, panel_tile_ref, v_tile_ref, mine_ref, got_ref, v_ref, v_mask_ref, first_column):
     left, right = [], []
+    tile_of = lax.broadcasted_iota(jnp.int32, (1, STEP_COLS), 1) // TILE
     for i in (2 * pair, 2 * pair + 1):
         v_tile = v_tile_ref[i]
         left.append(panel_at(panel_tile_ref[i], mine_ref, got_ref))
         v_row = jnp.minimum(v_tile, SECTIONS * KPT - 1)
-        right.append(v_ref[pl.ds(pl.multiple_of(v_row * TILE, TILE), TILE), :] * mask_ref[v_tile])
+        mask = jnp.zeros((1, STEP_COLS), jnp.float32)
+        for j in range(STEP_TILES):
+            kept = (v_mask_ref[v_row // KPT, lax.rem(v_row, KPT), first_column + j] != 0) & (v_row == v_tile)
+            mask = jnp.where(tile_of == j, kept.astype(jnp.float32), mask)
+        right.append(v_ref[pl.ds(pl.multiple_of(v_row * TILE, TILE), TILE), :] * mask.astype(jnp.bfloat16))
     return jnp.dot(
         jnp.concatenate(left, axis=1), jnp.concatenate(right, axis=0), preferred_element_type=jnp.float32
     )
 
 
 def ladder_kernel(
-    row_ref, panel_tile_ref, v_tile_ref, place_ref, mine_ref, got_ref, v_ref, mask_ref, out_ref, acc, staged, sem
+    row_ref, panel_tile_ref, v_tile_ref, place_ref, v_mask_ref, mine_ref, got_ref, v_ref, out_ref, acc, staged, sem
 ):
     step = pl.program_id(0)
     acc[...] = jnp.zeros_like(acc)
     for pair in range(PAIRS):
-        acc[row_ref[pair]] += pair_product(pair, panel_tile_ref, v_tile_ref, mine_ref, got_ref, v_ref, mask_ref)
+        acc[row_ref[pair]] += pair_product(
+            pair, panel_tile_ref, v_tile_ref, mine_ref, got_ref, v_ref, v_mask_ref, step * STEP_TILES
+        )
 
     def copy_to(q, place):
         return pltpu.make_async_copy(staged.at[q], out_ref.at[place], sem.at[q])
@@ -316,7 +323,7 @@
         lax.fori_loop(0, TILES, finish, 0)
 
 
-def ladder(mine, got, pairs, v, v_rows, places, slots):
+def ladder(mine, got, pairs, v, v_mask, places, slots):
     macs = 2 * PAIRS * TILE * TILE * NT_DEV * TILE
     return pl.pallas_call(
         ladder_kernel,
@@ -327,10 +334,10 @@
             SMEM,
             SMEM,
             SMEM,
+            SMEM,
             VMEM,
             VMEM,
             pl.BlockSpec((SECTIONS * KPT * TILE, STEP_COLS), lambda j: (0, j)),
-            pl.BlockSpec((SECTIONS * KPT + 1, 1, STEP_COLS), lambda j: (0, 0, j)),
         ],
         out_specs=HBM,
         scratch_shapes=[
@@ -341,7 +348,7 @@
         compiler_params=pltpu.CompilerParams(vmem_limit_bytes=55 * 1024 * 1024),
         cost_estimate=pl.CostEstimate(flops=4 * macs, bytes_accessed=24 * 1024 * 1024, transcendentals=0),
         name="ladder",
-    )(*pairs, places, mine, got, v, v_rows)
+    )(*pairs, places, v_mask, mine, got, v)
 
 
 def column_of(tile):
@@ -375,47 +382,48 @@
     tile_ref, goes_ref, at_ref, v_mask_ref, mine_ref, got_ref, v_ref, near_ref, far_ref, acc, panel_tiles, v_tiles
 ):
     terms = SECTIONS * KPT
+    counts = []
     for e in range(SPILL):
-
-        @pl.when(tile_ref[e] >= 0)
-        def _(e=e):
-            tile, goes = tile_ref[e], goes_ref[e]
-            count = jnp.int32(0)
-            for i in range(terms):
-                panel_tile = at_ref[lax.rem(tile, MT) * terms + i]
-                counts = (panel_tile >= 0) & (v_mask_ref[i // KPT, i % KPT, tile // MT] != 0)
-
-                @pl.when(counts)
-                def _(i=i, count=count, panel_tile=panel_tile):
-                    panel_tiles[count] = panel_tile
-                    v_tiles[count] = i
-
-                count = count + counts.astype(jnp.int32)
-            acc[...] = jnp.zeros_like(acc)
-            for first in range(0, terms, SPILL_TERMS):
-
-                @pl.when(count > first)
-                def _(first=first):
-                    left, right = [], []
-                    for j in range(first, min(first + SPILL_TERMS, terms)):
-                        used = j < count
-                        value = panel_at(jnp.where(used, panel_tiles[j], 0), mine_ref, got_ref)
-                        left.append(jnp.where(used, value, jnp.zeros_like(value)))
-                        rows = pl.ds(pl.multiple_of(jnp.where(used, v_tiles[j], 0) * TILE, TILE), TILE)
-                        right.append(v_ref[e, rows, :])
-                    acc[...] += jnp.dot(
-                        jnp.concatenate(left, axis=1),
-                        jnp.concatenate(right, axis=0),
-                        preferred_element_type=jnp.float32,
-                    )
-
-            @pl.when(goes < SPILL)
-            def _():
-                near_ref[jnp.minimum(goes, SPILL - 1)] = acc[...].astype(jnp.bfloat16)
-
-            @pl.when((goes >= SPILL) & (goes < SPILL + far_ref.shape[0]))
-            def _():
-                far_ref[jnp.clip(goes - SPILL, 0, far_ref.shape[0] - 1)] = acc[...].astype(jnp.bfloat16)
+        tile = jnp.maximum(tile_ref[e], 0)
+        count = jnp.int32(0)
+        for i in range(terms):
+            panel_tile = at_ref[lax.rem(tile, MT) * terms + i]
+            panel_tiles[e * (terms + 1) + count] = panel_tile
+            v_tiles[e * (terms + 1) + count] = i
+            counted = (panel_tile >= 0) & (v_mask_ref[i // KPT, i % KPT, tile // MT] != 0)
+            count = count + counted.astype(jnp.int32)
+        counts.append(count)
+
+    def product(e, first):
+        left, right = [], []
+        for j in range(first, min(first + SPILL_TERMS, terms)):
+            used = j < counts[e]
+            value = panel_at(jnp.where(used, panel_tiles[e * (terms + 1) + j], 0), mine_ref, got_ref)
+            left.append(jnp.where(used, value, jnp.zeros_like(value)))
+            v_row = jnp.where(used, v_tiles[e * (terms + 1) + j], 0)
+            right.append(v_ref[e, pl.ds(pl.multiple_of(v_row * TILE, TILE), TILE), :])
+        return jnp.dot(
+            jnp.concatenate(left, axis=1), jnp.concatenate(right, axis=0), preferred_element_type=jnp.float32
+        )
+
+    for e in range(SPILL):
+        acc[e] = product(e, 0)
+    for e in range(SPILL):
+        for first in range(SPILL_TERMS, terms, SPILL_TERMS):
+
+            @pl.when((counts[e] > first) & (tile_ref[e] >= 0))
+            def _(e=e, first=first):
+                acc[e] += product(e, first)
+
+        goes = goes_ref[e]
+
+        @pl.when((goes >= 0) & (goes < SPILL))
+        def _(e=e, goes=goes):
+            near_ref[jnp.clip(goes, 0, SPILL - 1)] = acc[e].astype(jnp.bfloat16)
+
+        @pl.when((goes >= SPILL) & (goes < SPILL + far_ref.shape[0]))
+        def _(e=e, goes=goes):
+            far_ref[jnp.clip(goes - SPILL, 0, far_ref.shape[0] - 1)] = acc[e].astype(jnp.bfloat16)
 
 
 def spilled(far_each, mine, got, at, columns, v_mask, tiles, goes):
@@ -429,9 +437,9 @@
         in_specs=[SMEM] * 4 + [VMEM] * 3,
         out_specs=(VMEM, VMEM),
         scratch_shapes=[
-            pltpu.VMEM((TILE, TILE), jnp.float32),
-            pltpu.SMEM((terms,), jnp.int32),
-            pltpu.SMEM((terms,), jnp.int32),
+            pltpu.VMEM((SPILL, TILE, TILE), jnp.float32),
+            pltpu.SMEM((SPILL * (terms + 1),), jnp.int32),
+            pltpu.SMEM((SPILL * (terms + 1),), jnp.int32),
         ],
         compiler_params=pltpu.CompilerParams(vmem_limit_bytes=24 * 1024 * 1024),
         name="spilled",
@@ -588,8 +596,6 @@
         direct,
     )
     v = v_blocks.reshape(SECTIONS * KPT * TILE, NT_DEV * TILE)
-    v_rows = jnp.repeat(v_mask.reshape(SECTIONS * KPT, 1, NT_DEV).astype(jnp.bfloat16), TILE, axis=2)
-    v_rows = jnp.pad(v_rows, ((0, 1), (0, 0), (0, 0)))
     columns = fetch_columns(v, spill_tiles)
 
     def digest(notes, xors):
@@ -629,19 +635,19 @@
     def gathered(spill):
         return lax.all_gather(spill, "row", axis=0, tiled=True, axis_index_groups=halves)
 
-    def short(far_each, mine, got, v, v_rows, columns, notes, spill_tiles, spill_goes, places, _):
+    def short(far_each, mine, got, v, v_mask, columns, notes, spill_tiles, spill_goes, places, _):
         near, far = spilled(far_each, mine, got, at, columns, v_mask, spill_tiles, spill_goes)
         near_spill = gathered(near)
         far = swap(far, top, ranks)
-        tiles = ladder(mine, got, pairs, v, v_rows, places, split)
+        tiles = ladder(mine, got, pairs, v, v_mask, places, split)
         far, tiles, notes = lax.optimization_barrier((far, tiles, notes))
         far_spill = gathered(far)
         table = table_of(notes, far_each)
         begun = begin_output(table, split, near_spill)
         return place_tiles(table, begun, exchange(tiles, ranks), split + top * SPILL, far_spill)
 
-    def long(mine, got, v, v_rows, _, notes, __, ___, ____, places):
-        tiles = ladder(mine, got, pairs, v, v_rows, places, ranks * slots_each)
+    def long(mine, got, v, v_mask, _, notes, __, ___, ____, places):
+        tiles = ladder(mine, got, pairs, v, v_mask, places, ranks * slots_each)
         unused = jnp.zeros((1, TILE, TILE), jnp.bfloat16)
         table = table_of(notes, 0)
         begun = begin_output(table, ranks * slots_each, unused)
@@ -654,7 +660,7 @@
         mine,
         got,
         v,
-        v_rows,
+        v_mask,
         columns,
         notes,
         spill_tiles,

time: 198 us -> 201 us (1.015); the launches traced: 201 us -> 201 us
  transfers between devices with their start and end apart: 19 -> 19, of which waited for: 15 -> 15; matrix products, arithmetic and copies ran while one was open for 3% -> 2% of each run, Pallas kernels for 11% -> 11%
where the time goes in v5:
time: 201 us
  waiting for transfers between devices  118 us (59%)
  Pallas kernels  36.3 us (18%)
  starting transfers between devices  23.5 us (12%)
  between operations  14.9 us (7%)
  other arithmetic  4.25 us (2%)
  local copies, waits for them, and re-layouts  3.08 us (2%)
    all_gather x2, waiting for transfers between devices, gathered(): lax.all_gather(spill, 'row', axis=0, tiled=True, axis_index_groups=halves)  60.5 us
    ppermute x15, waiting for transfers between devices, swap(): return lax.ppermute(x, 'row', [(i, i ^ bit) for i in range(ranks)])  30.1 us
    all_to_all x1, waiting for transfers between devices, exchange(): lax.all_to_all(sent, 'row', split_axis=0, concat_axis=0, tiled=True)  24.3 us
    ppermute x15, starting transfers between devices, swap(): return lax.ppermute(x, 'row', [(i, i ^ bit) for i in range(ranks)])  14.6 us
    pallas_call x1, Pallas kernels, ladder(): pl.pallas_call(ladder_kernel, out_shape=jax.ShapeDtypeStruct((slots, TILE...  11.2 us
    all_to_all x1, starting transfers between devices, exchange(): lax.all_to_all(sent, 'row', split_axis=0, concat_axis=0, tiled=True)  7.78 us
    pallas_call x1, Pallas kernels, place_tiles(): pl.pallas_call(functools.partial(place_kernel, direct.shape[0], far_from)...  6.46 us
    pallas_call x1, Pallas kernels, begin_output(): pl.pallas_call(functools.partial(begin_kernel, split), out_shape=jax.Shap...  4.74 us
  transfers between devices with their start and end apart: 19, of which 15 were waited for; matrix products, arithmetic and copies ran while one was open for 2% of the time, Pallas kernels for 11%

profile of v5, /device:TPU:16, one launch (start us, length us, event | category | flops | bytes accessed | tf_op | source)
XLA Modules:
  0.0 200.7 jit_solution(13521827364014483903)
XLA Ops:
  6.5 3.5 %prepare.1 = (bf16[1280,256]{1,0:T(8,128)(2,1)}, bf16[1296,256]{1,0:T(8,128)(2,1)}, s32[32]{0:T(128)S(1)}, s32[32]{0:T(128)S(1)}, s32[3]{0:T(128)S(1)}, /*index=5*/s32[3]{0:T(128)S(1)}) custom-call(s32[1]{0:T(128)} %bitcast.9.me_ref, s32[1,4,5]{2,1,0:T(4,128)} %mask_ref.1, s32[4,8]{1,0:T(4,128)} %bitcast.41, s32[4,8]{1,0:T(4,128)} %keep_ref.1, ...), custom_call_target="tpu_custom_call" | custom-call | tf_op jit(solution)/shard_map/prepare/pallas_call | solution.py:195
  10.8 1.6 collective-permute-done.2
  12.5 1.3 broadcast_select_fusion
  13.8 1.6 collective-permute-start.7
  15.5 1.6 collective-permute-start.3
  17.1 4.6 %fetch_columns.1 = bf16[3,2560,256]{2,1,0:T(8,128)(2,1)} custom-call(s32[3]{0:T(128)S(1)} %get-tuple-element.171.tile_ref, bf16[2560,2048]{1,0:T(8,128)(2,1)} %bitcast.27), custom_call_target="tpu_custom_call" | custom-call | bytes 8388608 | tf_op jit(solution)/shard_map/fetch_columns/pallas_call | solution.py:369
  22.3 2.9 %collective-permute-done.3 = bf16[642,256]{1,0:T(8,128)(2,1)S(1)} collective-permute-done((bf16[642,256]{1,0:T(8,128)(2,1)S(1)}, bf16[642,256]{1,0:T(8,128)(2,1)S(1)}, u32[]{:S(2)}, u32[]{:S(2)}) %collective-permute-start.3) | collective-permute-done | bytes 328736 | tf_op jit(solution)/shard_map/ppermute | solution.py:29
  25.3 1.6 collective-permute-start.8
  27.6 3.1 %collective-permute-done.8 = bf16[2,160,256]{2,1,0:T(8,128)(2,1)S(1)} collective-permute-done((bf16[2,160,256]{2,1,0:T(8,128)(2,1)S(1)}, bf16[2,160,256]{2,1,0:T(8,128)(2,1)S(1)}, u32[]{:S(2)}, u32[]{:S(2)}) %collective-permute-start.8) | collective-permute-done | bytes 163872 | tf_op jit(solution)/shard_map/ppermute | solution.py:29
  31.2 3.1 %collective-permute-done.5 = bf16[326,256]{1,0:T(8,128)(2,1)S(1)} collective-permute-done((bf16[326,256]{1,0:T(8,128)(2,1)S(1)}, bf16[326,256]{1,0:T(8,128)(2,1)S(1)}, u32[]{:S(2)}, u32[]{:S(2)}) %collective-permute-start.5) | collective-permute-done | bytes 166944 | tf_op jit(solution)/shard_map/ppermute | solution.py:29
  35.6 2.4 %collective-permute-done.10 = bf16[4,256]{1,0:T(4,128)(2,1)S(1)} collective-permute-done((bf16[4,256]{1,0:T(4,128)(2,1)S(1)}, bf16[4,256]{1,0:T(4,128)(2,1)S(1)}, u32[]{:S(2)}, u32[]{:S(2)}) %collective-permute-start.10) | collective-permute-done | bytes 2080 | tf_op jit(solution)/shard_map/ppermute | solution.py:29
  38.1 1.9 pair_up.1
  40.0 1.1 collective-permute-start.11
  41.0 2.6 %collective-permute-done.11 = s32[1,2]{1,0:T(1,128)S(1)} collective-permute-done((s32[1,2]{1,0:T(1,128)S(1)}, s32[1,2]{1,0:T(1,128)S(1)}, u32[]{:S(2)}, u32[]{:S(2)}) %collective-permute-start.11) | collective-permute-done | bytes 40 | tf_op jit(solution)/shard_map/ppermute | solution.py:68
  43.7 3.2 %collective-permute-start.12 = (bf16[2,160,256]{2,1,0:T(8,128)(2,1)S(1)}, bf16[2,160,256]{2,1,0:T(8,128)(2,1)S(1)}, u32[]{:S(2)}, u32[]{:S(2)}) collective-permute-start(bf16[2,160,256]{2,1,0:T(8,128)(2,1)S(1)} %get-tuple-element.176), channel_id=1, source_target_pairs={{0,4},{1,5},{2,6},{3,7},{4,0},{5,1},{6,2},{7,3},{8,12},{9,13},{10,... | collective-permute-start | bytes 491528 | tf_op jit(solution)/shard_map/ppermute | solution.py:29
  46.9 1.5 collective-permute-start.14
  48.4 1.8 collective-permute-done.12
  50.3 1.5 collective-permute-start.13
  51.8 1.8 collective-permute-done.14
  54.0 5.3 %collective-permute-done.13 = bf16[2,320,256]{2,1,0:T(8,128)(2,1)S(1)} collective-permute-done((bf16[2,320,256]{2,1,0:T(8,128)(2,1)S(1)}, bf16[2,320,256]{2,1,0:T(8,128)(2,1)S(1)}, u32[]{:S(2)}, u32[]{:S(2)}) %collective-permute-start.13) | collective-permute-done | bytes 327712 | tf_op jit(solution)/shard_map/ppermute | solution.py:29
  59.4 1.5 collective-permute-done.15
  63.1 1.2 collective-permute-done.16
  64.2 129.6 %conditional.1 = (bf16[16,4,256,256]{3,2,1,0:T(8,128)(2,1)}) conditional(s32[]{:T(128)} %bitcast.17, (s32[16]{0:T(128)S(1)}, s32[3]{0:T(128)S(1)}, s32[3]{0:T(128)S(1)}, s32[40]{0:T(128)S(1)}, s32[2,5,8]{2,0,1:T(2,128)S(1)}, /*index=5*/bf16[2560,256]{1,0:T(8,128)(2,1)S(1)}, bf16[2560,256]{1,0:T(8,128)(2,1)S(1)}, ...), branch_computations={%region_1.7_spmd, %region_7.13_spmd, %region_13.18_spmd} | conditional | flops 12885126144 | bytes 70557184 | solution.py:657
  64.2 3.9 %spilled.3 = (bf16[3,256,256]{2,1,0:T(8,128)(2,1)}, bf16[3,256,256]{2,1,0:T(8,128)(2,1)S(1)}) custom-call(s32[3]{0:T(128)S(1)} %get-tuple-element.113.tile_ref, s32[3]{0:T(128)S(1)} %get-tuple-element.114.goes_ref, s32[40]{0:T(128)S(1)} %get-tuple-element.115.at_ref, s32[2,5,8]{2,1,0:T(8,128)S(1)} %copy.28.v_mask_ref, ...), custom_call_target="tpu_custom_call" | custom-call | tf_op jit(solution)/shard_map/cond/branch_1_fun/spilled/pallas_call | solution.py:431
  68.9 11.2 %ladder.4 = bf16[32,256,256]{2,1,0:T(8,128)(2,1)} custom-call(s32[12]{0:T(128)S(1)} %get-tuple-element.121.row_ref, s32[24]{0:T(128)S(1)} %get-tuple-element.122.panel_tile_ref, s32[24]{0:T(128)S(1)} %get-tuple-element.123.v_tile_ref, s32[32]{0:T(128)S(1)} %get-tuple-element.124.place_ref, s32[2,5,8]{2,1,0:T(8,128)} %copy-done.1, ...), custom_call_target="tpu_custom_call" | custom-call | flops 12884901888 | bytes 25165824 | tf_op jit(solution)/shard_map/cond/branch_1_fun/ladder/pallas_call | solution.py:328
  80.1 5.5 %collective-permute-done.1 = bf16[3,256,256]{2,1,0:T(8,128)(2,1)S(1)} collective-permute-done((bf16[3,256,256]{2,1,0:T(8,128)(2,1)S(1)}, bf16[3,256,256]{2,1,0:T(8,128)(2,1)S(1)}, u32[]{:S(2)}, u32[]{:S(2)}) %collective-permute-start.1) | collective-permute-done | bytes 393248 | tf_op jit(solution)/shard_map/cond/branch_1_fun/ppermute | solution.py:29
  86.4 7.8 %all-to-all-start.1 = ((bf16[16,2,256,256]{3,2,1,0:T(8,128)(2,1)}), bf16[16,2,256,256]{3,2,1,0:T(8,128)(2,1)}, u32[]{:S(2)}, u32[]{:S(2)}) async-start(bf16[16,2,256,256]{3,2,1,0:T(8,128)(2,1)} %bitcast.36), calls=%async_computation.1 | async-start | bytes 8388608 | tf_op jit(solution)/shard_map/cond/branch_1_fun/all_to_all | solution.py:575
  97.4 2.6 %all-gather.9.cloned.1.call-done.near_ref = bf16[24,256,256]{2,1,0:T(8,128)(2,1)} async-done(((bf16[3,256,256]{2,1,0:T(8,128)(2,1)}), bf16[24,256,256]{2,1,0:T(8,128)(2,1)}) %all-gather.9.cloned.1.call-update) | async-done | bytes 3145744 | tf_op jit(solution)/shard_map/cond/branch_1_fun/all_gather | solution.py:636
  100.0 4.7 %begin_output.4.begun_ref = bf16[64,256,256]{2,1,0:T(8,128)(2,1)} custom-call(s32[64]{0:T(128)} %sub.25.table_ref, bf16[24,256,256]{2,1,0:T(8,128)(2,1)} %all-gather.9.cloned.1.call-done.near_ref), custom_call_target="tpu_custom_call" | custom-call | bytes 8388608 | tf_op jit(solution)/shard_map/cond/branch_1_fun/begin_output/pallas_call | solution.py:492
  104.8 57.8 %all-gather.11.cloned.1.call-done.far_ref = bf16[24,256,256]{2,1,0:T(8,128)(2,1)} async-done(((bf16[3,256,256]{2,1,0:T(8,128)(2,1)}), bf16[24,256,256]{2,1,0:T(8,128)(2,1)}) %all-gather.11.cloned.1.call-update) | async-done | bytes 3145744 | tf_op jit(solution)/shard_map/cond/branch_1_fun/all_gather | solution.py:636
  162.6 24.3 %all-to-all-done.1 = bf16[16,2,256,256]{3,2,1,0:T(8,128)(2,1)} async-done(((bf16[16,2,256,256]{3,2,1,0:T(8,128)(2,1)}), bf16[16,2,256,256]{3,2,1,0:T(8,128)(2,1)}, u32[]{:S(2)}, u32[]{:S(2)}) %all-to-all-start.1) | async-done | bytes 4194336 | tf_op jit(solution)/shard_map/cond/branch_1_fun/all_to_all | solution.py:575
  186.9 6.5 %place_tiles.4 = bf16[64,256,256]{2,1,0:T(8,128)(2,1)} custom-call(s32[64]{0:T(128)} %sub.25.table_ref, bf16[64,256,256]{2,1,0:T(8,128)(2,1)} %begin_output.4.begun_ref, bf16[32,256,256]{2,1,0:T(8,128)(2,1)} %bitcast.4.direct_ref, bf16[24,256,256]{2,1,0:T(8,128)(2,1)} %all-gather.11.cloned.1.call-done.far_ref), custom_call_target="tpu_custom_call", output_to_operand_aliasing={{}: (1, {})} | custom-call | tf_op jit(solution)/shard_map/cond/branch_1_fun/place_tiles/pallas_call | solution.py:556
  (77 shorter events, 10.3 us)
Async XLA Ops:
  6.5 4.2 %copy-start.5 = (s32[2]{0:T(128)S(1)}, s32[2]{0:T(128)}, u32[]{:S(2)}) copy-start(s32[2]{0:T(128)} %param.17) | copy-start | bytes 28
  10.0 2.4 %collective-permute-start.2 = (bf16[1296,256]{1,0:T(8,128)(2,1)}, bf16[1296,256]{1,0:T(8,128)(2,1)S(1)}, u32[]{:S(2)}, u32[]{:S(2)}) collective-permute-start(bf16[1296,256]{1,0:T(8,128)(2,1)} %get-tuple-element.165), channel_id=1, source_target_pairs={{0,1},{1,0},{2,3},{3,2},{4,5},{5,4},{6,7},{7,6},{8,9},{9,8},{10,11... | collective-permute-start | bytes 1990664 | tf_op jit(solution)/shard_map/ppermute | solution.py:29
  12.4 4.6 %copy-start.6 = (s32[16]{0:T(128)S(1)}, s32[16]{0:T(128)}, u32[]{:S(2)}) copy-start(s32[16]{0:T(128)} %constant.143.clone) | copy-start | bytes 196
  13.8 11.3 %collective-permute-start.7 = (bf16[2,320,256]{2,1,0:T(8,128)(2,1)S(1)}, bf16[2,320,256]{2,1,0:T(8,128)(2,1)S(1)}, u32[]{:S(2)}, u32[]{:S(2)}) collective-permute-start(bf16[2,320,256]{2,1,0:T(8,128)(2,1)S(1)} %get-tuple-element.375), channel_id=1, source_target_pairs={{0,4},{1,5},{2,6},{3,7},{4,0},{5,1},{6,2},{7,3},{8,12},{9,13},{10,... | collective-permute-start | bytes 983048 | tf_op jit(solution)/shard_map/ppermute | solution.py:29
  15.5 9.6 %collective-permute-start.3 = (bf16[642,256]{1,0:T(8,128)(2,1)S(1)}, bf16[642,256]{1,0:T(8,128)(2,1)S(1)}, u32[]{:S(2)}, u32[]{:S(2)}) collective-permute-start(bf16[642,256]{1,0:T(8,128)(2,1)S(1)} %pad_maximum_fusion.1), channel_id=1, source_target_pairs={{0,2},{1,3},{2,0},{3,1},{4,6},{5,7},{6,4},{7,5},{8,10},{9,11},{10,... | collective-permute-start | bytes 986120 | tf_op jit(solution)/shard_map/ppermute | solution.py:29
  21.9 5.1 %collective-permute-start.4 = (bf16[2,256]{1,0:T(2,128)(2,1)S(1)}, bf16[2,256]{1,0:T(2,128)(2,1)S(1)}, u32[]{:S(2)}, u32[]{:S(2)}) collective-permute-start(bf16[2,256]{1,0:T(2,128)(2,1)S(1)} %pad_maximum_fusion.5), channel_id=1, source_target_pairs={{0,8},{1,9},{2,10},{3,11},{4,12},{5,13},{6,14},{7,15},{8,0},{9,1},... | collective-permute-start | bytes 3080 | tf_op jit(solution)/shard_map/ppermute | solution.py:29
  25.3 5.4 %collective-permute-start.8 = (bf16[2,160,256]{2,1,0:T(8,128)(2,1)S(1)}, bf16[2,160,256]{2,1,0:T(8,128)(2,1)S(1)}, u32[]{:S(2)}, u32[]{:S(2)}) collective-permute-start(bf16[2,160,256]{2,1,0:T(8,128)(2,1)S(1)} %broadcast_select_fusion.11), channel_id=1, source_target_pairs={{0,2},{1,3},{2,0},{3,1},{4,6},{5,7},{6,4},{7,5},{8,10},{9,11},{10,... | collective-permute-start | bytes 491528 | tf_op jit(solution)/shard_map/ppermute | solution.py:29
  27.1 7.2 %collective-permute-start.5 = (bf16[326,256]{1,0:T(8,128)(2,1)S(1)}, bf16[326,256]{1,0:T(8,128)(2,1)S(1)}, u32[]{:S(2)}, u32[]{:S(2)}) collective-permute-start(bf16[326,256]{1,0:T(8,128)(2,1)S(1)} %concatenate.32), channel_id=1, source_target_pairs={{0,4},{1,5},{2,6},{3,7},{4,0},{5,1},{6,2},{7,3},{8,12},{9,13},{10,... | collective-permute-start | bytes 500744 | tf_op jit(solution)/shard_map/ppermute | solution.py:29
  30.8 12.8 %collective-permute-start.9 = (bf16[2,160,256]{2,1,0:T(8,128)(2,1)S(1)}, bf16[2,160,256]{2,1,0:T(8,128)(2,1)S(1)}, u32[]{:S(2)}, u32[]{:S(2)}) collective-permute-start(bf16[2,160,256]{2,1,0:T(8,128)(2,1)S(1)} %select_select_fusion.2), channel_id=1, source_target_pairs={{0,8},{1,9},{2,10},{3,11},{4,12},{5,13},{6,14},{7,15},{8,0},{9,1},... | collective-permute-start | bytes 491528 | tf_op jit(solution)/shard_map/ppermute | solution.py:29
  34.3 3.6 %collective-permute-start.10 = (bf16[4,256]{1,0:T(4,128)(2,1)S(1)}, bf16[4,256]{1,0:T(4,128)(2,1)S(1)}, u32[]{:S(2)}, u32[]{:S(2)}) collective-permute-start(bf16[4,256]{1,0:T(4,128)(2,1)S(1)} %pad_maximum_fusion.4), channel_id=1, source_target_pairs={{0,2},{1,3},{2,0},{3,1},{4,6},{5,7},{6,4},{7,5},{8,10},{9,11},{10,... | collective-permute-start | bytes 6152 | tf_op jit(solution)/shard_map/ppermute | solution.py:29
  34.7 8.9 %collective-permute-start.6 = (bf16[2,160,256]{2,1,0:T(8,128)(2,1)S(1)}, bf16[2,160,256]{2,1,0:T(8,128)(2,1)S(1)}, u32[]{:S(2)}, u32[]{:S(2)}) collective-permute-start(bf16[2,160,256]{2,1,0:T(8,128)(2,1)S(1)} %select_select_fusion.3), channel_id=1, source_target_pairs={{0,8},{1,9},{2,10},{3,11},{4,12},{5,13},{6,14},{7,15},{8,0},{9,1},... | collective-permute-start | bytes 491528 | tf_op jit(solution)/shard_map/ppermute | solution.py:29
  40.0 3.6 %collective-permute-start.11 = (s32[1,2]{1,0:T(1,128)S(1)}, s32[1,2]{1,0:T(1,128)S(1)}, u32[]{:S(2)}, u32[]{:S(2)}) collective-permute-start(s32[1,2]{1,0:T(1,128)S(1)} %get-tuple-element.166), channel_id=1, source_target_pairs={{0,16},{16,0},{1,17},{17,1},{2,18},{18,2},{3,19},{19,3},{4,20},{20... | collective-permute-start | bytes 32 | tf_op jit(solution)/shard_map/ppermute | solution.py:68
  43.7 6.5 %collective-permute-start.12 = (bf16[2,160,256]{2,1,0:T(8,128)(2,1)S(1)}, bf16[2,160,256]{2,1,0:T(8,128)(2,1)S(1)}, u32[]{:S(2)}, u32[]{:S(2)}) collective-permute-start(bf16[2,160,256]{2,1,0:T(8,128)(2,1)S(1)} %get-tuple-element.176), channel_id=1, source_target_pairs={{0,4},{1,5},{2,6},{3,7},{4,0},{5,1},{6,2},{7,3},{8,12},{9,13},{10,... | collective-permute-start | bytes 491528 | tf_op jit(solution)/shard_map/ppermute | solution.py:29
  46.9 6.8 %collective-permute-start.14 = (bf16[2,160,256]{2,1,0:T(8,128)(2,1)S(1)}, bf16[2,160,256]{2,1,0:T(8,128)(2,1)S(1)}, u32[]{:S(2)}, u32[]{:S(2)}) collective-permute-start(bf16[2,160,256]{2,1,0:T(8,128)(2,1)S(1)} %get-tuple-element.177), channel_id=1, source_target_pairs={{0,2},{1,3},{2,0},{3,1},{4,6},{5,7},{6,4},{7,5},{8,10},{9,11},{10,... | collective-permute-start | bytes 491528 | tf_op jit(solution)/shard_map/ppermute | solution.py:29
  50.3 9.0 %collective-permute-start.13 = (bf16[2,320,256]{2,1,0:T(8,128)(2,1)S(1)}, bf16[2,320,256]{2,1,0:T(8,128)(2,1)S(1)}, u32[]{:S(2)}, u32[]{:S(2)}) collective-permute-start(bf16[2,320,256]{2,1,0:T(8,128)(2,1)S(1)} %pad_maximum_fusion.2), channel_id=1, source_target_pairs={{0,2},{1,3},{2,0},{3,1},{4,6},{5,7},{6,4},{7,5},{8,10},{9,11},{10,... | collective-permute-start | bytes 983048 | tf_op jit(solution)/shard_map/ppermute | solution.py:29
  53.7 10.5 %copy-start.4 = (s32[2,5,8]{2,0,1:T(2,128)S(1)}, s32[2,5,8]{2,0,1:T(2,128)}, u32[]{:S(2)}) copy-start(s32[2,5,8]{2,0,1:T(2,128)} %param.14) | copy-start | bytes 964
  53.8 7.1 %collective-permute-start.15 = (bf16[2,320,256]{2,1,0:T(8,128)(2,1)S(1)}, bf16[2,320,256]{2,1,0:T(8,128)(2,1)S(1)}, u32[]{:S(2)}, u32[]{:S(2)}) collective-permute-start(bf16[2,320,256]{2,1,0:T(8,128)(2,1)S(1)} %pad_maximum_fusion.3), channel_id=1, source_target_pairs={{0,4},{1,5},{2,6},{3,7},{4,0},{5,1},{6,2},{7,3},{8,12},{9,13},{10,... | collective-permute-start | bytes 983048 | tf_op jit(solution)/shard_map/ppermute | solution.py:29
  61.1 3.1 %collective-permute-start.16 = (bf16[2,1280,256]{2,1,0:T(8,128)(2,1)S(1)}, bf16[2,1280,256]{2,1,0:T(8,128)(2,1)S(1)}, u32[]{:S(2)}, u32[]{:S(2)}) collective-permute-start(bf16[2,1280,256]{2,1,0:T(8,128)(2,1)S(1)} %pad_maximum_fusion), channel_id=1, source_target_pairs={{0,1},{1,0},{2,3},{3,2},{4,5},{5,4},{6,7},{7,6},{8,9},{9,8},{10,11... | collective-permute-start | bytes 3932168 | tf_op jit(solution)/shard_map/ppermute | solution.py:29
  64.2 35.8 %all-gather.9.cloned.1.call-start = ((), (), s32[]{:S(2)}) async-start(), calls=%async_computation.5 | async-start | bytes 3538944 | tf_op jit(solution)/shard_map/cond/branch_1_fun/all_gather | solution.py:636
  64.2 4.0 %copy-start.1 = (s32[2,5,8]{2,1,0:T(8,128)}, s32[2,5,8]{2,1,0:T(8,128)S(1)}, u32[]{:S(2)}) copy-start(s32[2,5,8]{2,1,0:T(8,128)S(1)} %copy.28.v_mask_ref) | copy-start | bytes 964 | tf_op jit(solution)/shard_map/cond
  68.2 17.4 %collective-permute-start.1 = (bf16[3,256,256]{2,1,0:T(8,128)(2,1)S(1)}, bf16[3,256,256]{2,1,0:T(8,128)(2,1)S(1)}, u32[]{:S(2)}, u32[]{:S(2)}) collective-permute-start(bf16[3,256,256]{2,1,0:T(8,128)(2,1)S(1)} %get-tuple-element.120), channel_id=1, source_target_pairs={{0,8},{1,9},{2,10},{3,11},{4,12},{5,13},{6,14},{7,15},{8,0},{9,1},... | collective-permute-start | bytes 1179656 | tf_op jit(solution)/shard_map/cond/branch_1_fun/ppermute | solution.py:29
  85.6 0.8 copy-start.2
  86.4 100.5 %all-to-all-start.1 = ((bf16[16,2,256,256]{3,2,1,0:T(8,128)(2,1)}), bf16[16,2,256,256]{3,2,1,0:T(8,128)(2,1)}, u32[]{:S(2)}, u32[]{:S(2)}) async-start(bf16[16,2,256,256]{3,2,1,0:T(8,128)(2,1)} %bitcast.36), calls=%async_computation.1 | async-start | bytes 8388608 | tf_op jit(solution)/shard_map/cond/branch_1_fun/all_to_all | solution.py:575
  94.2 68.4 %all-gather.11.cloned.1.call-start = ((), (), s32[]{:S(2)}) async-start(), calls=%async_computation.6 | async-start | bytes 3538944 | tf_op jit(solution)/shard_map/cond/branch_1_fun/all_gather | solution.py:636
Sparse Core Ops, SparseCore 0:
  68.3 31.6 all-gather.8
  101.6 60.9 all-gather.10

commit v6 on v5

--- a/solution.py
+++ b/solution.py
@@ -74,9 +74,9 @@
     rows = own.shape[0]
     got = swap(give, 1, ranks)
     note, xors = jnp.concatenate([give[rows : rows + 1], got[rows : rows + 1]], axis=0), [0, 1]
-    x = jnp.where(near(me, roots, 1), own[None], got[None, :rows])
-    half = rows // 2
-    a, b = x[:, :half], x[:, half:]
+    half, same = rows // 2, near(me, roots, 1)
+    a = jnp.where(same, own[None, :half], got[None, :half])
+    b = jnp.where(same, own[None, half:], got[None, half:rows])
     a, got_note = scatter_step(a, note, me, roots, 2, ranks)
     b, _ = scatter_step(b, None, me, roots, 4, ranks)
     across, across_xors, bit = note, xors, 8

time: 201 us -> 203 us (level); the launches traced: 201 us -> 206 us
  starting transfers between devices: 23.5 us -> 32.8 us
  waiting for transfers between devices: 118 us -> 115 us
    ppermute x15, starting transfers between devices: 14.6 us -> 23.4 us  [swap(): return lax.ppermute(x, 'row', [(i, i ^ bit) for i in range(ranks)])]
    ppermute x15, waiting for transfers between devices: 30.1 us -> 27.4 us  [swap(): return lax.ppermute(x, 'row', [(i, i ^ bit) for i in range(ranks)])]
  transfers between devices with their start and end apart: 19 -> 19, of which waited for: 15 -> 14; matrix products, arithmetic and copies ran while one was open for 2% -> 3% of each run, Pallas kernels for 11% -> 11%
where the time goes in v6:
time: 203 us; the launch traced here: 206 us
  waiting for transfers between devices  115 us (57%)
  Pallas kernels  34.4 us (17%)
  starting transfers between devices  32.8 us (16%)
  between operations  14.9 us (7%)
  other arithmetic  4.53 us (2%)
  local copies, waits for them, and re-layouts  3.19 us (2%)
    all_gather x2, waiting for transfers between devices, gathered(): lax.all_gather(spill, 'row', axis=0, tiled=True, axis_index_groups=halves)  60.1 us
    ppermute x15, waiting for transfers between devices, swap(): return lax.ppermute(x, 'row', [(i, i ^ bit) for i in range(ranks)])  27.4 us
    all_to_all x1, waiting for transfers between devices, exchange(): lax.all_to_all(sent, 'row', split_axis=0, concat_axis=0, tiled=True)  25.1 us
    ppermute x15, starting transfers between devices, swap(): return lax.ppermute(x, 'row', [(i, i ^ bit) for i in range(ranks)])  23.4 us
    pallas_call x1, Pallas kernels, ladder(): pl.pallas_call(ladder_kernel, out_shape=jax.ShapeDtypeStruct((slots, TILE...  11.4 us
    all_to_all x1, starting transfers between devices, exchange(): lax.all_to_all(sent, 'row', split_axis=0, concat_axis=0, tiled=True)  7.78 us
    pallas_call x1, Pallas kernels, place_tiles(): pl.pallas_call(functools.partial(place_kernel, direct.shape[0], far_from)...  5.03 us
    pallas_call x1, Pallas kernels, fetch_columns(): pl.pallas_call(fetch_kernel, out_shape=jax.ShapeDtypeStruct((SPILL, v.sha...  4.57 us
  transfers between devices with their start and end apart: 19, of which 14 were waited for; matrix products, arithmetic and copies ran while one was open for 3% of the time, Pallas kernels for 11%

profile of v6, /device:TPU:16, one launch (start us, length us, event | category | flops | bytes accessed | tf_op | source)
XLA Modules:
  0.0 205.7 jit_solution(1545906502263235664)
XLA Ops:
  6.5 3.3 %prepare.1 = (bf16[1280,256]{1,0:T(8,128)(2,1)}, bf16[1296,256]{1,0:T(8,128)(2,1)}, s32[32]{0:T(128)S(1)}, s32[32]{0:T(128)S(1)}, s32[3]{0:T(128)S(1)}, /*index=5*/s32[3]{0:T(128)S(1)}) custom-call(s32[1]{0:T(128)} %bitcast.9.me_ref, s32[1,4,5]{2,1,0:T(4,128)} %mask_ref.1, s32[4,8]{1,0:T(4,128)} %bitcast.41, s32[4,8]{1,0:T(4,128)} %keep_ref.1, ...), custom_call_target="tpu_custom_call" | custom-call | tf_op jit(solution)/shard_map/prepare/pallas_call | solution.py:195
  12.1 4.6 %fetch_columns.1 = bf16[3,2560,256]{2,1,0:T(8,128)(2,1)} custom-call(s32[3]{0:T(128)S(1)} %get-tuple-element.171.tile_ref, bf16[2560,2048]{1,0:T(8,128)(2,1)} %bitcast.27), custom_call_target="tpu_custom_call" | custom-call | bytes 8388608 | tf_op jit(solution)/shard_map/fetch_columns/pallas_call | solution.py:369
  17.3 2.1 %collective-permute-start.7 = (bf16[2,320,256]{2,1,0:T(8,128)(2,1)S(1)}, bf16[2,320,256]{2,1,0:T(8,128)(2,1)S(1)}, u32[]{:S(2)}, u32[]{:S(2)}) collective-permute-start(bf16[2,320,256]{2,1,0:T(8,128)(2,1)S(1)} %broadcast_select_fusion.4), channel_id=1, source_target_pairs={{0,4},{1,5},{2,6},{3,7},{4,0},{5,1},{6,2},{7,3},{8,12},{9,13},{10,... | collective-permute-start | bytes 983048 | tf_op jit(solution)/shard_map/ppermute | solution.py:29
  19.4 1.5 collective-permute-start.3
  20.9 6.5 %collective-permute-done.7 = bf16[2,320,256]{2,1,0:T(8,128)(2,1)S(1)} collective-permute-done((bf16[2,320,256]{2,1,0:T(8,128)(2,1)S(1)}, bf16[2,320,256]{2,1,0:T(8,128)(2,1)S(1)}, u32[]{:S(2)}, u32[]{:S(2)}) %collective-permute-start.7) | collective-permute-done | bytes 327712 | tf_op jit(solution)/shard_map/ppermute | solution.py:29
  27.6 1.6 collective-permute-start.8
  29.5 1.7 collective-permute-start.5
  31.2 2.3 %collective-permute-done.8 = bf16[2,160,256]{2,1,0:T(8,128)(2,1)S(1)} collective-permute-done((bf16[2,160,256]{2,1,0:T(8,128)(2,1)S(1)}, bf16[2,160,256]{2,1,0:T(8,128)(2,1)S(1)}, u32[]{:S(2)}, u32[]{:S(2)}) %collective-permute-start.8) | collective-permute-done | bytes 163872 | tf_op jit(solution)/shard_map/ppermute | solution.py:29
  33.6 2.4 %collective-permute-start.9 = (bf16[2,160,256]{2,1,0:T(8,128)(2,1)S(1)}, bf16[2,160,256]{2,1,0:T(8,128)(2,1)S(1)}, u32[]{:S(2)}, u32[]{:S(2)}) collective-permute-start(bf16[2,160,256]{2,1,0:T(8,128)(2,1)S(1)} %select_select_fusion.2), channel_id=1, source_target_pairs={{0,8},{1,9},{2,10},{3,11},{4,12},{5,13},{6,14},{7,15},{8,0},{9,1},... | collective-permute-start | bytes 491528 | tf_op jit(solution)/shard_map/ppermute | solution.py:29
  35.9 1.8 collective-permute-start.10
  37.8 1.3 collective-permute-start.6
  39.7 1.9 pair_up.1
  41.6 1.6 collective-permute-start.11
  43.2 2.0 collective-permute-done.11
  46.1 2.4 %collective-permute-done.6 = bf16[2,160,256]{2,1,0:T(8,128)(2,1)S(1)} collective-permute-done((bf16[2,160,256]{2,1,0:T(8,128)(2,1)S(1)}, bf16[2,160,256]{2,1,0:T(8,128)(2,1)S(1)}, u32[]{:S(2)}, u32[]{:S(2)}) %collective-permute-start.6) | collective-permute-done | bytes 163872 | tf_op jit(solution)/shard_map/ppermute | solution.py:29
  48.7 2.4 %collective-permute-start.12 = (bf16[2,160,256]{2,1,0:T(8,128)(2,1)S(1)}, bf16[2,160,256]{2,1,0:T(8,128)(2,1)S(1)}, u32[]{:S(2)}, u32[]{:S(2)}) collective-permute-start(bf16[2,160,256]{2,1,0:T(8,128)(2,1)S(1)} %get-tuple-element.176), channel_id=1, source_target_pairs={{0,4},{1,5},{2,6},{3,7},{4,0},{5,1},{6,2},{7,3},{8,12},{9,13},{10,... | collective-permute-start | bytes 491528 | tf_op jit(solution)/shard_map/ppermute | solution.py:29
  51.0 1.6 collective-permute-start.14
  52.7 1.7 collective-permute-done.12
  54.4 2.2 %collective-permute-start.13 = (bf16[2,320,256]{2,1,0:T(8,128)(2,1)S(1)}, bf16[2,320,256]{2,1,0:T(8,128)(2,1)S(1)}, u32[]{:S(2)}, u32[]{:S(2)}) collective-permute-start(bf16[2,320,256]{2,1,0:T(8,128)(2,1)S(1)} %pad_maximum_fusion.2), channel_id=1, source_target_pairs={{0,2},{1,3},{2,0},{3,1},{4,6},{5,7},{6,4},{7,5},{8,10},{9,11},{10,... | collective-permute-start | bytes 983048 | tf_op jit(solution)/shard_map/ppermute | solution.py:29
  56.6 1.8 collective-permute-start.15
  58.5 4.9 %collective-permute-done.13 = bf16[2,320,256]{2,1,0:T(8,128)(2,1)S(1)} collective-permute-done((bf16[2,320,256]{2,1,0:T(8,128)(2,1)S(1)}, bf16[2,320,256]{2,1,0:T(8,128)(2,1)S(1)}, u32[]{:S(2)}, u32[]{:S(2)}) %collective-permute-start.13) | collective-permute-done | bytes 327712 | tf_op jit(solution)/shard_map/ppermute | solution.py:29
  63.5 1.3 collective-permute-done.15
  68.2 130.7 %conditional.1 = (bf16[16,4,256,256]{3,2,1,0:T(8,128)(2,1)}) conditional(s32[]{:T(128)} %bitcast.17, (s32[16]{0:T(128)S(1)}, s32[3]{0:T(128)S(1)}, s32[3]{0:T(128)S(1)}, s32[40]{0:T(128)S(1)}, s32[2,5,8]{2,0,1:T(2,128)S(1)}, /*index=5*/bf16[2560,256]{1,0:T(8,128)(2,1)S(1)}, bf16[2560,256]{1,0:T(8,128)(2,1)S(1)}, ...), branch_computations={%region_1.7_spmd, %region_7.13_spmd, %region_13.18_spmd} | conditional | flops 12885126144 | bytes 70557184 | solution.py:657
  68.2 3.9 %spilled.3 = (bf16[3,256,256]{2,1,0:T(8,128)(2,1)}, bf16[3,256,256]{2,1,0:T(8,128)(2,1)S(1)}) custom-call(s32[3]{0:T(128)S(1)} %get-tuple-element.113.tile_ref, s32[3]{0:T(128)S(1)} %get-tuple-element.114.goes_ref, s32[40]{0:T(128)S(1)} %get-tuple-element.115.at_ref, s32[2,5,8]{2,1,0:T(8,128)S(1)} %copy.28.v_mask_ref, ...), custom_call_target="tpu_custom_call" | custom-call | tf_op jit(solution)/shard_map/cond/branch_1_fun/spilled/pallas_call | solution.py:431
  72.1 2.8 %collective-permute-start.1 = (bf16[3,256,256]{2,1,0:T(8,128)(2,1)S(1)}, bf16[3,256,256]{2,1,0:T(8,128)(2,1)S(1)}, u32[]{:S(2)}, u32[]{:S(2)}) collective-permute-start(bf16[3,256,256]{2,1,0:T(8,128)(2,1)S(1)} %get-tuple-element.120), channel_id=1, source_target_pairs={{0,8},{1,9},{2,10},{3,11},{4,12},{5,13},{6,14},{7,15},{8,0},{9,1},... | collective-permute-start | bytes 1179656 | tf_op jit(solution)/shard_map/cond/branch_1_fun/ppermute | solution.py:29
  75.0 11.4 %ladder.4 = bf16[32,256,256]{2,1,0:T(8,128)(2,1)} custom-call(s32[12]{0:T(128)S(1)} %get-tuple-element.121.row_ref, s32[24]{0:T(128)S(1)} %get-tuple-element.122.panel_tile_ref, s32[24]{0:T(128)S(1)} %get-tuple-element.123.v_tile_ref, s32[32]{0:T(128)S(1)} %get-tuple-element.124.place_ref, s32[2,5,8]{2,1,0:T(8,128)} %copy-done.1, ...), custom_call_target="tpu_custom_call" | custom-call | flops 12884901888 | bytes 25165824 | tf_op jit(solution)/shard_map/cond/branch_1_fun/ladder/pallas_call | solution.py:328
  86.3 5.7 %collective-permute-done.1 = bf16[3,256,256]{2,1,0:T(8,128)(2,1)S(1)} collective-permute-done((bf16[3,256,256]{2,1,0:T(8,128)(2,1)S(1)}, bf16[3,256,256]{2,1,0:T(8,128)(2,1)S(1)}, u32[]{:S(2)}, u32[]{:S(2)}) %collective-permute-start.1) | collective-permute-done | bytes 393248 | tf_op jit(solution)/shard_map/cond/branch_1_fun/ppermute | solution.py:29
  92.8 7.8 %all-to-all-start.1 = ((bf16[16,2,256,256]{3,2,1,0:T(8,128)(2,1)}), bf16[16,2,256,256]{3,2,1,0:T(8,128)(2,1)}, u32[]{:S(2)}, u32[]{:S(2)}) async-start(bf16[16,2,256,256]{3,2,1,0:T(8,128)(2,1)} %bitcast.36), calls=%async_computation.1 | async-start | bytes 8388608 | tf_op jit(solution)/shard_map/cond/branch_1_fun/all_to_all | solution.py:575
  104.2 4.3 %begin_output.4.begun_ref = bf16[64,256,256]{2,1,0:T(8,128)(2,1)} custom-call(s32[64]{0:T(128)} %sub.25.table_ref, bf16[24,256,256]{2,1,0:T(8,128)(2,1)} %all-gather.9.cloned.1.call-done.near_ref), custom_call_target="tpu_custom_call" | custom-call | bytes 8388608 | tf_op jit(solution)/shard_map/cond/branch_1_fun/begin_output/pallas_call | solution.py:492
  108.5 59.7 %all-gather.11.cloned.1.call-done.far_ref = bf16[24,256,256]{2,1,0:T(8,128)(2,1)} async-done(((bf16[3,256,256]{2,1,0:T(8,128)(2,1)}), bf16[24,256,256]{2,1,0:T(8,128)(2,1)}) %all-gather.11.cloned.1.call-update) | async-done | bytes 3145744 | tf_op jit(solution)/shard_map/cond/branch_1_fun/all_gather | solution.py:636
  168.2 25.1 %all-to-all-done.1 = bf16[16,2,256,256]{3,2,1,0:T(8,128)(2,1)} async-done(((bf16[16,2,256,256]{3,2,1,0:T(8,128)(2,1)}), bf16[16,2,256,256]{3,2,1,0:T(8,128)(2,1)}, u32[]{:S(2)}, u32[]{:S(2)}) %all-to-all-start.1) | async-done | bytes 4194336 | tf_op jit(solution)/shard_map/cond/branch_1_fun/all_to_all | solution.py:575
  193.3 5.0 %place_tiles.4 = bf16[64,256,256]{2,1,0:T(8,128)(2,1)} custom-call(s32[64]{0:T(128)} %sub.25.table_ref, bf16[64,256,256]{2,1,0:T(8,128)(2,1)} %begin_output.4.begun_ref, bf16[32,256,256]{2,1,0:T(8,128)(2,1)} %bitcast.4.direct_ref, bf16[24,256,256]{2,1,0:T(8,128)(2,1)} %all-gather.11.cloned.1.call-done.far_ref), custom_call_target="tpu_custom_call", output_to_operand_aliasing={{}: (1, {})} | custom-call | tf_op jit(solution)/shard_map/cond/branch_1_fun/place_tiles/pallas_call | solution.py:556
  (80 shorter events, 11.6 us)
Async XLA Ops:
  9.9 7.0 %collective-permute-start.2 = (bf16[1296,256]{1,0:T(8,128)(2,1)}, bf16[1296,256]{1,0:T(8,128)(2,1)S(1)}, u32[]{:S(2)}, u32[]{:S(2)}) collective-permute-start(bf16[1296,256]{1,0:T(8,128)(2,1)} %get-tuple-element.165), channel_id=1, source_target_pairs={{0,1},{1,0},{2,3},{3,2},{4,5},{5,4},{6,7},{7,6},{8,9},{9,8},{10,11... | collective-permute-start | bytes 1990664 | tf_op jit(solution)/shard_map/ppermute | solution.py:29
  12.1 4.6 %copy-start.6 = (s32[2]{0:T(128)S(1)}, s32[2]{0:T(128)}, u32[]{:S(2)}) copy-start(s32[2]{0:T(128)} %param.17) | copy-start | bytes 28
  12.1 4.6 %copy-start.2 = (bf16[1280,256]{1,0:T(8,128)(2,1)S(1)}, bf16[1280,256]{1,0:T(8,128)(2,1)}, u32[]{:S(2)}) copy-start(bf16[1280,256]{1,0:T(8,128)(2,1)} %get-tuple-element.164) | copy-start | bytes 1966084
  16.9 12.5 %collective-permute-start.4 = (bf16[2,256]{1,0:T(2,128)(2,1)S(1)}, bf16[2,256]{1,0:T(2,128)(2,1)S(1)}, u32[]{:S(2)}, u32[]{:S(2)}) collective-permute-start(bf16[2,256]{1,0:T(2,128)(2,1)S(1)} %pad_maximum_fusion.5), channel_id=1, source_target_pairs={{0,8},{1,9},{2,10},{3,11},{4,12},{5,13},{6,14},{7,15},{8,0},{9,1},... | collective-permute-start | bytes 3080 | tf_op jit(solution)/shard_map/ppermute | solution.py:29
  17.3 10.2 %collective-permute-start.7 = (bf16[2,320,256]{2,1,0:T(8,128)(2,1)S(1)}, bf16[2,320,256]{2,1,0:T(8,128)(2,1)S(1)}, u32[]{:S(2)}, u32[]{:S(2)}) collective-permute-start(bf16[2,320,256]{2,1,0:T(8,128)(2,1)S(1)} %broadcast_select_fusion.4), channel_id=1, source_target_pairs={{0,4},{1,5},{2,6},{3,7},{4,0},{5,1},{6,2},{7,3},{8,12},{9,13},{10,... | collective-permute-start | bytes 983048 | tf_op jit(solution)/shard_map/ppermute | solution.py:29
  19.4 9.8 %collective-permute-start.3 = (bf16[642,256]{1,0:T(8,128)(2,1)S(1)}, bf16[642,256]{1,0:T(8,128)(2,1)S(1)}, u32[]{:S(2)}, u32[]{:S(2)}) collective-permute-start(bf16[642,256]{1,0:T(8,128)(2,1)S(1)} %pad_maximum_fusion.1), channel_id=1, source_target_pairs={{0,2},{1,3},{2,0},{3,1},{4,6},{5,7},{6,4},{7,5},{8,10},{9,11},{10,... | collective-permute-start | bytes 986120 | tf_op jit(solution)/shard_map/ppermute | solution.py:29
  27.6 5.9 %collective-permute-start.8 = (bf16[2,160,256]{2,1,0:T(8,128)(2,1)S(1)}, bf16[2,160,256]{2,1,0:T(8,128)(2,1)S(1)}, u32[]{:S(2)}, u32[]{:S(2)}) collective-permute-start(bf16[2,160,256]{2,1,0:T(8,128)(2,1)S(1)} %broadcast_select_fusion.12), channel_id=1, source_target_pairs={{0,2},{1,3},{2,0},{3,1},{4,6},{5,7},{6,4},{7,5},{8,10},{9,11},{10,... | collective-permute-start | bytes 491528 | tf_op jit(solution)/shard_map/ppermute | solution.py:29
  29.5 6.4 %collective-permute-start.5 = (bf16[326,256]{1,0:T(8,128)(2,1)S(1)}, bf16[326,256]{1,0:T(8,128)(2,1)S(1)}, u32[]{:S(2)}, u32[]{:S(2)}) collective-permute-start(bf16[326,256]{1,0:T(8,128)(2,1)S(1)} %concatenate.32), channel_id=1, source_target_pairs={{0,4},{1,5},{2,6},{3,7},{4,0},{5,1},{6,2},{7,3},{8,12},{9,13},{10,... | collective-permute-start | bytes 500744 | tf_op jit(solution)/shard_map/ppermute | solution.py:29
  33.6 12.6 %collective-permute-start.9 = (bf16[2,160,256]{2,1,0:T(8,128)(2,1)S(1)}, bf16[2,160,256]{2,1,0:T(8,128)(2,1)S(1)}, u32[]{:S(2)}, u32[]{:S(2)}) collective-permute-start(bf16[2,160,256]{2,1,0:T(8,128)(2,1)S(1)} %select_select_fusion.2), channel_id=1, source_target_pairs={{0,8},{1,9},{2,10},{3,11},{4,12},{5,13},{6,14},{7,15},{8,0},{9,1},... | collective-permute-start | bytes 491528 | tf_op jit(solution)/shard_map/ppermute | solution.py:29
  35.9 3.6 %collective-permute-start.10 = (bf16[4,256]{1,0:T(4,128)(2,1)S(1)}, bf16[4,256]{1,0:T(4,128)(2,1)S(1)}, u32[]{:S(2)}, u32[]{:S(2)}) collective-permute-start(bf16[4,256]{1,0:T(4,128)(2,1)S(1)} %pad_maximum_fusion.4), channel_id=1, source_target_pairs={{0,2},{1,3},{2,0},{3,1},{4,6},{5,7},{6,4},{7,5},{8,10},{9,11},{10,... | collective-permute-start | bytes 6152 | tf_op jit(solution)/shard_map/ppermute | solution.py:29
  37.8 10.8 %collective-permute-start.6 = (bf16[2,160,256]{2,1,0:T(8,128)(2,1)S(1)}, bf16[2,160,256]{2,1,0:T(8,128)(2,1)S(1)}, u32[]{:S(2)}, u32[]{:S(2)}) collective-permute-start(bf16[2,160,256]{2,1,0:T(8,128)(2,1)S(1)} %select_select_fusion.3), channel_id=1, source_target_pairs={{0,8},{1,9},{2,10},{3,11},{4,12},{5,13},{6,14},{7,15},{8,0},{9,1},... | collective-permute-start | bytes 491528 | tf_op jit(solution)/shard_map/ppermute | solution.py:29
  41.6 3.6 %collective-permute-start.11 = (s32[1,2]{1,0:T(1,128)S(1)}, s32[1,2]{1,0:T(1,128)S(1)}, u32[]{:S(2)}, u32[]{:S(2)}) collective-permute-start(s32[1,2]{1,0:T(1,128)S(1)} %get-tuple-element.166), channel_id=1, source_target_pairs={{0,16},{16,0},{1,17},{17,1},{2,18},{18,2},{3,19},{19,3},{4,20},{20... | collective-permute-start | bytes 32 | tf_op jit(solution)/shard_map/ppermute | solution.py:68
  48.7 5.7 %collective-permute-start.12 = (bf16[2,160,256]{2,1,0:T(8,128)(2,1)S(1)}, bf16[2,160,256]{2,1,0:T(8,128)(2,1)S(1)}, u32[]{:S(2)}, u32[]{:S(2)}) collective-permute-start(bf16[2,160,256]{2,1,0:T(8,128)(2,1)S(1)} %get-tuple-element.176), channel_id=1, source_target_pairs={{0,4},{1,5},{2,6},{3,7},{4,0},{5,1},{6,2},{7,3},{8,12},{9,13},{10,... | collective-permute-start | bytes 491528 | tf_op jit(solution)/shard_map/ppermute | solution.py:29
  51.0 5.5 %collective-permute-start.14 = (bf16[2,160,256]{2,1,0:T(8,128)(2,1)S(1)}, bf16[2,160,256]{2,1,0:T(8,128)(2,1)S(1)}, u32[]{:S(2)}, u32[]{:S(2)}) collective-permute-start(bf16[2,160,256]{2,1,0:T(8,128)(2,1)S(1)} %get-tuple-element.177), channel_id=1, source_target_pairs={{0,2},{1,3},{2,0},{3,1},{4,6},{5,7},{6,4},{7,5},{8,10},{9,11},{10,... | collective-permute-start | bytes 491528 | tf_op jit(solution)/shard_map/ppermute | solution.py:29
  54.4 13.7 %copy-start.5 = (s32[2,5,8]{2,0,1:T(2,128)S(1)}, s32[2,5,8]{2,0,1:T(2,128)}, u32[]{:S(2)}) copy-start(s32[2,5,8]{2,0,1:T(2,128)} %param.14) | copy-start | bytes 964
  54.4 9.0 %collective-permute-start.13 = (bf16[2,320,256]{2,1,0:T(8,128)(2,1)S(1)}, bf16[2,320,256]{2,1,0:T(8,128)(2,1)S(1)}, u32[]{:S(2)}, u32[]{:S(2)}) collective-permute-start(bf16[2,320,256]{2,1,0:T(8,128)(2,1)S(1)} %pad_maximum_fusion.2), channel_id=1, source_target_pairs={{0,2},{1,3},{2,0},{3,1},{4,6},{5,7},{6,4},{7,5},{8,10},{9,11},{10,... | collective-permute-start | bytes 983048 | tf_op jit(solution)/shard_map/ppermute | solution.py:29
  56.6 8.2 %collective-permute-start.15 = (bf16[2,320,256]{2,1,0:T(8,128)(2,1)S(1)}, bf16[2,320,256]{2,1,0:T(8,128)(2,1)S(1)}, u32[]{:S(2)}, u32[]{:S(2)}) collective-permute-start(bf16[2,320,256]{2,1,0:T(8,128)(2,1)S(1)} %pad_maximum_fusion.3), channel_id=1, source_target_pairs={{0,4},{1,5},{2,6},{3,7},{4,0},{5,1},{6,2},{7,3},{8,12},{9,13},{10,... | collective-permute-start | bytes 983048 | tf_op jit(solution)/shard_map/ppermute | solution.py:29
  65.0 3.1 %collective-permute-start.16 = (bf16[2,1280,256]{2,1,0:T(8,128)(2,1)S(1)}, bf16[2,1280,256]{2,1,0:T(8,128)(2,1)S(1)}, u32[]{:S(2)}, u32[]{:S(2)}) collective-permute-start(bf16[2,1280,256]{2,1,0:T(8,128)(2,1)S(1)} %pad_maximum_fusion), channel_id=1, source_target_pairs={{0,1},{1,0},{2,3},{3,2},{4,5},{5,4},{6,7},{7,6},{8,9},{9,8},{10,11... | collective-permute-start | bytes 3932168 | tf_op jit(solution)/shard_map/ppermute | solution.py:29
  68.2 36.0 %all-gather.9.cloned.1.call-start = ((), (), s32[]{:S(2)}) async-start(), calls=%async_computation.5 | async-start | bytes 3538944 | tf_op jit(solution)/shard_map/cond/branch_1_fun/all_gather | solution.py:636
  68.2 4.0 %copy-start.1 = (s32[2,5,8]{2,1,0:T(8,128)}, s32[2,5,8]{2,1,0:T(8,128)S(1)}, u32[]{:S(2)}) copy-start(s32[2,5,8]{2,1,0:T(8,128)S(1)} %copy.28.v_mask_ref) | copy-start | bytes 964 | tf_op jit(solution)/shard_map/cond
  72.1 19.9 %collective-permute-start.1 = (bf16[3,256,256]{2,1,0:T(8,128)(2,1)S(1)}, bf16[3,256,256]{2,1,0:T(8,128)(2,1)S(1)}, u32[]{:S(2)}, u32[]{:S(2)}) collective-permute-start(bf16[3,256,256]{2,1,0:T(8,128)(2,1)S(1)} %get-tuple-element.120), channel_id=1, source_target_pairs={{0,8},{1,9},{2,10},{3,11},{4,12},{5,13},{6,14},{7,15},{8,0},{9,1},... | collective-permute-start | bytes 1179656 | tf_op jit(solution)/shard_map/cond/branch_1_fun/ppermute | solution.py:29
  92.1 0.8 copy-start.3
  92.8 100.5 %all-to-all-start.1 = ((bf16[16,2,256,256]{3,2,1,0:T(8,128)(2,1)}), bf16[16,2,256,256]{3,2,1,0:T(8,128)(2,1)}, u32[]{:S(2)}, u32[]{:S(2)}) async-start(bf16[16,2,256,256]{3,2,1,0:T(8,128)(2,1)} %bitcast.36), calls=%async_computation.1 | async-start | bytes 8388608 | tf_op jit(solution)/shard_map/cond/branch_1_fun/all_to_all | solution.py:575
  100.6 67.6 %all-gather.11.cloned.1.call-start = ((), (), s32[]{:S(2)}) async-start(), calls=%async_computation.6 | async-start | bytes 3538944 | tf_op jit(solution)/shard_map/cond/branch_1_fun/all_gather | solution.py:636
Sparse Core Ops, SparseCore 0:
  72.3 31.8 all-gather.8
  105.8 62.3 all-gather.10
